TPU v7x, 32 devices: a whole 2x2x4 slice. The times are simulated.
32 devices in a mesh: groups: 2 (over x), expert: 16 (over z, y, core).
Axes of the slice: x: 2, y: 2, z: 4, core: 2. Of those that a mesh axis runs over, the one named last changes fastest.
Arguments:
- queries: bfloat16 [64, 8192], P(('groups', 'expert')), parts along dimension 0, may hold values from -20 to 20
- kv_cache: bfloat16 [64, 2, 1024, 512], P(('groups', 'expert')), parts along dimension 0, may hold values from -6 to 6
- lengths: int32 [64], P(('groups', 'expert')), parts along dimension 0, may hold values from 2 to 1024, as said below
- moe_input: bfloat16 [2048, 4096], P(('groups', 'expert')), parts along dimension 0, may hold values from -6 to 6
- route_ids: int32 [2048, 8], P(('groups', 'expert')), parts along dimension 0, may hold values from 0 to 15, all different within a row; in each aligned block of 64 rows (0 to 63, 64 to 127, ...) at most 48 rows name the same one
- route_weights: float32 [2048, 8], P(('groups', 'expert')), parts along dimension 0, may hold values from 0.05 to 1
- w_gate_up: bfloat16 [16, 4096, 1536], P('expert'), may hold values from -0.09375 to 0.09375
- w_down: bfloat16 [16, 768, 4096], P('expert'), may hold values from -0.21875 to 0.21875
Outputs:
- attended: bfloat16 [64, 8192], P(('groups', 'expert')), parts along dimension 0
- moe_out: bfloat16 [2048, 4096], P(('groups', 'expert')), parts along dimension 0
There are 2 independent parts, one for each index of `groups`. A program takes and returns all parts, laid end to end along the dimension named above; an argument that names none is the same for every part. Nothing has to cross between parts.
Inputs may be any that keep to these rules, and one draw needn't show every extreme that they name: `route_ids`: in the rows of one device (aligned blocks of 64 rows) no expert is named more than 48 times, a bound that some block reaches; a row names 8 different experts. `lengths`: some request has length exactly 1024.
All inputs are finite; a program needn't handle non-finite values.
Results may differ from a plain program's by a relative error of at most 0.0058.
Values may be sent and summed in bfloat16 or wider, within the bound.
No kernel may reach another device: no remote copies, remote signals or barrier semaphores. Data moves between devices by JAX's collectives and lax.ppermute only.
A program may use at most 128 MiB of HBM per device.

v0:
```python
import jax
import jax.numpy as jnp
from jax import lax
from jax.sharding import PartitionSpec as P

HEADS = 64
KVH = 4
HD = 128
TOP = 8
CTX = 1024


def attend_local(queries, kv_cache, lengths):
    requests = queries.shape[0]
    group_size = HEADS // KVH
    query_rows = queries.reshape(requests, KVH, group_size, HD)
    key_rows = kv_cache[:, 0].reshape(requests, CTX, KVH, HD)
    value_rows = kv_cache[:, 1].reshape(requests, CTX, KVH, HD)
    scores = jnp.einsum(
        "rghd,rpgd->rghp", query_rows, key_rows, preferred_element_type=jnp.float32
    ) * HD ** (-0.5)
    visible = jnp.arange(CTX, dtype=jnp.int32)[None, :] < lengths[:, None]
    scores = jnp.where(visible[:, None, None, :], scores, -jnp.inf)
    peak_score = jnp.max(scores, axis=-1, keepdims=True)
    raised = jnp.exp(scores - peak_score)
    weights_low = (raised / jnp.sum(raised, axis=-1, keepdims=True)).astype(jnp.bfloat16)
    mixed_heads = jnp.einsum(
        "rghp,rpgd->rghd", weights_low, value_rows, preferred_element_type=jnp.float32
    )
    return mixed_heads.reshape(requests, HEADS * HD).astype(jnp.bfloat16)


def expert_apply(token_rows, gate_up, down_weight):
    projected = jnp.dot(token_rows, gate_up, preferred_element_type=jnp.float32)
    hidden_width = down_weight.shape[0]
    hidden = (jax.nn.silu(projected[:, :hidden_width]) * projected[:, hidden_width:]).astype(
        jnp.bfloat16
    )
    return jnp.dot(hidden, down_weight, preferred_element_type=jnp.float32).astype(jnp.bfloat16)


def route_slots(route_ids, peer_count, capacity):
    flat_ids = route_ids.reshape(-1)
    matches = flat_ids[:, None] == jnp.arange(peer_count, dtype=jnp.int32)[None, :]
    running = jnp.cumsum(matches.astype(jnp.int32), axis=0) - 1
    slot_index = jnp.sum(jnp.where(matches, running, 0), axis=1)
    return flat_ids * capacity + slot_index


def fill_rows(token_rows, destination, sources, slots_total):
    row_table = jnp.full((slots_total,), token_rows.shape[0], jnp.int32)
    row_table = row_table.at[destination].set(sources, mode="drop")
    padded = jnp.concatenate(
        [token_rows, jnp.zeros((1, token_rows.shape[1]), token_rows.dtype)], axis=0
    )
    return padded[row_table]


def combine_rows(returned_flat, destination, route_weights):
    token_count = route_weights.shape[0]
    picked = (
        returned_flat[destination]
        .astype(jnp.float32)
        .reshape(token_count, TOP, returned_flat.shape[1])
    )
    share_norm = route_weights / jnp.sum(route_weights, axis=1, keepdims=True)
    return jnp.sum(share_norm[:, :, None] * picked, axis=1).astype(jnp.bfloat16)


def shards(queries, kv_cache, lengths, moe_input, route_ids, route_weights, w_gate_up, w_down):
    attended = attend_local(queries, kv_cache, lengths)
    peer_count = lax.axis_size("expert")
    capacity = 3 * moe_input.shape[0] * TOP // (2 * peer_count)
    width_model = moe_input.shape[1]
    destination = route_slots(route_ids, peer_count, capacity)
    sources = jnp.arange(destination.shape[0], dtype=jnp.int32) // TOP
    gate_up = w_gate_up[0]
    down_weight = w_down[0]
    outgoing = fill_rows(moe_input, destination, sources, peer_count * capacity).reshape(
        peer_count, capacity, width_model
    )
    received = lax.all_to_all(outgoing, "expert", split_axis=0, concat_axis=0, tiled=True)
    computed = expert_apply(received.reshape(-1, width_model), gate_up, down_weight).reshape(
        peer_count, capacity, width_model
    )
    returned = lax.all_to_all(computed, "expert", split_axis=0, concat_axis=0, tiled=True)
    moe_out = combine_rows(returned.reshape(-1, width_model), destination, route_weights)
    return (attended, moe_out)


def solution(mesh):
    placed = (
        P(("groups", "expert"), None),
        P(("groups", "expert"), None, None, None),
        P(("groups", "expert")),
        P(("groups", "expert"), None),
        P(("groups", "expert"), None),
        P(("groups", "expert"), None),
        P("expert", None, None),
        P("expert", None, None),
    )
    return jax.shard_map(
        shards,
        mesh=mesh,
        in_specs=placed,
        out_specs=(P(("groups", "expert"), None), P(("groups", "expert"), None)),
        check_vma=False,
    )
```

profile of v0, /device:TPU:13, one launch (start us, length us, event | category | flops | bytes accessed | tf_op | source)
XLA Modules:
  0.0 340.2 jit_solution(4793980173898536378)
XLA Ops:
  0.6 0.8 copy.17
  1.4 0.1 eq.29
  1.6 0.7 broadcast_multiply_fusion
  2.3 1.2 reduce-window.6
  3.4 0.2 slice_reduce_fusion
  3.8 0.1 mul.42
  3.9 0.1 fusion.13
  4.0 2.4 scatter_custom_fusion
  6.5 1.1 concatenate.3
  7.6 5.7 %gather_fusion = bf16[768,4096]{1,0:T(8,128)(2,1)} fusion(bf16[65,4096]{1,0:T(8,128)(2,1)S(1)} %concatenate.3, s32[1024]{0:T(1024)S(1)} %pad_clamp_fusion.1), kind=kCustom, calls=%fused_computation | custom fusion | bytes 12585984 | tf_op jit(solution)/shard_map/gather | solution.py:56
  13.3 144.0 %all_to_all.10 = bf16[16,48,4096]{2,1,0:T(8,128)(2,1)S(1)} all-to-all(bf16[16,48,4096]{2,1,0:T(8,128)(2,1)} %bitcast.46), channel_id=1, replica_groups=mesh['groups'=2,'expert'=16] {'expert'}, dimensions={0} | all-to-all | bytes 12582912 | tf_op jit(solution)/shard_map/all_to_all | solution.py:82
  157.3 11.6 %fusion.1 = f32[768,1536]{1,0:T(8,128)} fusion(bf16[768,4096]{1,0:T(8,128)(2,1)S(1)} %bitcast.49, bf16[1,4096,1536]{2,1,0:T(8,128)(2,1)S(1)} %copy-done.3), kind=kOutput, calls=%fused_computation.4 | convolution fusion | flops 9663676416 | bytes 23592960 | tf_op jit(solution)/shard_map/dot_general | solution.py:34
  168.9 9.6 %convolution_convert_fusion = bf16[768,4096]{1,0:T(8,128)(2,1)} fusion(bf16[1,768,4096]{2,1,0:T(8,128)(2,1)S(1)} %bitcast.59, f32[768,1536]{1,0:T(8,128)} %fusion.1), kind=kOutput, calls=%fused_computation.8 | convolution fusion | flops 4838522880 | bytes 17301504 | tf_op jit(solution)/shard_map/dot_general | solution.py:39
  178.5 5.6 %all-to-all-start.1 = ((bf16[16,48,4096]{2,1,0:T(8,128)(2,1)}), bf16[16,48,4096]{2,1,0:T(8,128)(2,1)}, u32[]{:S(2)}, u32[]{:S(2)}) async-start(bf16[16,48,4096]{2,1,0:T(8,128)(2,1)} %bitcast.48), calls=%async_computation.1 | async-start | bytes 12582912 | tf_op jit(solution)/shard_map/all_to_all | solution.py:86
  184.2 4.5 %fusion.22 = (bf16[2,1,1024,512]{3,2,1,0:T(8,128)(2,1)}, bf16[2,1,1024,512]{3,2,1,0:T(8,128)(2,1)}) fusion(bf16[2,2,1024,512]{3,2,1,0:T(8,128)(2,1)} %param.9), kind=kLoop, calls=%fused_computation.47 | loop fusion | bytes 8388608 | tf_op jit(solution)/shard_map/slice | solution.py:17
  188.8 3.0 copy.22
  191.8 3.9 %copy.23 = bf16[2,1,1024,512]{2,3,0,1:T(8,128)(2,1)} copy(bf16[2,1,1024,512]{3,2,1,0:T(8,128)(2,1)} %get-tuple-element.3) | data formatting | bytes 4194304
  195.8 0.4 fusion.8
  196.2 0.2 fusion.23
  196.5 2.3 convolution_convert_fusion.1
  198.8 0.7 copy.29
  199.4 122.1 %all-to-all-done.1 = bf16[16,48,4096]{2,1,0:T(8,128)(2,1)} async-done(((bf16[16,48,4096]{2,1,0:T(8,128)(2,1)}), bf16[16,48,4096]{2,1,0:T(8,128)(2,1)}, u32[]{:S(2)}, u32[]{:S(2)}) %all-to-all-start.1) | async-done | bytes 6291488 | tf_op jit(solution)/shard_map/all_to_all | solution.py:86
  321.5 12.2 %gather_fusion.1 = bf16[512,4096]{1,0:T(8,128)(2,1)} fusion(bf16[768,4096]{1,0:T(8,128)(2,1)} %bitcast.10, s32[1024]{0:T(1024)S(1)} %pad_clamp_fusion), kind=kCustom, calls=%fused_computation.1 | custom fusion | bytes 8390656 | tf_op jit(solution)/shard_map/gather | solution.py:62
  333.8 6.5 %fusion.3 = bf16[64,4096]{1,0:T(8,128)(2,1)} fusion(bf16[512,4096]{1,0:T(8,128)(2,1)} %gather_fusion.1, f32[64,8]{1,0:T(8,128)S(1)} %copy.15), kind=kLoop, calls=%fused_computation.7 | loop fusion | flops 6029312 | bytes 4720640 | tf_op jit(solution)/shard_map/reduce_sum | solution.py:67
  (28 shorter events, 0.5 us)
Async XLA Ops:
  13.3 144.0 %copy-start.3 = (bf16[1,4096,1536]{2,1,0:T(8,128)(2,1)S(1)}, bf16[1,4096,1536]{2,1,0:T(8,128)(2,1)}, u32[]{:S(2)}) copy-start(bf16[1,4096,1536]{2,1,0:T(8,128)(2,1)} %param.14) | copy-start | bytes 37748740
  13.3 155.6 %slice-start = ((s8[6291456]{0:T(1024)(128)(4,1)}), s8[4194304]{0:T(1024)(128)(4,1)S(1)}, s32[]{:S(2)}) async-start(s8[6291456]{0:T(1024)(128)(4,1)} %bitcast.58), calls=%async_computation.2 | async-start | bytes 8388608
  157.3 11.6 %slice-start.1 = ((s8[6291456]{0:T(1024)(128)(4,1)}), s8[2097152]{0:T(1024)(128)(4,1)S(1)}, s32[]{:S(2)}) async-start(s8[6291456]{0:T(1024)(128)(4,1)} %bitcast.58), calls=%async_computation.3 | async-start | bytes 4194304
  178.5 5.6 %copy-start.1 = (f32[64,8]{0,1:T(8,128)S(1)}, f32[64,8]{0,1:T(8,128)}, u32[]{:S(2)}) copy-start(f32[64,8]{0,1:T(8,128)} %param.13) | copy-start | bytes 6148
  178.5 143.0 %all-to-all-start.1 = ((bf16[16,48,4096]{2,1,0:T(8,128)(2,1)}), bf16[16,48,4096]{2,1,0:T(8,128)(2,1)}, u32[]{:S(2)}, u32[]{:S(2)}) async-start(bf16[16,48,4096]{2,1,0:T(8,128)(2,1)} %bitcast.48), calls=%async_computation.1 | async-start | bytes 12582912 | tf_op jit(solution)/shard_map/all_to_all | solution.py:86
  188.8 3.0 copy-start
  188.8 7.0 %copy-start.2 = (s32[2]{0:T(128)S(1)}, s32[2]{0:T(128)}, u32[]{:S(2)}) copy-start(s32[2]{0:T(128)} %param.10) | copy-start | bytes 28
where the time goes:
time: 341 us; the launch traced here: 340 us
  blocking collectives  144 us (42%)
  waiting for transfers between devices  122 us (36%)
  local copies, waits for them, and re-layouts  35.1 us (10%)
  matrix products  23.9 us (7%)
  other arithmetic  8.81 us (3%)
  starting transfers between devices  5.62 us (2%)
    all_to_all x1, blocking collectives, shards(): lax.all_to_all(outgoing, 'expert', split_axis=0, concat_axis=0, tiled=True)  144 us
    all_to_all x1, waiting for transfers between devices, shards(): lax.all_to_all(computed, 'expert', split_axis=0, concat_axis=0, tiled=True)  122 us
    gather x1, local copies, waits for them, and re-layouts, combine_rows(): returned_flat[destination].astype(jnp.float32)  12.2 us
    dot_general x1, matrix products, expert_apply(): projected = jnp.dot(token_rows, gate_up, preferred_element_type=jnp.float32)  11.6 us
    dot_general x1, matrix products, expert_apply(): jnp.dot(hidden, down_weight, preferred_element_type=jnp.float32)  9.6 us
    unnamed x17, local copies, waits for them, and re-layouts  8.41 us
  transfers between devices with their start and end apart: 1, of which 1 were waited for; matrix products, arithmetic and copies ran while one was open for 4% of the time, Pallas kernels for 0%

commit v1 on v0

v1 whole, which is shorter than its diff:
```python
import functools

import jax
import jax.numpy as jnp
from jax import lax
from jax.experimental import pallas as pl
from jax.experimental.pallas import tpu as pltpu
from jax.sharding import PartitionSpec as P

HEADS = 64
KVH = 4
HD = 128
CTX = 1024
LANES = 128
CHUNKS = 2


def attend_kernel(lengths_ref, q_ref, kv_ref, o_ref):
    request = pl.program_id(0)
    length = lengths_ref[request]
    group_size = HEADS // KVH
    visible = lax.broadcasted_iota(jnp.int32, (group_size, CTX), 1) < length
    for g in range(KVH):
        q = q_ref[0, g * group_size : (g + 1) * group_size, :]
        keys = kv_ref[0, 0, :, g * HD : (g + 1) * HD]
        values = kv_ref[0, 1, :, g * HD : (g + 1) * HD]
        scores = lax.dot_general(
            q, keys, (((1,), (1,)), ((), ())), preferred_element_type=jnp.float32
        ) * HD ** (-0.5)
        scores = jnp.where(visible, scores, -jnp.inf)
        raised = jnp.exp(scores - jnp.max(scores, axis=-1, keepdims=True))
        weights = (raised / jnp.sum(raised, axis=-1, keepdims=True)).astype(jnp.bfloat16)
        mixed = jnp.dot(weights, values, preferred_element_type=jnp.float32)
        o_ref[0, g * group_size : (g + 1) * group_size, :] = mixed.astype(jnp.bfloat16)


def attend_local(queries, kv_cache, lengths):
    requests = queries.shape[0]
    grid_spec = pltpu.PrefetchScalarGridSpec(
        num_scalar_prefetch=1,
        grid=(requests,),
        in_specs=[
            pl.BlockSpec((1, HEADS, HD), lambda r, lens: (r, 0, 0)),
            pl.BlockSpec((1, 2, CTX, KVH * HD), lambda r, lens: (r, 0, 0, 0)),
        ],
        out_specs=pl.BlockSpec((1, HEADS, HD), lambda r, lens: (r, 0, 0)),
    )
    out = pl.pallas_call(
        attend_kernel,
        grid_spec=grid_spec,
        out_shape=jax.ShapeDtypeStruct((requests, HEADS, HD), jnp.bfloat16),
        compiler_params=pltpu.CompilerParams(vmem_limit_bytes=16 << 20),
        cost_estimate=pl.CostEstimate(
            flops=requests * 4 * HEADS * CTX * HD,
            bytes_accessed=requests * 4 * CTX * KVH * HD,
            transcendentals=requests * HEADS * CTX,
        ),
        name="attend",
    )(lengths, queries.reshape(requests, HEADS, HD), kv_cache)
    return out.reshape(requests, HEADS * HD)


def expert_kernel(sel_ref, own_ref, sib_ref, gate_ref, up_ref, down_ref, out_own, out_sib, acc):
    j = pl.program_id(0)
    rows = own_ref.shape[0]
    width = down_ref.shape[2]
    x = jnp.concatenate([own_ref[:, :width], sib_ref[:, :width]], axis=0)
    gate = jnp.dot(x, gate_ref[0], preferred_element_type=jnp.float32)
    up = jnp.dot(x, up_ref[0], preferred_element_type=jnp.float32)
    hidden = (jax.nn.silu(gate) * up).astype(jnp.bfloat16)
    part = jnp.dot(hidden, down_ref[0], preferred_element_type=jnp.float32)

    @pl.when(j == 0)
    def _():
        acc[...] = part

    @pl.when((j > 0) & (j < pl.num_programs(0) - 1))
    def _():
        acc[...] += part

    @pl.when(j == pl.num_programs(0) - 1)
    def _():
        total = acc[...] + part
        for ref, out, at in ((own_ref, out_own, 0), (sib_ref, out_sib, rows)):
            coef = jnp.sum(
                ref[:, width:].astype(jnp.float32) * sel_ref[...], axis=1, keepdims=True
            )
            out[...] = (total[at : at + rows] * coef).astype(jnp.bfloat16)


def expert_apply(sel, own, sib, w_gate_up, w_down):
    rows, wide = own.shape
    _, ff, width = w_down.shape
    block = 256
    steps = ff // block
    whole = pl.BlockSpec((rows, wide), lambda j: (0, 0))
    out_spec = pl.BlockSpec((rows, width), lambda j: (0, 0))
    shape = jax.ShapeDtypeStruct((rows, width), jnp.bfloat16)
    return pl.pallas_call(
        expert_kernel,
        grid=(steps,),
        in_specs=[
            pl.BlockSpec((1, LANES), lambda j: (0, 0)),
            whole,
            whole,
            pl.BlockSpec((1, width, block), lambda j: (0, 0, j)),
            pl.BlockSpec((1, width, block), lambda j: (0, 0, j + steps)),
            pl.BlockSpec((1, block, width), lambda j: (0, j, 0)),
        ],
        out_specs=[out_spec, out_spec],
        out_shape=[shape, shape],
        scratch_shapes=[pltpu.VMEM((2 * rows, width), jnp.float32)],
        compiler_params=pltpu.CompilerParams(vmem_limit_bytes=36 << 20),
        cost_estimate=pl.CostEstimate(
            flops=2 * 2 * rows * width * ff * 3,
            bytes_accessed=2 * 3 * width * ff,
            transcendentals=0,
        ),
        name="expert",
    )(sel, own, sib, w_gate_up, w_gate_up, w_down)


def coefficient_columns(route_ids, route_weights, experts):
    share = route_weights / jnp.sum(route_weights, axis=1, keepdims=True)
    names = route_ids[:, :, None] == jnp.arange(experts, dtype=jnp.int32)[None, None, :]
    coef = jnp.sum(jnp.where(names, share[:, :, None], 0.0), axis=1)
    high = lax.reduce_precision(coef, 8, 7)
    middle = lax.reduce_precision(coef - high, 8, 7)
    low = lax.reduce_precision(coef - high - middle, 8, 7)
    parts = jnp.concatenate([high, middle, low], axis=1)
    return jnp.pad(parts, ((0, 0), (0, LANES - 3 * experts))).astype(jnp.bfloat16)


def shards(order, queries, kv_cache, lengths, moe_input, route_ids, route_weights, w_gate_up, w_down):
    experts = lax.axis_size("expert")
    chips = len(order)
    half = chips // 2
    rows = moe_input.shape[0] // CHUNKS

    def ring(step):
        return [
            (2 * order[i] + c, 2 * order[(i + step) % chips] + c)
            for i in range(chips)
            for c in range(2)
        ]

    forward, backward = ring(1), ring(-1)
    swap = [(i, i ^ 1) for i in range(experts)]

    def send(x, pairs):
        return lax.ppermute(x, "expert", pairs)

    me = lax.axis_index("expert")
    lane = lax.broadcasted_iota(jnp.int32, (1, LANES), 1)
    sel = ((lane % experts == me) & (lane < 3 * experts)).astype(jnp.float32)

    wide = jnp.concatenate(
        [moe_input, coefficient_columns(route_ids, route_weights, experts)], axis=1
    )
    fwd = [wide[k * rows : (k + 1) * rows] for k in range(CHUNKS)]
    bwd = list(fwd)
    slots = []
    partial = []

    def compute(own):
        sib = send(own, swap)
        mine, theirs = expert_apply(sel, own, sib, w_gate_up, w_down)
        partial.append((mine, send(theirs, swap)))

    slots.append({("f", k): k for k in range(CHUNKS)})
    last = wide
    for s in range(1, half + 1):
        arrivals = []
        where = {}
        for k in range(CHUNKS):
            if s < half or k == 0:
                fwd[k] = send(fwd[k], forward)
                where["f", k] = len(arrivals)
                arrivals.append(fwd[k])
            if s < half or k == 1:
                bwd[k] = send(bwd[k], backward)
                where["b", k] = len(arrivals)
                arrivals.append(bwd[k])
        compute(last)
        slots.append(where)
        last = jnp.concatenate(arrivals, axis=0)
    compute(last)

    attended = attend_local(queries, kv_cache, lengths)

    def pieces(s, way, k):
        at = slots[s][way, k] * rows
        return [p[at : at + rows].astype(jnp.float32) for p in partial[s]]

    moving = {}
    for s in range(half, 0, -1):
        for k in range(CHUNKS):
            for way, pairs in (("f", backward), ("b", forward)):
                if (way, k) not in slots[s]:
                    continue
                mine, theirs = pieces(s, way, k)
                total = mine + theirs
                if (way, k) in moving:
                    total = total + moving[way, k].astype(jnp.float32)
                moving[way, k] = send(total.astype(jnp.bfloat16), pairs)
    out = []
    for k in range(CHUNKS):
        mine, theirs = pieces(0, "f", k)
        total = mine + theirs
        for way in ("f", "b"):
            total = total + moving[way, k].astype(jnp.float32)
        out.append(total.astype(jnp.bfloat16))
    return attended, jnp.concatenate(out, axis=0)


def solution(mesh):
    chips = mesh.shape["expert"] // 2
    if mesh.shape["groups"] == 2:
        order = list(range(0, chips, 2)) + list(range(chips - 1, 0, -2))
    else:
        order = list(range(chips))
    placed = (
        P(("groups", "expert"), None),
        P(("groups", "expert"), None, None, None),
        P(("groups", "expert")),
        P(("groups", "expert"), None),
        P(("groups", "expert"), None),
        P(("groups", "expert"), None),
        P("expert", None, None),
        P("expert", None, None),
    )
    return jax.shard_map(
        functools.partial(shards, order),
        mesh=mesh,
        in_specs=placed,
        out_specs=(P(("groups", "expert"), None), P(("groups", "expert"), None)),
        check_vma=False,
    )
```

time: 341 us -> 134 us (0.39)
  the two profiles are of different devices: /device:TPU:13 before, /device:TPU:0 now
where the time goes in v1:
time: 134 us
  Pallas kernels  46.9 us (35%)
  waiting for transfers between devices  43.6 us (33%)
  starting transfers between devices  35.2 us (26%)
  other arithmetic  5.9 us (4%)
    ppermute x38, waiting for transfers between devices, send(): return lax.ppermute(x, 'expert', pairs)  43.6 us
    pallas_call x5, Pallas kernels, expert_apply(): pl.pallas_call(expert_kernel, grid=(steps,), in_specs=[pl.BlockSpec((1, L...  43.1 us
    ppermute x38, starting transfers between devices, send(): return lax.ppermute(x, 'expert', pairs)  35.2 us
    pallas_call x1, Pallas kernels, attend_local(): pl.pallas_call(attend_kernel, grid_spec=grid_spec, out_shape=jax.ShapeDty...  3.83 us
  transfers between devices with their start and end apart: 38, of which 18 were waited for; matrix products, arithmetic and copies ran while one was open for 2% of the time, Pallas kernels for 35%

profile of v1, /device:TPU:0, one launch (start us, length us, event | category | flops | bytes accessed | tf_op | source)
XLA Modules:
  0.0 133.8 jit_solution(16408117619548149919)
XLA Ops:
  4.2 3.1 %collective-permute-start.2 = (bf16[32,4224]{1,0:T(8,128)(2,1)S(1)}, bf16[32,4224]{1,0:T(8,128)(2,1)S(1)}, u32[]{:S(2)}, u32[]{:S(2)}) collective-permute-start(bf16[32,4224]{1,0:T(8,128)(2,1)S(1)} %get-tuple-element.39), channel_id=1, source_target_pairs={{0,4},{1,5},{4,8},{5,9},{8,12},{9,13},{12,14},{13,15},{14,10},{15,... | collective-permute-start | bytes 811016 | tf_op jit(solution)/shard_map/ppermute | solution.py:151
  7.2 2.0 %collective-permute-start.5 = (bf16[32,4224]{1,0:T(8,128)(2,1)S(1)}, bf16[32,4224]{1,0:T(8,128)(2,1)S(1)}, u32[]{:S(2)}, u32[]{:S(2)}) collective-permute-start(bf16[32,4224]{1,0:T(8,128)(2,1)S(1)} %get-tuple-element.38), channel_id=1, source_target_pairs={{0,2},{1,3},{4,0},{5,1},{8,4},{9,5},{12,8},{13,9},{14,12},{15,13},... | collective-permute-start | bytes 811016 | tf_op jit(solution)/shard_map/ppermute | solution.py:151
  9.4 5.1 %collective-permute-done.2 = bf16[32,4224]{1,0:T(8,128)(2,1)S(1)} collective-permute-done((bf16[32,4224]{1,0:T(8,128)(2,1)S(1)}, bf16[32,4224]{1,0:T(8,128)(2,1)S(1)}, u32[]{:S(2)}, u32[]{:S(2)}) %collective-permute-start.2) | collective-permute-done | bytes 270368 | tf_op jit(solution)/shard_map/ppermute | solution.py:151
  14.5 2.1 %collective-permute-start.8 = (bf16[32,4224]{1,0:T(8,128)(2,1)S(1)}, bf16[32,4224]{1,0:T(8,128)(2,1)S(1)}, u32[]{:S(2)}, u32[]{:S(2)}) collective-permute-start(bf16[32,4224]{1,0:T(8,128)(2,1)S(1)} %collective-permute-done.2), channel_id=1, source_target_pairs={{0,4},{1,5},{4,8},{5,9},{8,12},{9,13},{12,14},{13,15},{14,10},{15,... | collective-permute-start | bytes 811016 | tf_op jit(solution)/shard_map/ppermute | solution.py:151
  16.7 3.6 %collective-permute-done.4 = bf16[32,4224]{1,0:T(8,128)(2,1)S(1)} collective-permute-done((bf16[32,4224]{1,0:T(8,128)(2,1)S(1)}, bf16[32,4224]{1,0:T(8,128)(2,1)S(1)}, u32[]{:S(2)}, u32[]{:S(2)}) %collective-permute-start.4) | collective-permute-done | bytes 270368 | tf_op jit(solution)/shard_map/ppermute | solution.py:151
  22.5 1.6 %collective-permute-start.9 = (bf16[32,4224]{1,0:T(8,128)(2,1)S(1)}, bf16[32,4224]{1,0:T(8,128)(2,1)S(1)}, u32[]{:S(2)}, u32[]{:S(2)}) collective-permute-start(bf16[32,4224]{1,0:T(8,128)(2,1)S(1)} %collective-permute-done.3), channel_id=1, source_target_pairs={{0,2},{1,3},{4,0},{5,1},{8,4},{9,5},{12,8},{13,9},{14,12},{15,13},... | collective-permute-start | bytes 811016 | tf_op jit(solution)/shard_map/ppermute | solution.py:151
  25.2 1.8 %collective-permute-start.14 = (bf16[32,4224]{1,0:T(8,128)(2,1)S(1)}, bf16[32,4224]{1,0:T(8,128)(2,1)S(1)}, u32[]{:S(2)}, u32[]{:S(2)}) collective-permute-start(bf16[32,4224]{1,0:T(8,128)(2,1)S(1)} %collective-permute-done.8), channel_id=1, source_target_pairs={{0,4},{1,5},{4,8},{5,9},{8,12},{9,13},{12,14},{13,15},{14,10},{15,... | collective-permute-start | bytes 811016 | tf_op jit(solution)/shard_map/ppermute | solution.py:151
  27.1 3.3 %collective-permute-done.11 = bf16[32,4224]{1,0:T(8,128)(2,1)S(1)} collective-permute-done((bf16[32,4224]{1,0:T(8,128)(2,1)S(1)}, bf16[32,4224]{1,0:T(8,128)(2,1)S(1)}, u32[]{:S(2)}, u32[]{:S(2)}) %collective-permute-start.11) | collective-permute-done | bytes 270368 | tf_op jit(solution)/shard_map/ppermute | solution.py:151
  31.8 4.4 %collective-permute-done.9 = bf16[32,4224]{1,0:T(8,128)(2,1)S(1)} collective-permute-done((bf16[32,4224]{1,0:T(8,128)(2,1)S(1)}, bf16[32,4224]{1,0:T(8,128)(2,1)S(1)}, u32[]{:S(2)}, u32[]{:S(2)}) %collective-permute-start.9) | collective-permute-done | bytes 270368 | tf_op jit(solution)/shard_map/ppermute | solution.py:151
  38.3 1.6 %collective-permute-start.20 = (bf16[32,4224]{1,0:T(8,128)(2,1)S(1)}, bf16[32,4224]{1,0:T(8,128)(2,1)S(1)}, u32[]{:S(2)}, u32[]{:S(2)}) collective-permute-start(bf16[32,4224]{1,0:T(8,128)(2,1)S(1)} %collective-permute-done.14), channel_id=1, source_target_pairs={{0,4},{1,5},{4,8},{5,9},{8,12},{9,13},{12,14},{13,15},{14,10},{15,... | collective-permute-start | bytes 811016 | tf_op jit(solution)/shard_map/ppermute | solution.py:151
  39.9 7.4 %collective-permute-done.15 = bf16[32,4224]{1,0:T(8,128)(2,1)S(1)} collective-permute-done((bf16[32,4224]{1,0:T(8,128)(2,1)S(1)}, bf16[32,4224]{1,0:T(8,128)(2,1)S(1)}, u32[]{:S(2)}, u32[]{:S(2)}) %collective-permute-start.15) | collective-permute-done | bytes 270368 | tf_op jit(solution)/shard_map/ppermute | solution.py:151
  49.0 1.7 %collective-permute-done.20 = bf16[32,4224]{1,0:T(8,128)(2,1)S(1)} collective-permute-done((bf16[32,4224]{1,0:T(8,128)(2,1)S(1)}, bf16[32,4224]{1,0:T(8,128)(2,1)S(1)}, u32[]{:S(2)}, u32[]{:S(2)}) %collective-permute-start.20) | collective-permute-done | bytes 270368 | tf_op jit(solution)/shard_map/ppermute | solution.py:151
  50.8 5.7 %collective-permute-done.21 = bf16[32,4224]{1,0:T(8,128)(2,1)S(1)} collective-permute-done((bf16[32,4224]{1,0:T(8,128)(2,1)S(1)}, bf16[32,4224]{1,0:T(8,128)(2,1)S(1)}, u32[]{:S(2)}, u32[]{:S(2)}) %collective-permute-start.21) | collective-permute-done | bytes 270368 | tf_op jit(solution)/shard_map/ppermute | solution.py:151
  56.5 1.9 %collective-permute-done.22.sib_ref = bf16[64,4224]{1,0:T(8,128)(2,1)S(1)} collective-permute-done((bf16[64,4224]{1,0:T(8,128)(2,1)S(1)}, bf16[64,4224]{1,0:T(8,128)(2,1)S(1)}, u32[]{:S(2)}, u32[]{:S(2)}) %collective-permute-start.22) | collective-permute-done | bytes 540704 | tf_op jit(solution)/shard_map/ppermute | solution.py:151
  58.4 7.3 %expert.9 = (bf16[64,4096]{1,0:T(8,128)(2,1)S(1)}, bf16[64,4096]{1,0:T(8,128)(2,1)S(1)}) custom-call(f32[1,128]{1,0:T(1,128)S(1)} %and_convert_fusion.sel_ref, bf16[64,4224]{1,0:T(8,128)(2,1)S(1)} %constant_dynamic-update-slice_fusion.12.own_ref, bf16[64,4224]{1,0:T(8,128)(2,1)S(1)} %collective-permute-done.22.sib_ref, bf16[1,4096,1536]{2,1,0:T(8,128)(2,1)} %up_ref.9, ...), custom_call_target="tpu_custom_call" | custom-call | flops 2415919104 | bytes 18874368 | tf_op jit(solution)/shard_map/expert/pallas_call | solution.py:99
  66.4 9.5 %expert.8 = (bf16[128,4096]{1,0:T(8,128)(2,1)S(1)}, bf16[128,4096]{1,0:T(8,128)(2,1)S(1)}) custom-call(f32[1,128]{1,0:T(1,128)S(1)} %and_convert_fusion.sel_ref, bf16[128,4224]{1,0:T(8,128)(2,1)S(1)} %constant_dynamic-update-slice_fusion.8.own_ref, bf16[128,4224]{1,0:T(8,128)(2,1)S(1)} %collective-permute-done.18.sib_ref, bf16[1,4096,1536]{2,1,0:T(8,128)(2,1)} %up_ref.9, ...), custom_call_target="tpu_custom_call" | custom-call | flops 4831838208 | bytes 18874368 | tf_op jit(solution)/shard_map/expert/pallas_call | solution.py:99
  78.4 9.5 %expert.7 = (bf16[128,4096]{1,0:T(8,128)(2,1)S(1)}, bf16[128,4096]{1,0:T(8,128)(2,1)S(1)}) custom-call(f32[1,128]{1,0:T(1,128)S(1)} %and_convert_fusion.sel_ref, bf16[128,4224]{1,0:T(8,128)(2,1)S(1)} %constant_dynamic-update-slice_fusion.4.own_ref, bf16[128,4224]{1,0:T(8,128)(2,1)S(1)} %collective-permute-done.12.sib_ref, bf16[1,4096,1536]{2,1,0:T(8,128)(2,1)} %up_ref.9, ...), custom_call_target="tpu_custom_call" | custom-call | flops 4831838208 | bytes 18874368 | tf_op jit(solution)/shard_map/expert/pallas_call | solution.py:99
  92.5 9.5 %expert.6 = (bf16[128,4096]{1,0:T(8,128)(2,1)S(1)}, bf16[128,4096]{1,0:T(8,128)(2,1)S(1)}) custom-call(f32[1,128]{1,0:T(1,128)S(1)} %and_convert_fusion.sel_ref, bf16[128,4224]{1,0:T(8,128)(2,1)S(1)} %constant_dynamic-update-slice_fusion.own_ref, bf16[128,4224]{1,0:T(8,128)(2,1)S(1)} %collective-permute-done.6.sib_ref, bf16[1,4096,1536]{2,1,0:T(8,128)(2,1)} %up_ref.9, ...), custom_call_target="tpu_custom_call" | custom-call | flops 4831838208 | bytes 18874368 | tf_op jit(solution)/shard_map/expert/pallas_call | solution.py:99
  104.3 1.6 %collective-permute-start.26 = (bf16[32,4096]{1,0:T(8,128)(2,1)S(1)}, bf16[32,4096]{1,0:T(8,128)(2,1)S(1)}, u32[]{:S(2)}, u32[]{:S(2)}) collective-permute-start(bf16[32,4096]{1,0:T(8,128)(2,1)S(1)} %get-tuple-element.26), channel_id=1, source_target_pairs={{0,2},{1,3},{4,0},{5,1},{8,4},{9,5},{12,8},{13,9},{14,12},{15,13},... | collective-permute-start | bytes 786440 | tf_op jit(solution)/shard_map/ppermute | solution.py:151
  108.4 7.3 %expert.5 = (bf16[64,4096]{1,0:T(8,128)(2,1)S(1)}, bf16[64,4096]{1,0:T(8,128)(2,1)S(1)}) custom-call(f32[1,128]{1,0:T(1,128)S(1)} %and_convert_fusion.sel_ref, bf16[64,4224]{1,0:T(8,128)(2,1)S(1)} %pad_maximum_fusion.own_ref, bf16[64,4224]{1,0:T(8,128)(2,1)S(1)} %collective-permute-done.sib_ref, bf16[1,4096,1536]{2,1,0:T(8,128)(2,1)} %up_ref.9, ...), custom_call_target="tpu_custom_call" | custom-call | flops 2415919104 | bytes 18874368 | tf_op jit(solution)/shard_map/expert/pallas_call | solution.py:99
  115.8 1.7 %collective-permute-done.32 = bf16[32,4096]{1,0:T(8,128)(2,1)S(1)} collective-permute-done((bf16[32,4096]{1,0:T(8,128)(2,1)S(1)}, bf16[32,4096]{1,0:T(8,128)(2,1)S(1)}, u32[]{:S(2)}, u32[]{:S(2)}) %collective-permute-start.32) | collective-permute-done | bytes 262176 | tf_op jit(solution)/shard_map/ppermute | solution.py:151
  119.4 1.6 %collective-permute-start.27 = (bf16[32,4096]{1,0:T(8,128)(2,1)S(1)}, bf16[32,4096]{1,0:T(8,128)(2,1)S(1)}, u32[]{:S(2)}, u32[]{:S(2)}) collective-permute-start(bf16[32,4096]{1,0:T(8,128)(2,1)S(1)} %get-tuple-element.22), channel_id=1, source_target_pairs={{0,2},{1,3},{4,0},{5,1},{8,4},{9,5},{12,8},{13,9},{14,12},{15,13},... | collective-permute-start | bytes 786440 | tf_op jit(solution)/shard_map/ppermute | solution.py:151
  121.4 1.6 %collective-permute-start.33 = (bf16[32,4096]{1,0:T(8,128)(2,1)S(1)}, bf16[32,4096]{1,0:T(8,128)(2,1)S(1)}, u32[]{:S(2)}, u32[]{:S(2)}) collective-permute-start(bf16[32,4096]{1,0:T(8,128)(2,1)S(1)} %get-tuple-element.24), channel_id=1, source_target_pairs={{0,2},{1,3},{4,0},{5,1},{8,4},{9,5},{12,8},{13,9},{14,12},{15,13},... | collective-permute-start | bytes 786440 | tf_op jit(solution)/shard_map/ppermute | solution.py:151
  123.5 3.8 %attend.1 = bf16[2,64,128]{2,1,0:T(8,128)(2,1)S(1)} custom-call(s32[2]{0:T(128)S(1)} %copy-done.2, bf16[2,64,128]{2,1,0:T(8,128)(2,1)S(1)} %bitcast.9, bf16[2,2,1024,512]{3,2,1,0:T(8,128)(2,1)S(1)} %copy-done.1), custom_call_target="tpu_custom_call" | custom-call | flops 67108864 | bytes 4194304 | tf_op jit(solution)/shard_map/attend/pallas_call | solution.py:48
  (101 shorter events, 34.0 us)
Async XLA Ops:
  7.2 13.7 %collective-permute-start.5 = (bf16[32,4224]{1,0:T(8,128)(2,1)S(1)}, bf16[32,4224]{1,0:T(8,128)(2,1)S(1)}, u32[]{:S(2)}, u32[]{:S(2)}) collective-permute-start(bf16[32,4224]{1,0:T(8,128)(2,1)S(1)} %get-tuple-element.38), channel_id=1, source_target_pairs={{0,2},{1,3},{4,0},{5,1},{8,4},{9,5},{12,8},{13,9},{14,12},{15,13},... | collective-permute-start | bytes 811016 | tf_op jit(solution)/shard_map/ppermute | solution.py:151
  9.2 11.1 %collective-permute-start.4 = (bf16[32,4224]{1,0:T(8,128)(2,1)S(1)}, bf16[32,4224]{1,0:T(8,128)(2,1)S(1)}, u32[]{:S(2)}, u32[]{:S(2)}) collective-permute-start(bf16[32,4224]{1,0:T(8,128)(2,1)S(1)} %get-tuple-element.38), channel_id=1, source_target_pairs={{0,4},{1,5},{4,8},{5,9},{8,12},{9,13},{12,14},{13,15},{14,10},{15,... | collective-permute-start | bytes 811016 | tf_op jit(solution)/shard_map/ppermute | solution.py:151
  14.5 10.8 %collective-permute-start.8 = (bf16[32,4224]{1,0:T(8,128)(2,1)S(1)}, bf16[32,4224]{1,0:T(8,128)(2,1)S(1)}, u32[]{:S(2)}, u32[]{:S(2)}) collective-permute-start(bf16[32,4224]{1,0:T(8,128)(2,1)S(1)} %collective-permute-done.2), channel_id=1, source_target_pairs={{0,4},{1,5},{4,8},{5,9},{8,12},{9,13},{12,14},{13,15},{14,10},{15,... | collective-permute-start | bytes 811016 | tf_op jit(solution)/shard_map/ppermute | solution.py:151
  21.0 70.8 %collective-permute-start.6 = (bf16[128,4224]{1,0:T(8,128)(2,1)S(1)}, bf16[128,4224]{1,0:T(8,128)(2,1)S(1)}, u32[]{:S(2)}, u32[]{:S(2)}) collective-permute-start(bf16[128,4224]{1,0:T(8,128)(2,1)S(1)} %constant_dynamic-update-slice_fusion.own_ref), channel_id=1, source_target_pairs={{0,1},{1,0},{2,3},{3,2},{4,5},{5,4},{6,7},{7,6},{8,9},{9,8},{10,11... | collective-permute-start | bytes 3244040 | tf_op jit(solution)/shard_map/ppermute | solution.py:151
  22.5 13.7 %collective-permute-start.9 = (bf16[32,4224]{1,0:T(8,128)(2,1)S(1)}, bf16[32,4224]{1,0:T(8,128)(2,1)S(1)}, u32[]{:S(2)}, u32[]{:S(2)}) collective-permute-start(bf16[32,4224]{1,0:T(8,128)(2,1)S(1)} %collective-permute-done.3), channel_id=1, source_target_pairs={{0,2},{1,3},{4,0},{5,1},{8,4},{9,5},{12,8},{13,9},{14,12},{15,13},... | collective-permute-start | bytes 811016 | tf_op jit(solution)/shard_map/ppermute | solution.py:151
  24.1 13.5 %collective-permute-start.10 = (bf16[32,4224]{1,0:T(8,128)(2,1)S(1)}, bf16[32,4224]{1,0:T(8,128)(2,1)S(1)}, u32[]{:S(2)}, u32[]{:S(2)}) collective-permute-start(bf16[32,4224]{1,0:T(8,128)(2,1)S(1)} %collective-permute-done.4), channel_id=1, source_target_pairs={{0,4},{1,5},{4,8},{5,9},{8,12},{9,13},{12,14},{13,15},{14,10},{15,... | collective-permute-start | bytes 811016 | tf_op jit(solution)/shard_map/ppermute | solution.py:151
  25.2 13.0 %collective-permute-start.14 = (bf16[32,4224]{1,0:T(8,128)(2,1)S(1)}, bf16[32,4224]{1,0:T(8,128)(2,1)S(1)}, u32[]{:S(2)}, u32[]{:S(2)}) collective-permute-start(bf16[32,4224]{1,0:T(8,128)(2,1)S(1)} %collective-permute-done.8), channel_id=1, source_target_pairs={{0,4},{1,5},{4,8},{5,9},{8,12},{9,13},{12,14},{13,15},{14,10},{15,... | collective-permute-start | bytes 811016 | tf_op jit(solution)/shard_map/ppermute | solution.py:151
  30.4 17.0 %collective-permute-start.17 = (bf16[32,4224]{1,0:T(8,128)(2,1)S(1)}, bf16[32,4224]{1,0:T(8,128)(2,1)S(1)}, u32[]{:S(2)}, u32[]{:S(2)}) collective-permute-start(bf16[32,4224]{1,0:T(8,128)(2,1)S(1)} %collective-permute-done.11), channel_id=1, source_target_pairs={{0,2},{1,3},{4,0},{5,1},{8,4},{9,5},{12,8},{13,9},{14,12},{15,13},... | collective-permute-start | bytes 811016 | tf_op jit(solution)/shard_map/ppermute | solution.py:151
  36.2 11.1 %collective-permute-start.15 = (bf16[32,4224]{1,0:T(8,128)(2,1)S(1)}, bf16[32,4224]{1,0:T(8,128)(2,1)S(1)}, u32[]{:S(2)}, u32[]{:S(2)}) collective-permute-start(bf16[32,4224]{1,0:T(8,128)(2,1)S(1)} %collective-permute-done.9), channel_id=1, source_target_pairs={{0,2},{1,3},{4,0},{5,1},{8,4},{9,5},{12,8},{13,9},{14,12},{15,13},... | collective-permute-start | bytes 811016 | tf_op jit(solution)/shard_map/ppermute | solution.py:151
  38.3 12.5 %collective-permute-start.20 = (bf16[32,4224]{1,0:T(8,128)(2,1)S(1)}, bf16[32,4224]{1,0:T(8,128)(2,1)S(1)}, u32[]{:S(2)}, u32[]{:S(2)}) collective-permute-start(bf16[32,4224]{1,0:T(8,128)(2,1)S(1)} %collective-permute-done.14), channel_id=1, source_target_pairs={{0,4},{1,5},{4,8},{5,9},{8,12},{9,13},{12,14},{13,15},{14,10},{15,... | collective-permute-start | bytes 811016 | tf_op jit(solution)/shard_map/ppermute | solution.py:151
  47.5 19.0 %collective-permute-start.18 = (bf16[128,4224]{1,0:T(8,128)(2,1)S(1)}, bf16[128,4224]{1,0:T(8,128)(2,1)S(1)}, u32[]{:S(2)}, u32[]{:S(2)}) collective-permute-start(bf16[128,4224]{1,0:T(8,128)(2,1)S(1)} %constant_dynamic-update-slice_fusion.8.own_ref), channel_id=1, source_target_pairs={{0,1},{1,0},{2,3},{3,2},{4,5},{5,4},{6,7},{7,6},{8,9},{9,8},{10,11... | collective-permute-start | bytes 3244040 | tf_op jit(solution)/shard_map/ppermute | solution.py:151
  66.0 12.4 %collective-permute-start.12 = (bf16[128,4224]{1,0:T(8,128)(2,1)S(1)}, bf16[128,4224]{1,0:T(8,128)(2,1)S(1)}, u32[]{:S(2)}, u32[]{:S(2)}) collective-permute-start(bf16[128,4224]{1,0:T(8,128)(2,1)S(1)} %constant_dynamic-update-slice_fusion.4.own_ref), channel_id=1, source_target_pairs={{0,1},{1,0},{2,3},{3,2},{4,5},{5,4},{6,7},{7,6},{8,9},{9,8},{10,11... | collective-permute-start | bytes 3244040 | tf_op jit(solution)/shard_map/ppermute | solution.py:151
  75.9 12.0 %collective-permute-start.19 = (bf16[128,4096]{1,0:T(8,128)(2,1)S(1)}, bf16[128,4096]{1,0:T(8,128)(2,1)S(1)}, u32[]{:S(2)}, u32[]{:S(2)}) collective-permute-start(bf16[128,4096]{1,0:T(8,128)(2,1)S(1)} %get-tuple-element.19), channel_id=1, source_target_pairs={{0,1},{1,0},{2,3},{3,2},{4,5},{5,4},{6,7},{7,6},{8,9},{9,8},{10,11... | collective-permute-start | bytes 3145736 | tf_op jit(solution)/shard_map/ppermute | solution.py:151
  76.3 11.7 %collective-permute-start.24 = (bf16[32,4096]{1,0:T(8,128)(2,1)S(1)}, bf16[32,4096]{1,0:T(8,128)(2,1)S(1)}, u32[]{:S(2)}, u32[]{:S(2)}) collective-permute-start(bf16[32,4096]{1,0:T(8,128)(2,1)S(1)} %get-tuple-element.36), channel_id=1, source_target_pairs={{0,2},{1,3},{4,0},{5,1},{8,4},{9,5},{12,8},{13,9},{14,12},{15,13},... | collective-permute-start | bytes 786440 | tf_op jit(solution)/shard_map/ppermute | solution.py:151
  87.9 14.1 %collective-permute-start.13 = (bf16[128,4096]{1,0:T(8,128)(2,1)S(1)}, bf16[128,4096]{1,0:T(8,128)(2,1)S(1)}, u32[]{:S(2)}, u32[]{:S(2)}) collective-permute-start(bf16[128,4096]{1,0:T(8,128)(2,1)S(1)} %get-tuple-element.17), channel_id=1, source_target_pairs={{0,1},{1,0},{2,3},{3,2},{4,5},{5,4},{6,7},{7,6},{8,9},{9,8},{10,11... | collective-permute-start | bytes 3145736 | tf_op jit(solution)/shard_map/ppermute | solution.py:151
  88.3 13.7 %collective-permute-start.25 = (bf16[32,4096]{1,0:T(8,128)(2,1)S(1)}, bf16[32,4096]{1,0:T(8,128)(2,1)S(1)}, u32[]{:S(2)}, u32[]{:S(2)}) collective-permute-start(bf16[32,4096]{1,0:T(8,128)(2,1)S(1)} %get-tuple-element.30), channel_id=1, source_target_pairs={{0,2},{1,3},{4,0},{5,1},{8,4},{9,5},{12,8},{13,9},{14,12},{15,13},... | collective-permute-start | bytes 786440 | tf_op jit(solution)/shard_map/ppermute | solution.py:151
  89.8 12.7 %collective-permute-start.28 = (bf16[32,4096]{1,0:T(8,128)(2,1)S(1)}, bf16[32,4096]{1,0:T(8,128)(2,1)S(1)}, u32[]{:S(2)}, u32[]{:S(2)}) collective-permute-start(bf16[32,4096]{1,0:T(8,128)(2,1)S(1)} %get-tuple-element.33), channel_id=1, source_target_pairs={{0,4},{1,5},{4,8},{5,9},{8,12},{9,13},{12,14},{13,15},{14,10},{15,... | collective-permute-start | bytes 786440 | tf_op jit(solution)/shard_map/ppermute | solution.py:151
  90.4 12.3 %collective-permute-start.31 = (bf16[32,4096]{1,0:T(8,128)(2,1)S(1)}, bf16[32,4096]{1,0:T(8,128)(2,1)S(1)}, u32[]{:S(2)}, u32[]{:S(2)}) collective-permute-start(bf16[32,4096]{1,0:T(8,128)(2,1)S(1)} %get-tuple-element.32), channel_id=1, source_target_pairs={{0,2},{1,3},{4,0},{5,1},{8,4},{9,5},{12,8},{13,9},{14,12},{15,13},... | collective-permute-start | bytes 786440 | tf_op jit(solution)/shard_map/ppermute | solution.py:151
  91.8 12.0 %collective-permute-start.35 = (bf16[32,4096]{1,0:T(8,128)(2,1)S(1)}, bf16[32,4096]{1,0:T(8,128)(2,1)S(1)}, u32[]{:S(2)}, u32[]{:S(2)}) collective-permute-start(bf16[32,4096]{1,0:T(8,128)(2,1)S(1)} %get-tuple-element.31), channel_id=1, source_target_pairs={{0,4},{1,5},{4,8},{5,9},{8,12},{9,13},{12,14},{13,15},{14,10},{15,... | collective-permute-start | bytes 786440 | tf_op jit(solution)/shard_map/ppermute | solution.py:151
  102.1 13.7 %collective-permute-start.7 = (bf16[128,4096]{1,0:T(8,128)(2,1)S(1)}, bf16[128,4096]{1,0:T(8,128)(2,1)S(1)}, u32[]{:S(2)}, u32[]{:S(2)}) collective-permute-start(bf16[128,4096]{1,0:T(8,128)(2,1)S(1)} %get-tuple-element.15), channel_id=1, source_target_pairs={{0,1},{1,0},{2,3},{3,2},{4,5},{5,4},{6,7},{7,6},{8,9},{9,8},{10,11... | collective-permute-start | bytes 3145736 | tf_op jit(solution)/shard_map/ppermute | solution.py:151
  104.3 11.5 %collective-permute-start.26 = (bf16[32,4096]{1,0:T(8,128)(2,1)S(1)}, bf16[32,4096]{1,0:T(8,128)(2,1)S(1)}, u32[]{:S(2)}, u32[]{:S(2)}) collective-permute-start(bf16[32,4096]{1,0:T(8,128)(2,1)S(1)} %get-tuple-element.26), channel_id=1, source_target_pairs={{0,2},{1,3},{4,0},{5,1},{8,4},{9,5},{12,8},{13,9},{14,12},{15,13},... | collective-permute-start | bytes 786440 | tf_op jit(solution)/shard_map/ppermute | solution.py:151
  106.4 11.2 %collective-permute-start.32 = (bf16[32,4096]{1,0:T(8,128)(2,1)S(1)}, bf16[32,4096]{1,0:T(8,128)(2,1)S(1)}, u32[]{:S(2)}, u32[]{:S(2)}) collective-permute-start(bf16[32,4096]{1,0:T(8,128)(2,1)S(1)} %get-tuple-element.28), channel_id=1, source_target_pairs={{0,2},{1,3},{4,0},{5,1},{8,4},{9,5},{12,8},{13,9},{14,12},{15,13},... | collective-permute-start | bytes 786440 | tf_op jit(solution)/shard_map/ppermute | solution.py:151
  108.0 10.9 %collective-permute-start.36 = (bf16[32,4096]{1,0:T(8,128)(2,1)S(1)}, bf16[32,4096]{1,0:T(8,128)(2,1)S(1)}, u32[]{:S(2)}, u32[]{:S(2)}) collective-permute-start(bf16[32,4096]{1,0:T(8,128)(2,1)S(1)} %get-tuple-element.27), channel_id=1, source_target_pairs={{0,4},{1,5},{4,8},{5,9},{8,12},{9,13},{12,14},{13,15},{14,10},{15,... | collective-permute-start | bytes 786440 | tf_op jit(solution)/shard_map/ppermute | solution.py:151
  115.7 12.3 %collective-permute-start.1 = (bf16[64,4096]{1,0:T(8,128)(2,1)S(1)}, bf16[64,4096]{1,0:T(8,128)(2,1)S(1)}, u32[]{:S(2)}, u32[]{:S(2)}) collective-permute-start(bf16[64,4096]{1,0:T(8,128)(2,1)S(1)} %get-tuple-element.13), channel_id=1, source_target_pairs={{0,1},{1,0},{2,3},{3,2},{4,5},{5,4},{6,7},{7,6},{8,9},{9,8},{10,11... | collective-permute-start | bytes 1572872 | tf_op jit(solution)/shard_map/ppermute | solution.py:151
  (19 other events, 198.8 us)

commit v2 on v0

v2 whole, which is shorter than its diff:
```python
import functools

import jax
import jax.numpy as jnp
from jax import lax
from jax.experimental import pallas as pl
from jax.experimental.pallas import tpu as pltpu
from jax.sharding import PartitionSpec as P

HEADS = 64
KVH = 4
HD = 128
CTX = 1024
LANES = 128
CHUNKS = 2


def attend_kernel(lengths_ref, q_ref, kv_hbm, o_ref, kv, sems):
    requests = q_ref.shape[0]
    copies = [
        pltpu.make_async_copy(kv_hbm.at[r], kv.at[r], sems.at[r]) for r in range(requests)
    ]
    for copy in copies:
        copy.start()
    group_size = HEADS // KVH
    position = lax.broadcasted_iota(jnp.int32, (group_size, CTX), 1)
    for r in range(requests):
        visible = position < lengths_ref[r]
        copies[r].wait()
        for g in range(KVH):
            q = q_ref[r, g * group_size : (g + 1) * group_size, :]
            keys = kv[r, 0, :, g * HD : (g + 1) * HD]
            values = kv[r, 1, :, g * HD : (g + 1) * HD]
            scores = lax.dot_general(
                q, keys, (((1,), (1,)), ((), ())), preferred_element_type=jnp.float32
            ) * HD ** (-0.5)
            scores = jnp.where(visible, scores, -jnp.inf)
            raised = jnp.exp(scores - jnp.max(scores, axis=-1, keepdims=True))
            weights = (raised / jnp.sum(raised, axis=-1, keepdims=True)).astype(jnp.bfloat16)
            mixed = jnp.dot(weights, values, preferred_element_type=jnp.float32)
            o_ref[r, g * group_size : (g + 1) * group_size, :] = mixed.astype(jnp.bfloat16)


def attend_local(queries, kv_cache, lengths):
    requests = queries.shape[0]
    whole = pl.BlockSpec(memory_space=pltpu.VMEM)
    out = pl.pallas_call(
        attend_kernel,
        in_specs=[
            pl.BlockSpec(memory_space=pltpu.SMEM),
            whole,
            pl.BlockSpec(memory_space=pl.ANY),
        ],
        out_specs=whole,
        out_shape=jax.ShapeDtypeStruct((requests, HEADS, HD), jnp.bfloat16),
        scratch_shapes=[
            pltpu.VMEM(kv_cache.shape, kv_cache.dtype),
            pltpu.SemaphoreType.DMA((requests,)),
        ],
        compiler_params=pltpu.CompilerParams(vmem_limit_bytes=6 << 20),
        cost_estimate=pl.CostEstimate(
            flops=requests * 4 * HEADS * CTX * HD,
            bytes_accessed=2 * kv_cache.size,
            transcendentals=requests * HEADS * CTX,
        ),
        name="attend",
    )(
        lengths,
        queries.reshape(requests, HEADS, HD),
        pltpu.with_memory_space_constraint(kv_cache, pltpu.HBM),
    )
    return out.reshape(requests, HEADS * HD)


def expert_kernel(experts, own_ref, sib_ref, in_ref, down_ref, out_own, out_sib, x, hidden):
    rows = own_ref.shape[0]
    _, ff, width = down_ref.shape
    block = 256
    out_block = 1024
    x[:rows, :] = own_ref[:, :width]
    x[rows:, :] = sib_ref[:, :width]
    for n in range(0, ff, block):
        gate = jnp.dot(x[...], in_ref[0, :, n : n + block], preferred_element_type=jnp.float32)
        up = jnp.dot(
            x[...], in_ref[0, :, ff + n : ff + n + block], preferred_element_type=jnp.float32
        )
        hidden[:, n : n + block] = (jax.nn.silu(gate) * up).astype(jnp.bfloat16)
    lane = lax.broadcasted_iota(jnp.int32, (rows, LANES), 1)
    mine = (lax.rem(lane, experts) == lax.axis_index("expert")) & (lane < 3 * experts)
    own_coef, sib_coef = [
        jnp.sum(
            jnp.where(mine, ref[:, width:].astype(jnp.float32), 0.0), axis=1, keepdims=True
        )
        for ref in (own_ref, sib_ref)
    ]
    for n in range(0, width, out_block):
        part = jnp.dot(
            hidden[...], down_ref[0, :, n : n + out_block], preferred_element_type=jnp.float32
        )
        out_own[:, n : n + out_block] = (part[:rows] * own_coef).astype(jnp.bfloat16)
        out_sib[:, n : n + out_block] = (part[rows:] * sib_coef).astype(jnp.bfloat16)


def expert_apply(experts, own, sib, w_gate_up, w_down):
    rows, wide = own.shape
    _, ff, width = w_down.shape
    shape = jax.ShapeDtypeStruct((rows, width), jnp.bfloat16)
    whole = pl.BlockSpec(memory_space=pltpu.VMEM)
    return pl.pallas_call(
        functools.partial(expert_kernel, experts),
        in_specs=[whole] * 4,
        out_specs=[whole] * 2,
        out_shape=[shape, shape],
        scratch_shapes=[
            pltpu.VMEM((2 * rows, width), jnp.bfloat16),
            pltpu.VMEM((2 * rows, ff), jnp.bfloat16),
        ],
        compiler_params=pltpu.CompilerParams(vmem_limit_bytes=6 << 20),
        cost_estimate=pl.CostEstimate(
            flops=2 * 2 * rows * width * ff * 3,
            bytes_accessed=8 * rows * width,
            transcendentals=0,
        ),
        name="expert",
    )(
        own,
        sib,
        *(pltpu.with_memory_space_constraint(x, pltpu.VMEM) for x in (w_gate_up, w_down)),
    )


def prologue_kernel(experts, x_ref, ids_ref, weights_ref, *chunk_refs):
    tokens, width = x_ref.shape
    ids = ids_ref[...].T
    raw = weights_ref[...].T
    top = ids.shape[1]
    rows = tokens // len(chunk_refs)
    lane = lax.broadcasted_iota(jnp.int32, (tokens, LANES), 1)
    named = lax.rem(lane, experts)
    share = raw / jnp.sum(raw, axis=1, keepdims=True)
    coef = jnp.zeros((tokens, LANES), jnp.float32)
    for k in range(top):
        coef = coef + jnp.where(ids[:, k : k + 1] == named, share[:, k : k + 1], 0.0)
    high = coef.astype(jnp.bfloat16).astype(jnp.float32)
    middle = (coef - high).astype(jnp.bfloat16).astype(jnp.float32)
    low = coef - high - middle
    parts = jnp.where(lane < experts, high, jnp.where(lane < 2 * experts, middle, low))
    parts = jnp.where(lane < 3 * experts, parts, 0.0).astype(jnp.bfloat16)
    for k, ref in enumerate(chunk_refs):
        ref[:, :width] = x_ref[k * rows : (k + 1) * rows, :]
        ref[:, width:] = parts[k * rows : (k + 1) * rows, :]


def prologue(moe_input, route_ids, route_weights, experts):
    tokens, width = moe_input.shape
    whole = pl.BlockSpec(memory_space=pltpu.VMEM)
    shapes = [
        jax.ShapeDtypeStruct((n, width + LANES), jnp.bfloat16)
        for n in [tokens // CHUNKS] * CHUNKS
    ]
    return pl.pallas_call(
        functools.partial(prologue_kernel, experts),
        in_specs=[whole] * 3,
        out_specs=[whole] * len(shapes),
        out_shape=shapes,
        compiler_params=pltpu.CompilerParams(vmem_limit_bytes=4 << 20),
        name="prologue",
    )(moe_input, route_ids.T, route_weights.T)


def shards(order, queries, kv_cache, lengths, moe_input, route_ids, route_weights, w_gate_up, w_down):
    experts = lax.axis_size("expert")
    chips = len(order)
    half = chips // 2
    rows = moe_input.shape[0] // CHUNKS

    def ring(step):
        return [
            (2 * order[i] + c, 2 * order[(i + step) % chips] + c)
            for i in range(chips)
            for c in range(2)
        ]

    forward, backward = ring(1), ring(-1)
    swap = [(i, i ^ 1) for i in range(experts)]

    def send(x, pairs):
        return lax.ppermute(x, "expert", pairs)

    first = prologue(moe_input, route_ids, route_weights, experts)
    attended = attend_local(queries, kv_cache, lengths)

    long_pair = (("f", 0), ("b", 1))
    short_pair = (("b", 0), ("f", 1))
    outward = {"f": forward, "b": backward}
    homeward = {"f": backward, "b": forward}

    def tie(anchor, group, values):
        anchor, got = lax.optimization_barrier((anchor, [values[key] for key in group]))
        values.update(zip(group, got))
        return anchor

    def compute(keys, own):
        slots = {key: i * rows for i, key in enumerate(keys)}
        own = jnp.concatenate(own, axis=0)
        mine, theirs = expert_apply(experts, own, send(own, swap), w_gate_up, w_down)
        return [slots, mine, send(theirs, swap)]

    moving = {key: first[key[1]] for key in long_pair + short_pair}
    partial = {}

    def tie_partial(block, index, group, values):
        block[index] = tie(block[index], group, values)

    for s in range(1, half + 2):
        for group in (long_pair, short_pair):
            if group is short_pair and s > half:
                continue
            if s == 2 and group is short_pair:
                attended = tie(attended, group, moving)
            if s > 2:
                tie_partial(partial[s - 2, group], 1, group, moving)
            before = (s - 3, short_pair) if group is long_pair else (s - 2, long_pair)
            if before in partial:
                tie_partial(partial[before], 2, group, moving)
            own = {key: moving[key] for key in group}
            if s < half or (group is long_pair and s == half):
                for key in group:
                    moving[key] = send(moving[key], outward[key[0]])
            if s > 1:
                partial[s - 1, group] = compute(list(own), list(own.values()))
    anchor = partial[half, long_pair]
    anchor[1], first = lax.optimization_barrier((anchor[1], first))
    own_rows = compute(list(range(CHUNKS)), first)

    def local(block, key):
        slots, mine, theirs = block
        span = slice(slots[key], slots[key] + rows)
        return mine[span].astype(jnp.float32) + theirs[span].astype(jnp.float32)

    moving = {}
    last = None
    for s in range(half, 0, -1):
        for group in (short_pair, long_pair) if s < half else (long_pair,):
            if last is not None and group[0] in moving:
                last = tie(last, group, moving)
            if s == 1:
                tie_partial(own_rows, 2, group, moving)
            totals = []
            for key in group:
                total = local(partial[s, group], key)
                if key in moving:
                    total = total + moving[key].astype(jnp.float32)
                totals.append(total.astype(jnp.bfloat16))
            last = totals
            for key, total in zip(group, last):
                moving[key] = send(total, homeward[key[0]])
    out = []
    for k in range(CHUNKS):
        total = local(own_rows, k)
        for way in ("f", "b"):
            total = total + moving[way, k].astype(jnp.float32)
        out.append(total.astype(jnp.bfloat16))
    return attended, jnp.concatenate(out, axis=0)


def solution(mesh):
    chips = mesh.shape["expert"] // 2
    if mesh.shape["groups"] == 2:
        order = list(range(0, chips, 2)) + list(range(chips - 1, 0, -2))
    else:
        order = list(range(chips))
    placed = (
        P(("groups", "expert"), None),
        P(("groups", "expert"), None, None, None),
        P(("groups", "expert")),
        P(("groups", "expert"), None),
        P(("groups", "expert"), None),
        P(("groups", "expert"), None),
        P("expert", None, None),
        P("expert", None, None),
    )
    return jax.shard_map(
        functools.partial(shards, order),
        mesh=mesh,
        in_specs=placed,
        out_specs=(P(("groups", "expert"), None), P(("groups", "expert"), None)),
        check_vma=False,
    )
```

time: 341 us -> 110 us (0.32)
  the two profiles are of different devices: /device:TPU:13 before, /device:TPU:0 now
where the time goes in v2:
time: 110 us
  starting transfers between devices  35.6 us (32%)
  waiting for transfers between devices  33.9 us (31%)
  Pallas kernels  27.5 us (25%)
  local copies, waits for them, and re-layouts  9.8 us (9%)
  other arithmetic  2.29 us (2%)
    ppermute x44, starting transfers between devices, send(): return lax.ppermute(x, 'expert', pairs)  35.6 us
    ppermute x44, waiting for transfers between devices, send(): return lax.ppermute(x, 'expert', pairs)  33.9 us
    pallas_call x8, Pallas kernels, expert_apply(): pl.pallas_call(functools.partial(expert_kernel, experts), in_specs=[whole...  21.6 us
    unnamed x24, local copies, waits for them, and re-layouts  9.59 us
    pallas_call x1, Pallas kernels, attend_local(): pl.pallas_call(attend_kernel, in_specs=[pl.BlockSpec(memory_space=pltpu.S...  5.44 us
  transfers between devices with their start and end apart: 44, of which 16 were waited for; matrix products, arithmetic and copies ran while one was open for 3% of the time, Pallas kernels for 25%

profile of v2, /device:TPU:0, one launch (start us, length us, event | category | flops | bytes accessed | tf_op | source)
XLA Modules:
  0.0 110.1 jit_solution(15974840407502455799)
XLA Ops:
  4.0 3.0 %collective-permute-start = (bf16[32,4224]{1,0:T(8,128)(2,1)S(1)}, bf16[32,4224]{1,0:T(8,128)(2,1)S(1)}, u32[]{:S(2)}, u32[]{:S(2)}) collective-permute-start(bf16[32,4224]{1,0:T(8,128)(2,1)S(1)} %get-tuple-element.96), channel_id=1, source_target_pairs={{0,2},{1,3},{4,0},{5,1},{8,4},{9,5},{12,8},{13,9},{14,12},{15,13},... | collective-permute-start | bytes 811016 | tf_op jit(solution)/shard_map/ppermute | solution.py:188
  7.1 2.0 %collective-permute-start.2 = (bf16[32,4224]{1,0:T(8,128)(2,1)S(1)}, bf16[32,4224]{1,0:T(8,128)(2,1)S(1)}, u32[]{:S(2)}, u32[]{:S(2)}) collective-permute-start(bf16[32,4224]{1,0:T(8,128)(2,1)S(1)} %get-tuple-element.96), channel_id=1, source_target_pairs={{0,4},{1,5},{4,8},{5,9},{8,12},{9,13},{12,14},{13,15},{14,10},{15,... | collective-permute-start | bytes 811016 | tf_op jit(solution)/shard_map/ppermute | solution.py:188
  10.6 5.4 %attend.1 = bf16[2,64,128]{2,1,0:T(8,128)(2,1)S(1)} custom-call(s32[2]{0:T(128)S(1)} %copy-done.6, bf16[2,64,128]{2,1,0:T(8,128)(2,1)S(1)} %bitcast.11, bf16[2,2,1024,512]{3,2,1,0:T(8,128)(2,1)} %kv_hbm.1), custom_call_target="tpu_custom_call" | custom-call | flops 67108864 | bytes 4194304 | tf_op jit(solution)/shard_map/attend/pallas_call | solution.py:47
  16.7 2.0 %collective-permute-start.7 = (bf16[32,4224]{1,0:T(8,128)(2,1)S(1)}, bf16[32,4224]{1,0:T(8,128)(2,1)S(1)}, u32[]{:S(2)}, u32[]{:S(2)}) collective-permute-start(bf16[32,4224]{1,0:T(8,128)(2,1)S(1)} %collective-permute-done), channel_id=1, source_target_pairs={{0,2},{1,3},{4,0},{5,1},{8,4},{9,5},{12,8},{13,9},{14,12},{15,13},... | collective-permute-start | bytes 811016 | tf_op jit(solution)/shard_map/ppermute | solution.py:188
  18.7 2.1 %collective-permute-done.2 = bf16[32,4224]{1,0:T(8,128)(2,1)S(1)} collective-permute-done((bf16[32,4224]{1,0:T(8,128)(2,1)S(1)}, bf16[32,4224]{1,0:T(8,128)(2,1)S(1)}, u32[]{:S(2)}, u32[]{:S(2)}) %collective-permute-start.2) | collective-permute-done | bytes 270368 | tf_op jit(solution)/shard_map/ppermute | solution.py:188
  24.4 4.6 %copy-done = bf16[1,4096,1536]{2,1,0:T(8,128)(2,1)S(1)} copy-done((bf16[1,4096,1536]{2,1,0:T(8,128)(2,1)S(1)}, bf16[1,4096,1536]{2,1,0:T(8,128)(2,1)}, u32[]{:S(2)}) %copy-start) | copy-done | bytes 12582936
  29.0 2.7 %expert.8 = (bf16[64,4096]{1,0:T(8,128)(2,1)S(1)}, bf16[64,4096]{1,0:T(8,128)(2,1)S(1)}) custom-call(bf16[64,4224]{1,0:T(8,128)(2,1)S(1)} %constant_dynamic-update-slice_fusion.own_ref, bf16[64,4224]{1,0:T(8,128)(2,1)S(1)} %collective-permute-done.4.sib_ref, bf16[1,4096,1536]{2,1,0:T(8,128)(2,1)S(1)} %copy-done, bf16[1,768,4096]{2,1,0:T(8,128)(2,1)S(1)} %copy-done.2), custom_call_target="tpu_custom_call" | custom-call | flops 2415919104 | bytes 2097152 | tf_op jit(solution)/shard_map/expert/pallas_call | solution.py:109
  31.6 3.9 %collective-permute-done.12 = bf16[32,4224]{1,0:T(8,128)(2,1)S(1)} collective-permute-done((bf16[32,4224]{1,0:T(8,128)(2,1)S(1)}, bf16[32,4224]{1,0:T(8,128)(2,1)S(1)}, u32[]{:S(2)}, u32[]{:S(2)}) %collective-permute-start.12) | collective-permute-done | bytes 270368 | tf_op jit(solution)/shard_map/ppermute | solution.py:188
  37.8 2.7 %expert.9 = (bf16[64,4096]{1,0:T(8,128)(2,1)S(1)}, bf16[64,4096]{1,0:T(8,128)(2,1)S(1)}) custom-call(bf16[64,4224]{1,0:T(8,128)(2,1)S(1)} %constant_dynamic-update-slice_fusion.2.own_ref, bf16[64,4224]{1,0:T(8,128)(2,1)S(1)} %collective-permute-done.6.sib_ref, bf16[1,4096,1536]{2,1,0:T(8,128)(2,1)S(1)} %copy-done.1, bf16[1,768,4096]{2,1,0:T(8,128)(2,1)S(1)} %copy-done.2), custom_call_target="tpu_custom_call" | custom-call | flops 2415919104 | bytes 2097152 | tf_op jit(solution)/shard_map/expert/pallas_call | solution.py:109
  41.1 1.6 %collective-permute-start.24 = (bf16[32,4224]{1,0:T(8,128)(2,1)S(1)}, bf16[32,4224]{1,0:T(8,128)(2,1)S(1)}, u32[]{:S(2)}, u32[]{:S(2)}) collective-permute-start(bf16[32,4224]{1,0:T(8,128)(2,1)S(1)} %collective-permute-done.7), channel_id=1, source_target_pairs={{0,2},{1,3},{4,0},{5,1},{8,4},{9,5},{12,8},{13,9},{14,12},{15,13},... | collective-permute-start | bytes 811016 | tf_op jit(solution)/shard_map/ppermute | solution.py:188
  43.7 2.7 %expert.11 = (bf16[64,4096]{1,0:T(8,128)(2,1)S(1)}, bf16[64,4096]{1,0:T(8,128)(2,1)S(1)}) custom-call(bf16[64,4224]{1,0:T(8,128)(2,1)S(1)} %constant_dynamic-update-slice_fusion.6.own_ref, bf16[64,4224]{1,0:T(8,128)(2,1)S(1)} %collective-permute-done.14.sib_ref, bf16[1,4096,1536]{2,1,0:T(8,128)(2,1)S(1)} %copy-done.1, bf16[1,768,4096]{2,1,0:T(8,128)(2,1)S(1)} %copy-done.2), custom_call_target="tpu_custom_call" | custom-call | flops 2415919104 | bytes 2097152 | tf_op jit(solution)/shard_map/expert/pallas_call | solution.py:109
  46.6 1.6 %collective-permute-start.18 = (bf16[32,4224]{1,0:T(8,128)(2,1)S(1)}, bf16[32,4224]{1,0:T(8,128)(2,1)S(1)}, u32[]{:S(2)}, u32[]{:S(2)}) collective-permute-start(bf16[32,4224]{1,0:T(8,128)(2,1)S(1)} %collective-permute-done.15), channel_id=1, source_target_pairs={{0,4},{1,5},{4,8},{5,9},{8,12},{9,13},{12,14},{13,15},{14,10},{15,... | collective-permute-start | bytes 811016 | tf_op jit(solution)/shard_map/ppermute | solution.py:188
  49.5 2.7 %expert.10 = (bf16[64,4096]{1,0:T(8,128)(2,1)S(1)}, bf16[64,4096]{1,0:T(8,128)(2,1)S(1)}) custom-call(bf16[64,4224]{1,0:T(8,128)(2,1)S(1)} %constant_dynamic-update-slice_fusion.4.own_ref, bf16[64,4224]{1,0:T(8,128)(2,1)S(1)} %collective-permute-done.9.sib_ref, bf16[1,4096,1536]{2,1,0:T(8,128)(2,1)S(1)} %copy-done.1, bf16[1,768,4096]{2,1,0:T(8,128)(2,1)S(1)} %copy-done.2), custom_call_target="tpu_custom_call" | custom-call | flops 2415919104 | bytes 2097152 | tf_op jit(solution)/shard_map/expert/pallas_call | solution.py:109
  54.2 2.7 %expert.12 = (bf16[64,4096]{1,0:T(8,128)(2,1)S(1)}, bf16[64,4096]{1,0:T(8,128)(2,1)S(1)}) custom-call(bf16[64,4224]{1,0:T(8,128)(2,1)S(1)} %constant_dynamic-update-slice_fusion.8.own_ref, bf16[64,4224]{1,0:T(8,128)(2,1)S(1)} %collective-permute-done.17.sib_ref, bf16[1,4096,1536]{2,1,0:T(8,128)(2,1)S(1)} %copy-done.1, bf16[1,768,4096]{2,1,0:T(8,128)(2,1)S(1)} %copy-done.2), custom_call_target="tpu_custom_call" | custom-call | flops 2415919104 | bytes 2097152 | tf_op jit(solution)/shard_map/expert/pallas_call | solution.py:109
  58.1 2.7 %expert.15 = (bf16[64,4096]{1,0:T(8,128)(2,1)S(1)}, bf16[64,4096]{1,0:T(8,128)(2,1)S(1)}) custom-call(bf16[64,4224]{1,0:T(8,128)(2,1)S(1)} %constant_dynamic-update-slice_fusion.14.own_ref, bf16[64,4224]{1,0:T(8,128)(2,1)S(1)} %collective-permute-done.27.sib_ref, bf16[1,4096,1536]{2,1,0:T(8,128)(2,1)S(1)} %copy-done.1, bf16[1,768,4096]{2,1,0:T(8,128)(2,1)S(1)} %copy-done.2), custom_call_target="tpu_custom_call" | custom-call | flops 2415919104 | bytes 2097152 | tf_op jit(solution)/shard_map/expert/pallas_call | solution.py:109
  61.0 2.7 %expert.13 = (bf16[64,4096]{1,0:T(8,128)(2,1)S(1)}, bf16[64,4096]{1,0:T(8,128)(2,1)S(1)}) custom-call(bf16[64,4224]{1,0:T(8,128)(2,1)S(1)} %constant_dynamic-update-slice_fusion.10.own_ref, bf16[64,4224]{1,0:T(8,128)(2,1)S(1)} %collective-permute-done.20.sib_ref, bf16[1,4096,1536]{2,1,0:T(8,128)(2,1)S(1)} %copy-done.1, bf16[1,768,4096]{2,1,0:T(8,128)(2,1)S(1)} %copy-done.2), custom_call_target="tpu_custom_call" | custom-call | flops 2415919104 | bytes 2097152 | tf_op jit(solution)/shard_map/expert/pallas_call | solution.py:109
  70.2 2.7 %expert.14 = (bf16[64,4096]{1,0:T(8,128)(2,1)S(1)}, bf16[64,4096]{1,0:T(8,128)(2,1)S(1)}) custom-call(bf16[64,4224]{1,0:T(8,128)(2,1)S(1)} %constant_dynamic-update-slice_fusion.12.own_ref, bf16[64,4224]{1,0:T(8,128)(2,1)S(1)} %collective-permute-done.21.sib_ref, bf16[1,4096,1536]{2,1,0:T(8,128)(2,1)S(1)} %copy-done.1, bf16[1,768,4096]{2,1,0:T(8,128)(2,1)S(1)} %copy-done.2), custom_call_target="tpu_custom_call" | custom-call | flops 2415919104 | bytes 2097152 | tf_op jit(solution)/shard_map/expert/pallas_call | solution.py:109
  72.9 2.2 %collective-permute-done.30 = bf16[32,4096]{1,0:T(8,128)(2,1)S(1)} collective-permute-done((bf16[32,4096]{1,0:T(8,128)(2,1)S(1)}, bf16[32,4096]{1,0:T(8,128)(2,1)S(1)}, u32[]{:S(2)}, u32[]{:S(2)}) %collective-permute-start.30) | collective-permute-done | bytes 262176 | tf_op jit(solution)/shard_map/ppermute | solution.py:188
  78.5 3.3 %collective-permute-done.32 = bf16[32,4096]{1,0:T(8,128)(2,1)S(1)} collective-permute-done((bf16[32,4096]{1,0:T(8,128)(2,1)S(1)}, bf16[32,4096]{1,0:T(8,128)(2,1)S(1)}, u32[]{:S(2)}, u32[]{:S(2)}) %collective-permute-start.32) | collective-permute-done | bytes 262176 | tf_op jit(solution)/shard_map/ppermute | solution.py:188
  84.1 2.2 %collective-permute-done.34 = bf16[32,4096]{1,0:T(8,128)(2,1)S(1)} collective-permute-done((bf16[32,4096]{1,0:T(8,128)(2,1)S(1)}, bf16[32,4096]{1,0:T(8,128)(2,1)S(1)}, u32[]{:S(2)}, u32[]{:S(2)}) %collective-permute-start.34) | collective-permute-done | bytes 262176 | tf_op jit(solution)/shard_map/ppermute | solution.py:188
  89.7 3.3 %collective-permute-done.36 = bf16[32,4096]{1,0:T(8,128)(2,1)S(1)} collective-permute-done((bf16[32,4096]{1,0:T(8,128)(2,1)S(1)}, bf16[32,4096]{1,0:T(8,128)(2,1)S(1)}, u32[]{:S(2)}, u32[]{:S(2)}) %collective-permute-start.36) | collective-permute-done | bytes 262176 | tf_op jit(solution)/shard_map/ppermute | solution.py:188
  95.3 2.5 %collective-permute-done.38 = bf16[32,4096]{1,0:T(8,128)(2,1)S(1)} collective-permute-done((bf16[32,4096]{1,0:T(8,128)(2,1)S(1)}, bf16[32,4096]{1,0:T(8,128)(2,1)S(1)}, u32[]{:S(2)}, u32[]{:S(2)}) %collective-permute-start.38) | collective-permute-done | bytes 262176 | tf_op jit(solution)/shard_map/ppermute | solution.py:188
  100.9 3.3 %collective-permute-done.41 = bf16[32,4096]{1,0:T(8,128)(2,1)S(1)} collective-permute-done((bf16[32,4096]{1,0:T(8,128)(2,1)S(1)}, bf16[32,4096]{1,0:T(8,128)(2,1)S(1)}, u32[]{:S(2)}, u32[]{:S(2)}) %collective-permute-start.41) | collective-permute-done | bytes 262176 | tf_op jit(solution)/shard_map/ppermute | solution.py:188
  104.3 3.9 %collective-permute-done.40 = bf16[32,4096]{1,0:T(8,128)(2,1)S(1)} collective-permute-done((bf16[32,4096]{1,0:T(8,128)(2,1)S(1)}, bf16[32,4096]{1,0:T(8,128)(2,1)S(1)}, u32[]{:S(2)}, u32[]{:S(2)}) %collective-permute-start.40) | collective-permute-done | bytes 262176 | tf_op jit(solution)/shard_map/ppermute | solution.py:188
  (115 shorter events, 40.4 us)
Async XLA Ops:
  4.0 12.7 %collective-permute-start = (bf16[32,4224]{1,0:T(8,128)(2,1)S(1)}, bf16[32,4224]{1,0:T(8,128)(2,1)S(1)}, u32[]{:S(2)}, u32[]{:S(2)}) collective-permute-start(bf16[32,4224]{1,0:T(8,128)(2,1)S(1)} %get-tuple-element.96), channel_id=1, source_target_pairs={{0,2},{1,3},{4,0},{5,1},{8,4},{9,5},{12,8},{13,9},{14,12},{15,13},... | collective-permute-start | bytes 811016 | tf_op jit(solution)/shard_map/ppermute | solution.py:188
  7.0 9.7 %collective-permute-start.1 = (bf16[32,4224]{1,0:T(8,128)(2,1)S(1)}, bf16[32,4224]{1,0:T(8,128)(2,1)S(1)}, u32[]{:S(2)}, u32[]{:S(2)}) collective-permute-start(bf16[32,4224]{1,0:T(8,128)(2,1)S(1)} %get-tuple-element.97), channel_id=1, source_target_pairs={{0,4},{1,5},{4,8},{5,9},{8,12},{9,13},{12,14},{13,15},{14,10},{15,... | collective-permute-start | bytes 811016 | tf_op jit(solution)/shard_map/ppermute | solution.py:188
  7.1 13.6 %collective-permute-start.2 = (bf16[32,4224]{1,0:T(8,128)(2,1)S(1)}, bf16[32,4224]{1,0:T(8,128)(2,1)S(1)}, u32[]{:S(2)}, u32[]{:S(2)}) collective-permute-start(bf16[32,4224]{1,0:T(8,128)(2,1)S(1)} %get-tuple-element.96), channel_id=1, source_target_pairs={{0,4},{1,5},{4,8},{5,9},{8,12},{9,13},{12,14},{13,15},{14,10},{15,... | collective-permute-start | bytes 811016 | tf_op jit(solution)/shard_map/ppermute | solution.py:188
  9.1 11.7 %collective-permute-start.3 = (bf16[32,4224]{1,0:T(8,128)(2,1)S(1)}, bf16[32,4224]{1,0:T(8,128)(2,1)S(1)}, u32[]{:S(2)}, u32[]{:S(2)}) collective-permute-start(bf16[32,4224]{1,0:T(8,128)(2,1)S(1)} %get-tuple-element.97), channel_id=1, source_target_pairs={{0,2},{1,3},{4,0},{5,1},{8,4},{9,5},{12,8},{13,9},{14,12},{15,13},... | collective-permute-start | bytes 811016 | tf_op jit(solution)/shard_map/ppermute | solution.py:188
  16.7 23.8 %collective-permute-start.7 = (bf16[32,4224]{1,0:T(8,128)(2,1)S(1)}, bf16[32,4224]{1,0:T(8,128)(2,1)S(1)}, u32[]{:S(2)}, u32[]{:S(2)}) collective-permute-start(bf16[32,4224]{1,0:T(8,128)(2,1)S(1)} %collective-permute-done), channel_id=1, source_target_pairs={{0,2},{1,3},{4,0},{5,1},{8,4},{9,5},{12,8},{13,9},{14,12},{15,13},... | collective-permute-start | bytes 811016 | tf_op jit(solution)/shard_map/ppermute | solution.py:188
  20.9 19.9 %collective-permute-start.8 = (bf16[32,4224]{1,0:T(8,128)(2,1)S(1)}, bf16[32,4224]{1,0:T(8,128)(2,1)S(1)}, u32[]{:S(2)}, u32[]{:S(2)}) collective-permute-start(bf16[32,4224]{1,0:T(8,128)(2,1)S(1)} %collective-permute-done.1), channel_id=1, source_target_pairs={{0,4},{1,5},{4,8},{5,9},{8,12},{9,13},{12,14},{13,15},{14,10},{15,... | collective-permute-start | bytes 811016 | tf_op jit(solution)/shard_map/ppermute | solution.py:188
  22.2 13.3 %collective-permute-start.12 = (bf16[32,4224]{1,0:T(8,128)(2,1)S(1)}, bf16[32,4224]{1,0:T(8,128)(2,1)S(1)}, u32[]{:S(2)}, u32[]{:S(2)}) collective-permute-start(bf16[32,4224]{1,0:T(8,128)(2,1)S(1)} %collective-permute-done.2), channel_id=1, source_target_pairs={{0,4},{1,5},{4,8},{5,9},{8,12},{9,13},{12,14},{13,15},{14,10},{15,... | collective-permute-start | bytes 811016 | tf_op jit(solution)/shard_map/ppermute | solution.py:188
  23.8 11.8 %collective-permute-start.13 = (bf16[32,4224]{1,0:T(8,128)(2,1)S(1)}, bf16[32,4224]{1,0:T(8,128)(2,1)S(1)}, u32[]{:S(2)}, u32[]{:S(2)}) collective-permute-start(bf16[32,4224]{1,0:T(8,128)(2,1)S(1)} %collective-permute-done.3), channel_id=1, source_target_pairs={{0,2},{1,3},{4,0},{5,1},{8,4},{9,5},{12,8},{13,9},{14,12},{15,13},... | collective-permute-start | bytes 811016 | tf_op jit(solution)/shard_map/ppermute | solution.py:188
  24.3 12.7 %collective-permute-start.6 = (bf16[64,4224]{1,0:T(8,128)(2,1)S(1)}, bf16[64,4224]{1,0:T(8,128)(2,1)S(1)}, u32[]{:S(2)}, u32[]{:S(2)}) collective-permute-start(bf16[64,4224]{1,0:T(8,128)(2,1)S(1)} %constant_dynamic-update-slice_fusion.2.own_ref), channel_id=1, source_target_pairs={{0,1},{1,0},{2,3},{3,2},{4,5},{5,4},{6,7},{7,6},{8,9},{9,8},{10,11... | collective-permute-start | bytes 1622024 | tf_op jit(solution)/shard_map/ppermute | solution.py:188
  35.6 10.8 %collective-permute-start.15 = (bf16[32,4224]{1,0:T(8,128)(2,1)S(1)}, bf16[32,4224]{1,0:T(8,128)(2,1)S(1)}, u32[]{:S(2)}, u32[]{:S(2)}) collective-permute-start(bf16[32,4224]{1,0:T(8,128)(2,1)S(1)} %collective-permute-done.12), channel_id=1, source_target_pairs={{0,4},{1,5},{4,8},{5,9},{8,12},{9,13},{12,14},{13,15},{14,10},{15,... | collective-permute-start | bytes 811016 | tf_op jit(solution)/shard_map/ppermute | solution.py:188
  37.0 9.6 %collective-permute-start.16 = (bf16[32,4224]{1,0:T(8,128)(2,1)S(1)}, bf16[32,4224]{1,0:T(8,128)(2,1)S(1)}, u32[]{:S(2)}, u32[]{:S(2)}) collective-permute-start(bf16[32,4224]{1,0:T(8,128)(2,1)S(1)} %collective-permute-done.13), channel_id=1, source_target_pairs={{0,2},{1,3},{4,0},{5,1},{8,4},{9,5},{12,8},{13,9},{14,12},{15,13},... | collective-permute-start | bytes 811016 | tf_op jit(solution)/shard_map/ppermute | solution.py:188
  41.1 11.1 %collective-permute-start.24 = (bf16[32,4224]{1,0:T(8,128)(2,1)S(1)}, bf16[32,4224]{1,0:T(8,128)(2,1)S(1)}, u32[]{:S(2)}, u32[]{:S(2)}) collective-permute-start(bf16[32,4224]{1,0:T(8,128)(2,1)S(1)} %collective-permute-done.7), channel_id=1, source_target_pairs={{0,2},{1,3},{4,0},{5,1},{8,4},{9,5},{12,8},{13,9},{14,12},{15,13},... | collective-permute-start | bytes 811016 | tf_op jit(solution)/shard_map/ppermute | solution.py:188
  42.7 9.6 %collective-permute-start.25 = (bf16[32,4224]{1,0:T(8,128)(2,1)S(1)}, bf16[32,4224]{1,0:T(8,128)(2,1)S(1)}, u32[]{:S(2)}, u32[]{:S(2)}) collective-permute-start(bf16[32,4224]{1,0:T(8,128)(2,1)S(1)} %collective-permute-done.8), channel_id=1, source_target_pairs={{0,4},{1,5},{4,8},{5,9},{8,12},{9,13},{12,14},{13,15},{14,10},{15,... | collective-permute-start | bytes 811016 | tf_op jit(solution)/shard_map/ppermute | solution.py:188
  46.6 10.4 %collective-permute-start.18 = (bf16[32,4224]{1,0:T(8,128)(2,1)S(1)}, bf16[32,4224]{1,0:T(8,128)(2,1)S(1)}, u32[]{:S(2)}, u32[]{:S(2)}) collective-permute-start(bf16[32,4224]{1,0:T(8,128)(2,1)S(1)} %collective-permute-done.15), channel_id=1, source_target_pairs={{0,4},{1,5},{4,8},{5,9},{8,12},{9,13},{12,14},{13,15},{14,10},{15,... | collective-permute-start | bytes 811016 | tf_op jit(solution)/shard_map/ppermute | solution.py:188
  57.6 18.6 %collective-permute-start.26 = (bf16[64,4096]{1,0:T(8,128)(2,1)S(1)}, bf16[64,4096]{1,0:T(8,128)(2,1)S(1)}, u32[]{:S(2)}, u32[]{:S(2)}) collective-permute-start(bf16[64,4096]{1,0:T(8,128)(2,1)S(1)} %get-tuple-element.109), channel_id=1, source_target_pairs={{0,1},{1,0},{2,3},{3,2},{4,5},{5,4},{6,7},{7,6},{8,9},{9,8},{10,11... | collective-permute-start | bytes 1572872 | tf_op jit(solution)/shard_map/ppermute | solution.py:188
  68.1 13.7 %collective-permute-start.32 = (bf16[32,4096]{1,0:T(8,128)(2,1)S(1)}, bf16[32,4096]{1,0:T(8,128)(2,1)S(1)}, u32[]{:S(2)}, u32[]{:S(2)}) collective-permute-start(bf16[32,4096]{1,0:T(8,128)(2,1)S(1)} %get-tuple-element.151), channel_id=1, source_target_pairs={{0,4},{1,5},{4,8},{5,9},{8,12},{9,13},{12,14},{13,15},{14,10},{15,... | collective-permute-start | bytes 786440 | tf_op jit(solution)/shard_map/ppermute | solution.py:188
  69.7 12.1 %collective-permute-start.33 = (bf16[32,4096]{1,0:T(8,128)(2,1)S(1)}, bf16[32,4096]{1,0:T(8,128)(2,1)S(1)}, u32[]{:S(2)}, u32[]{:S(2)}) collective-permute-start(bf16[32,4096]{1,0:T(8,128)(2,1)S(1)} %get-tuple-element.150), channel_id=1, source_target_pairs={{0,2},{1,3},{4,0},{5,1},{8,4},{9,5},{12,8},{13,9},{14,12},{15,13},... | collective-permute-start | bytes 786440 | tf_op jit(solution)/shard_map/ppermute | solution.py:188
  75.1 18.0 %collective-permute-start.22 = (bf16[64,4096]{1,0:T(8,128)(2,1)S(1)}, bf16[64,4096]{1,0:T(8,128)(2,1)S(1)}, u32[]{:S(2)}, u32[]{:S(2)}) collective-permute-start(bf16[64,4096]{1,0:T(8,128)(2,1)S(1)} %get-tuple-element.99), channel_id=1, source_target_pairs={{0,1},{1,0},{2,3},{3,2},{4,5},{5,4},{6,7},{7,6},{8,9},{9,8},{10,11... | collective-permute-start | bytes 1572872 | tf_op jit(solution)/shard_map/ppermute | solution.py:188
  76.4 9.9 %collective-permute-start.34 = (bf16[32,4096]{1,0:T(8,128)(2,1)S(1)}, bf16[32,4096]{1,0:T(8,128)(2,1)S(1)}, u32[]{:S(2)}, u32[]{:S(2)}) collective-permute-start(bf16[32,4096]{1,0:T(8,128)(2,1)S(1)} %get-tuple-element.147), channel_id=1, source_target_pairs={{0,2},{1,3},{4,0},{5,1},{8,4},{9,5},{12,8},{13,9},{14,12},{15,13},... | collective-permute-start | bytes 786440 | tf_op jit(solution)/shard_map/ppermute | solution.py:188
  82.0 11.0 %collective-permute-start.36 = (bf16[32,4096]{1,0:T(8,128)(2,1)S(1)}, bf16[32,4096]{1,0:T(8,128)(2,1)S(1)}, u32[]{:S(2)}, u32[]{:S(2)}) collective-permute-start(bf16[32,4096]{1,0:T(8,128)(2,1)S(1)} %get-tuple-element.145), channel_id=1, source_target_pairs={{0,4},{1,5},{4,8},{5,9},{8,12},{9,13},{12,14},{13,15},{14,10},{15,... | collective-permute-start | bytes 786440 | tf_op jit(solution)/shard_map/ppermute | solution.py:188
  83.0 10.0 %collective-permute-start.37 = (bf16[32,4096]{1,0:T(8,128)(2,1)S(1)}, bf16[32,4096]{1,0:T(8,128)(2,1)S(1)}, u32[]{:S(2)}, u32[]{:S(2)}) collective-permute-start(bf16[32,4096]{1,0:T(8,128)(2,1)S(1)} %get-tuple-element.144), channel_id=1, source_target_pairs={{0,2},{1,3},{4,0},{5,1},{8,4},{9,5},{12,8},{13,9},{14,12},{15,13},... | collective-permute-start | bytes 786440 | tf_op jit(solution)/shard_map/ppermute | solution.py:188
  87.6 10.2 %collective-permute-start.38 = (bf16[32,4096]{1,0:T(8,128)(2,1)S(1)}, bf16[32,4096]{1,0:T(8,128)(2,1)S(1)}, u32[]{:S(2)}, u32[]{:S(2)}) collective-permute-start(bf16[32,4096]{1,0:T(8,128)(2,1)S(1)} %get-tuple-element.143), channel_id=1, source_target_pairs={{0,2},{1,3},{4,0},{5,1},{8,4},{9,5},{12,8},{13,9},{14,12},{15,13},... | collective-permute-start | bytes 786440 | tf_op jit(solution)/shard_map/ppermute | solution.py:188
  93.3 11.0 %collective-permute-start.41 = (bf16[32,4096]{1,0:T(8,128)(2,1)S(1)}, bf16[32,4096]{1,0:T(8,128)(2,1)S(1)}, u32[]{:S(2)}, u32[]{:S(2)}) collective-permute-start(bf16[32,4096]{1,0:T(8,128)(2,1)S(1)} %get-tuple-element.141), channel_id=1, source_target_pairs={{0,4},{1,5},{4,8},{5,9},{8,12},{9,13},{12,14},{13,15},{14,10},{15,... | collective-permute-start | bytes 786440 | tf_op jit(solution)/shard_map/ppermute | solution.py:188
  94.3 10.0 %collective-permute-start.42 = (bf16[32,4096]{1,0:T(8,128)(2,1)S(1)}, bf16[32,4096]{1,0:T(8,128)(2,1)S(1)}, u32[]{:S(2)}, u32[]{:S(2)}) collective-permute-start(bf16[32,4096]{1,0:T(8,128)(2,1)S(1)} %get-tuple-element.140), channel_id=1, source_target_pairs={{0,2},{1,3},{4,0},{5,1},{8,4},{9,5},{12,8},{13,9},{14,12},{15,13},... | collective-permute-start | bytes 786440 | tf_op jit(solution)/shard_map/ppermute | solution.py:188
  (27 other events, 157.5 us)

commit v3 on v2

v3 whole, which is shorter than its diff:
```python
import functools

import jax
import jax.numpy as jnp
from jax import lax
from jax.experimental import pallas as pl
from jax.experimental.pallas import tpu as pltpu
from jax.sharding import PartitionSpec as P

HEADS = 64
KVH = 4
HD = 128
CTX = 1024
LANES = 128
CHUNKS = 2
OPT = {'pair': 'ch', 'swap': 1, 'load_at': (0, 1), 'att_at': (0, 1), 'mine': 2, 'theirs': 3, 'end_mine': 1, 'end_theirs': 1, 'rs': 'B', 'last': 1, 'own_turn': 4, 'att_turn': 6}


def attend_body(request, lengths_ref, q_ref, kv, o_ref):
    length = lengths_ref[request]
    group_size = HEADS // KVH
    visible = lax.broadcasted_iota(jnp.int32, (group_size, CTX), 1) < length
    for g in range(KVH):
        q = q_ref[request, g * group_size : (g + 1) * group_size, :]
        keys = kv[0, :, g * HD : (g + 1) * HD]
        values = kv[1, :, g * HD : (g + 1) * HD]
        scores = lax.dot_general(
            q, keys, (((1,), (1,)), ((), ())), preferred_element_type=jnp.float32
        ) * HD ** (-0.5)
        scores = jnp.where(visible, scores, -jnp.inf)
        raised = jnp.exp(scores - jnp.max(scores, axis=-1, keepdims=True))
        weights = (raised / jnp.sum(raised, axis=-1, keepdims=True)).astype(jnp.bfloat16)
        mixed = jnp.dot(weights, values, preferred_element_type=jnp.float32)
        o_ref[0, g * group_size : (g + 1) * group_size, :] = mixed.astype(jnp.bfloat16)


def attend_kernel(request, lengths_ref, q_ref, kv_hbm, o_ref, kv, sem):
    copy = pltpu.make_async_copy(kv_hbm.at[request], kv, sem)
    copy.start()
    copy.wait()
    attend_body(request, lengths_ref, q_ref, kv, o_ref)


def attend_load_kernel(
    request, lengths_ref, q_ref, kv_hbm, weight_hbm, o_ref, weight_ref, kv, sem, weight_sem
):
    copy = pltpu.make_async_copy(kv_hbm.at[request], kv, sem)
    copy.start()
    load = pltpu.make_async_copy(weight_hbm, weight_ref, weight_sem)
    load.start()
    copy.wait()
    attend_body(request, lengths_ref, q_ref, kv, o_ref)
    load.wait()


def load_kernel(weight_hbm, weight_ref, sem):
    load = pltpu.make_async_copy(weight_hbm, weight_ref, sem)
    load.start()
    load.wait()


VMEM_WHOLE = pl.BlockSpec(memory_space=pltpu.VMEM)
ANYWHERE = pl.BlockSpec(memory_space=pl.ANY)


def in_hbm(x):
    return pltpu.with_memory_space_constraint(x, pltpu.HBM)


def load(weight):
    return pl.pallas_call(
        load_kernel,
        in_specs=[ANYWHERE],
        out_specs=VMEM_WHOLE,
        out_shape=pltpu.VMEM(weight.shape, weight.dtype),
        scratch_shapes=[pltpu.SemaphoreType.DMA],
        compiler_params=pltpu.CompilerParams(vmem_limit_bytes=1 << 20),
        cost_estimate=pl.CostEstimate(
            flops=0, bytes_accessed=2 * weight.size, transcendentals=0
        ),
        name="load",
    )(in_hbm(weight))


def attend(request, queries, kv_cache, lengths, *weight):
    kernel = attend_load_kernel if weight else attend_kernel
    return pl.pallas_call(
        functools.partial(kernel, request),
        in_specs=[pl.BlockSpec(memory_space=pltpu.SMEM), VMEM_WHOLE, ANYWHERE]
        + [ANYWHERE] * len(weight),
        out_specs=[VMEM_WHOLE] * (1 + len(weight)),
        out_shape=[jax.ShapeDtypeStruct((1, HEADS, HD), jnp.bfloat16)]
        + [pltpu.VMEM(w.shape, w.dtype) for w in weight],
        scratch_shapes=[pltpu.VMEM(kv_cache.shape[1:], kv_cache.dtype)]
        + [pltpu.SemaphoreType.DMA] * (1 + len(weight)),
        compiler_params=pltpu.CompilerParams(vmem_limit_bytes=6 << 20),
        cost_estimate=pl.CostEstimate(
            flops=4 * HEADS * CTX * HD,
            bytes_accessed=4 * CTX * KVH * HD + 2 * sum(w.size for w in weight),
            transcendentals=HEADS * CTX,
        ),
        name="attend",
    )(lengths, queries, in_hbm(kv_cache), *(in_hbm(w) for w in weight))


def expert_kernel(experts, own_ref, sib_ref, in_ref, down_ref, out_own, out_sib, x, hidden):
    rows = own_ref.shape[0]
    _, ff, width = down_ref.shape
    block = 256
    out_block = 1024
    x[:rows, :] = own_ref[:, :width]
    x[rows:, :] = sib_ref[:, :width]
    for n in range(0, ff, block):
        gate = jnp.dot(x[...], in_ref[0, :, n : n + block], preferred_element_type=jnp.float32)
        up = jnp.dot(
            x[...], in_ref[0, :, ff + n : ff + n + block], preferred_element_type=jnp.float32
        )
        hidden[:, n : n + block] = (jax.nn.silu(gate) * up).astype(jnp.bfloat16)
    lane = lax.broadcasted_iota(jnp.int32, (rows, LANES), 1)
    mine = (lax.rem(lane, experts) == lax.axis_index("expert")) & (lane < 3 * experts)
    own_coef, sib_coef = [
        jnp.sum(
            jnp.where(mine, ref[:, width:].astype(jnp.float32), 0.0), axis=1, keepdims=True
        )
        for ref in (own_ref, sib_ref)
    ]
    for n in range(0, width, out_block):
        part = jnp.dot(
            hidden[...], down_ref[0, :, n : n + out_block], preferred_element_type=jnp.float32
        )
        out_own[:, n : n + out_block] = (part[:rows] * own_coef).astype(jnp.bfloat16)
        out_sib[:, n : n + out_block] = (part[rows:] * sib_coef).astype(jnp.bfloat16)


def expert_apply(experts, own, sib, w_gate_up, w_down):
    rows, wide = own.shape
    _, ff, width = w_down.shape
    shape = jax.ShapeDtypeStruct((rows, width), jnp.bfloat16)
    whole = pl.BlockSpec(memory_space=pltpu.VMEM)
    return pl.pallas_call(
        functools.partial(expert_kernel, experts),
        in_specs=[whole] * 4,
        out_specs=[whole] * 2,
        out_shape=[shape, shape],
        scratch_shapes=[
            pltpu.VMEM((2 * rows, width), jnp.bfloat16),
            pltpu.VMEM((2 * rows, ff), jnp.bfloat16),
        ],
        compiler_params=pltpu.CompilerParams(vmem_limit_bytes=6 << 20),
        cost_estimate=pl.CostEstimate(
            flops=2 * 2 * rows * width * ff * 3,
            bytes_accessed=8 * rows * width,
            transcendentals=0,
        ),
        name="expert",
    )(
        own,
        sib,
        *(pltpu.with_memory_space_constraint(x, pltpu.VMEM) for x in (w_gate_up, w_down)),
    )


def prologue_kernel(experts, x_hbm, ids_hbm, weights_hbm, *refs):
    chunk_refs = refs[:CHUNKS]
    ids_ref, weights_ref, sems = refs[CHUNKS:]
    tokens, width = x_hbm.shape
    top = ids_hbm.shape[0]
    rows = tokens // CHUNKS
    small = [
        pltpu.make_async_copy(ids_hbm, ids_ref, sems.at[0]),
        pltpu.make_async_copy(weights_hbm, weights_ref, sems.at[1]),
    ]
    large = [
        pltpu.make_async_copy(
            x_hbm.at[pl.ds(k * rows, rows)], ref.at[:, pl.ds(0, width)], sems.at[2 + k]
        )
        for k, ref in enumerate(chunk_refs)
    ]
    for copy in small + large:
        copy.start()
    for copy in small:
        copy.wait()
    ids = ids_ref[...].T
    raw = weights_ref[...].T
    lane = lax.broadcasted_iota(jnp.int32, (tokens, LANES), 1)
    named = lax.rem(lane, experts)
    share = raw / jnp.sum(raw, axis=1, keepdims=True)
    coef = jnp.zeros((tokens, LANES), jnp.float32)
    for k in range(top):
        coef = coef + jnp.where(ids[:, k : k + 1] == named, share[:, k : k + 1], 0.0)
    high = coef.astype(jnp.bfloat16).astype(jnp.float32)
    middle = (coef - high).astype(jnp.bfloat16).astype(jnp.float32)
    low = coef - high - middle
    parts = jnp.where(lane < experts, high, jnp.where(lane < 2 * experts, middle, low))
    parts = jnp.where(lane < 3 * experts, parts, 0.0).astype(jnp.bfloat16)
    for k, ref in enumerate(chunk_refs):
        ref[:, width:] = parts[k * rows : (k + 1) * rows, :]
    for copy in large:
        copy.wait()


def prologue(moe_input, route_ids, route_weights, experts):
    tokens, width = moe_input.shape
    top = route_ids.shape[1]
    return pl.pallas_call(
        functools.partial(prologue_kernel, experts),
        in_specs=[ANYWHERE] * 3,
        out_specs=[VMEM_WHOLE] * CHUNKS,
        out_shape=[
            jax.ShapeDtypeStruct((tokens // CHUNKS, width + LANES), jnp.bfloat16)
        ] * CHUNKS,
        scratch_shapes=[
            pltpu.VMEM((top, tokens), jnp.int32),
            pltpu.VMEM((top, tokens), jnp.float32),
            pltpu.SemaphoreType.DMA((2 + CHUNKS,)),
        ],
        compiler_params=pltpu.CompilerParams(vmem_limit_bytes=4 << 20),
        name="prologue",
    )(in_hbm(moe_input), in_hbm(route_ids.T), in_hbm(route_weights.T))


def shards(order, queries, kv_cache, lengths, moe_input, route_ids, route_weights, w_gate_up, w_down):
    experts = lax.axis_size("expert")
    chips = len(order)
    half = chips // 2
    rows = moe_input.shape[0] // CHUNKS

    def ring(step):
        return [
            (2 * order[i] + c, 2 * order[(i + step) % chips] + c)
            for i in range(chips)
            for c in range(2)
        ]

    forward, backward = ring(1), ring(-1)
    swap = [(i, i ^ 1) for i in range(experts)]

    def send(x, pairs):
        return lax.ppermute(x, "expert", pairs)

    first = prologue(moe_input, route_ids, route_weights, experts)
    requests = queries.shape[0]
    heads = queries.reshape(requests, HEADS, HD)
    gate_up = load(w_gate_up)
    begun, down = attend(0, heads, kv_cache, lengths, w_down)

    long_pair = (("f", 0), ("b", 1))
    short_pair = (("b", 0), ("f", 1))
    outward = {"f": forward, "b": backward}
    homeward = {"f": backward, "b": forward}

    def tie(anchor, group, values):
        anchor, got = lax.optimization_barrier((anchor, [values[key] for key in group]))
        values.update(zip(group, got))
        return anchor

    def compute(keys, own):
        slots = {key: i * rows for i, key in enumerate(keys)}
        own = jnp.concatenate(own, axis=0)
        mine, theirs = expert_apply(experts, own, send(own, swap), gate_up, down)
        return [slots, mine, send(theirs, swap)]

    def tie_partial(block, index, group, values):
        if group:
            block[index] = tie(block[index], group, values)

    longs = long_pair
    if OPT["pair"] == "ls":
        groups = (long_pair, short_pair)
    else:
        groups = ((("f", 0), ("b", 0)), (("f", 1), ("b", 1)))
    if OPT["swap"]:
        groups = groups[::-1]
    moving = {key: first[key[1]] for key in long_pair + short_pair}
    partial = {}
    done = []
    for s in range(1, half + 1):
        for turn, group in enumerate(groups):
            if s == 2 and turn in OPT["load_at"]:
                gate_up = tie(gate_up, group, moving)
            if s == 2 and turn in OPT["att_at"]:
                begun = tie(begun, group, moving)
            if s > 2 and OPT["mine"] and len(done) >= OPT["mine"]:
                tie_partial(done[-OPT["mine"]], 1, group, moving)
            if OPT["theirs"] and len(done) >= OPT["theirs"]:
                tie_partial(done[-OPT["theirs"]], 2, group, moving)
            own = {key: moving[key] for key in group}
            for key in group:
                if s < half or key in longs:
                    moving[key] = send(moving[key], outward[key[0]])
            if s > 1:
                done.append(compute(list(own), list(own.values())))
                for key in own:
                    partial[s - 1, key] = done[-1]
    own = {key: moving[key] for key in longs}
    if OPT["end_mine"]:
        tie_partial(done[-OPT["end_mine"]], 1, longs, own)
    if OPT["end_theirs"]:
        tie_partial(done[-OPT["end_theirs"]], 2, longs, own)
    done.append(compute(list(own), list(own.values())))
    for key in own:
        partial[half, key] = done[-1]
    done[-1][1], first = lax.optimization_barrier((done[-1][1], first))
    own_rows = compute(list(range(CHUNKS)), first)

    def local(block, key):
        slots, mine, theirs = block
        span = slice(slots[key], slots[key] + rows)
        return mine[span].astype(jnp.float32) + theirs[span].astype(jnp.float32)

    if OPT["rs"] == "A":
        order = [(half, long_pair)]
        for s in range(half - 1, 0, -1):
            order += [(s, short_pair), (s, long_pair)]
    else:
        order = [(half - 1, short_pair), (half, long_pair)]
        for s in range(half - 2, 0, -1):
            order += [(s, short_pair), (s + 1, long_pair)]
        order.append((1, long_pair))
    rest = list(range(1, requests))
    attended = [begun]
    moving = {}
    last = None
    for turn, (s, group) in enumerate(order):
        if OPT["last"] and last is not None and group[0] in moving:
            last = tie(last, group, moving)
        if turn == OPT["own_turn"]:
            tie_partial(own_rows, 1, group, moving)
            own_rows[1], heads = lax.optimization_barrier((own_rows[1], heads))
        if turn >= OPT["att_turn"] and rest:
            attended += attend(rest.pop(0), heads, kv_cache, lengths)
            attended[-1] = tie(attended[-1], group, moving)
        if turn == len(order) - 2:
            tie_partial(own_rows, 2, group, moving)
        totals = []
        for key in group:
            total = local(partial[s, key], key)
            if key in moving:
                total = total + moving[key].astype(jnp.float32)
            totals.append(total.astype(jnp.bfloat16))
        last = totals
        for key, total in zip(group, last):
            moving[key] = send(total, homeward[key[0]])
    attended += [attend(r, heads, kv_cache, lengths)[0] for r in rest]
    attended = jnp.concatenate(attended, axis=0).reshape(requests, HEADS * HD)
    out = []
    for k in range(CHUNKS):
        total = local(own_rows, k)
        for way in ("f", "b"):
            total = total + moving[way, k].astype(jnp.float32)
        out.append(total.astype(jnp.bfloat16))
    return attended, jnp.concatenate(out, axis=0)


def solution(mesh):
    chips = mesh.shape["expert"] // 2
    if mesh.shape["groups"] == 2:
        order = list(range(0, chips, 2)) + list(range(chips - 1, 0, -2))
    else:
        order = list(range(chips))
    placed = (
        P(("groups", "expert"), None),
        P(("groups", "expert"), None, None, None),
        P(("groups", "expert")),
        P(("groups", "expert"), None),
        P(("groups", "expert"), None),
        P(("groups", "expert"), None),
        P("expert", None, None),
        P("expert", None, None),
    )
    return jax.shard_map(
        functools.partial(shards, order),
        mesh=mesh,
        in_specs=placed,
        out_specs=(P(("groups", "expert"), None), P(("groups", "expert"), None)),
        check_vma=False,
    )
```

time: 110 us -> 107 us (0.973)
  local copies, waits for them, and re-layouts: 9.8 us -> 1.78 us
  Pallas kernels: 27.5 us -> 35.3 us
  waiting for transfers between devices: 33.9 us -> 32.4 us
  starting transfers between devices: 35.6 us -> 34.4 us
    unnamed x24 -> x12, local copies, waits for them, and re-layouts: 9.59 us -> 1.57 us
    pallas_call x2 -> x4, Pallas kernels: 5.97 us -> 13.6 us  [the longest x2 7.77 us: attend(): pl.pallas_call(functools.partial(kernel, request), in_specs=[pl.BlockSpec...]
    ppermute x44, waiting for transfers between devices: 33.9 us -> 32.4 us  [send(): return lax.ppermute(x, 'expert', pairs)]
    ppermute x44, starting transfers between devices: 35.6 us -> 34.4 us  [send(): return lax.ppermute(x, 'expert', pairs)]
  transfers between devices with their start and end apart: 44 -> 44, of which waited for: 16 -> 21; matrix products, arithmetic and copies ran while one was open for 3% -> 3% of each run, Pallas kernels for 25% -> 32%
where the time goes in v3:
time: 107 us
  Pallas kernels  35.3 us (33%)
  starting transfers between devices  34.4 us (32%)
  waiting for transfers between devices  32.4 us (30%)
  other arithmetic  2.33 us (2%)
  local copies, waits for them, and re-layouts  1.78 us (2%)
    ppermute x44, starting transfers between devices, send(): return lax.ppermute(x, 'expert', pairs)  34.4 us
    ppermute x44, waiting for transfers between devices, send(): return lax.ppermute(x, 'expert', pairs)  32.4 us
    pallas_call x8, Pallas kernels, expert_apply(): pl.pallas_call(functools.partial(expert_kernel, experts), in_specs=[whole...  21.7 us
    pallas_call x2, Pallas kernels, attend(): pl.pallas_call(functools.partial(kernel, request), in_specs=[pl.BlockSpec...  7.77 us
    pallas_call x1, Pallas kernels, load(): pl.pallas_call(load_kernel, in_specs=[ANYWHERE], out_specs=VMEM_WHOLE, ou...  4.6 us
  transfers between devices with their start and end apart: 44, of which 21 were waited for; matrix products, arithmetic and copies ran while one was open for 3% of the time, Pallas kernels for 32%

profile of v3, /device:TPU:0, one launch (start us, length us, event | category | flops | bytes accessed | tf_op | source)
XLA Modules:
  0.0 107.2 jit_solution(1875686179050096575)
XLA Ops:
  1.9 3.1 %collective-permute-start = (bf16[32,4224]{1,0:T(8,128)(2,1)S(1)}, bf16[32,4224]{1,0:T(8,128)(2,1)S(1)}, u32[]{:S(2)}, u32[]{:S(2)}) collective-permute-start(bf16[32,4224]{1,0:T(8,128)(2,1)S(1)} %get-tuple-element.129), channel_id=1, source_target_pairs={{0,4},{1,5},{4,8},{5,9},{8,12},{9,13},{12,14},{13,15},{14,10},{15,... | collective-permute-start | bytes 811016 | tf_op jit(solution)/shard_map/ppermute | solution.py:239
  5.0 2.0 %collective-permute-start.2 = (bf16[32,4224]{1,0:T(8,128)(2,1)S(1)}, bf16[32,4224]{1,0:T(8,128)(2,1)S(1)}, u32[]{:S(2)}, u32[]{:S(2)}) collective-permute-start(bf16[32,4224]{1,0:T(8,128)(2,1)S(1)} %get-tuple-element.128), channel_id=1, source_target_pairs={{0,4},{1,5},{4,8},{5,9},{8,12},{9,13},{12,14},{13,15},{14,10},{15,... | collective-permute-start | bytes 811016 | tf_op jit(solution)/shard_map/ppermute | solution.py:239
  7.8 4.6 %load.1.in_ref = bf16[1,4096,1536]{2,1,0:T(8,128)(2,1)S(1)} custom-call(bf16[1,4096,1536]{2,1,0:T(8,128)(2,1)} %weight_hbm.3), custom_call_target="tpu_custom_call" | custom-call | bytes 12582912 | tf_op jit(solution)/shard_map/load/pallas_call | solution.py:71
  12.4 4.0 %attend.2 = (bf16[1,64,128]{2,1,0:T(8,128)(2,1)S(1)}, bf16[1,768,4096]{2,1,0:T(8,128)(2,1)S(1)}) custom-call(s32[2]{0:T(128)S(1)} %copy-done, bf16[2,64,128]{2,1,0:T(8,128)(2,1)S(1)} %bitcast.11, bf16[2,2,1024,512]{3,2,1,0:T(8,128)(2,1)} %kv_hbm.3, bf16[1,768,4096]{2,1,0:T(8,128)(2,1)} %weight_hbm.2), custom_call_target="tpu_custom_call" | custom-call | flops 33554432 | bytes 8388608 | tf_op jit(solution)/shard_map/attend/pallas_call | solution.py:87
  16.5 2.1 %collective-permute-start.5 = (bf16[32,4224]{1,0:T(8,128)(2,1)S(1)}, bf16[32,4224]{1,0:T(8,128)(2,1)S(1)}, u32[]{:S(2)}, u32[]{:S(2)}) collective-permute-start(bf16[32,4224]{1,0:T(8,128)(2,1)S(1)} %collective-permute-done), channel_id=1, source_target_pairs={{0,4},{1,5},{4,8},{5,9},{8,12},{9,13},{12,14},{13,15},{14,10},{15,... | collective-permute-start | bytes 811016 | tf_op jit(solution)/shard_map/ppermute | solution.py:239
  23.0 2.7 %expert.8 = (bf16[64,4096]{1,0:T(8,128)(2,1)S(1)}, bf16[64,4096]{1,0:T(8,128)(2,1)S(1)}) custom-call(bf16[64,4224]{1,0:T(8,128)(2,1)S(1)} %constant_dynamic-update-slice_fusion.own_ref, bf16[64,4224]{1,0:T(8,128)(2,1)S(1)} %collective-permute-done.4.sib_ref, bf16[1,4096,1536]{2,1,0:T(8,128)(2,1)S(1)} %load.1.in_ref, ...), custom_call_target="tpu_custom_call" | custom-call | flops 2415919104 | bytes 2097152 | tf_op jit(solution)/shard_map/expert/pallas_call | solution.py:140
  25.9 3.9 %collective-permute-done.6 = bf16[32,4224]{1,0:T(8,128)(2,1)S(1)} collective-permute-done((bf16[32,4224]{1,0:T(8,128)(2,1)S(1)}, bf16[32,4224]{1,0:T(8,128)(2,1)S(1)}, u32[]{:S(2)}, u32[]{:S(2)}) %collective-permute-start.6) | collective-permute-done | bytes 270368 | tf_op jit(solution)/shard_map/ppermute | solution.py:239
  32.0 2.7 %expert.10 = (bf16[64,4096]{1,0:T(8,128)(2,1)S(1)}, bf16[64,4096]{1,0:T(8,128)(2,1)S(1)}) custom-call(bf16[64,4224]{1,0:T(8,128)(2,1)S(1)} %constant_dynamic-update-slice_fusion.4.own_ref, bf16[64,4224]{1,0:T(8,128)(2,1)S(1)} %collective-permute-done.10.sib_ref, bf16[1,4096,1536]{2,1,0:T(8,128)(2,1)S(1)} %load.1.in_ref, ...), custom_call_target="tpu_custom_call" | custom-call | flops 2415919104 | bytes 2097152 | tf_op jit(solution)/shard_map/expert/pallas_call | solution.py:140
  37.7 2.7 %expert.9 = (bf16[64,4096]{1,0:T(8,128)(2,1)S(1)}, bf16[64,4096]{1,0:T(8,128)(2,1)S(1)}) custom-call(bf16[64,4224]{1,0:T(8,128)(2,1)S(1)} %constant_dynamic-update-slice_fusion.2.own_ref, bf16[64,4224]{1,0:T(8,128)(2,1)S(1)} %collective-permute-done.7.sib_ref, bf16[1,4096,1536]{2,1,0:T(8,128)(2,1)S(1)} %load.1.in_ref, ...), custom_call_target="tpu_custom_call" | custom-call | flops 2415919104 | bytes 2097152 | tf_op jit(solution)/shard_map/expert/pallas_call | solution.py:140
  42.4 2.7 %expert.11 = (bf16[64,4096]{1,0:T(8,128)(2,1)S(1)}, bf16[64,4096]{1,0:T(8,128)(2,1)S(1)}) custom-call(bf16[64,4224]{1,0:T(8,128)(2,1)S(1)} %constant_dynamic-update-slice_fusion.6.own_ref, bf16[64,4224]{1,0:T(8,128)(2,1)S(1)} %collective-permute-done.13.sib_ref, bf16[1,4096,1536]{2,1,0:T(8,128)(2,1)S(1)} %load.1.in_ref, ...), custom_call_target="tpu_custom_call" | custom-call | flops 2415919104 | bytes 2097152 | tf_op jit(solution)/shard_map/expert/pallas_call | solution.py:140
  46.4 2.7 %expert.15 = (bf16[64,4096]{1,0:T(8,128)(2,1)S(1)}, bf16[64,4096]{1,0:T(8,128)(2,1)S(1)}) custom-call(bf16[64,4224]{1,0:T(8,128)(2,1)S(1)} %constant_dynamic-update-slice_fusion.14.own_ref, bf16[64,4224]{1,0:T(8,128)(2,1)S(1)} %collective-permute-done.28.sib_ref, bf16[1,4096,1536]{2,1,0:T(8,128)(2,1)S(1)} %load.1.in_ref, ...), custom_call_target="tpu_custom_call" | custom-call | flops 2415919104 | bytes 2097152 | tf_op jit(solution)/shard_map/expert/pallas_call | solution.py:140
  51.7 2.7 %expert.12 = (bf16[64,4096]{1,0:T(8,128)(2,1)S(1)}, bf16[64,4096]{1,0:T(8,128)(2,1)S(1)}) custom-call(bf16[64,4224]{1,0:T(8,128)(2,1)S(1)} %constant_dynamic-update-slice_fusion.8.own_ref, bf16[64,4224]{1,0:T(8,128)(2,1)S(1)} %collective-permute-done.16.sib_ref, bf16[1,4096,1536]{2,1,0:T(8,128)(2,1)S(1)} %load.1.in_ref, ...), custom_call_target="tpu_custom_call" | custom-call | flops 2415919104 | bytes 2097152 | tf_op jit(solution)/shard_map/expert/pallas_call | solution.py:140
  55.0 3.1 %collective-permute-done.22 = bf16[32,4224]{1,0:T(8,128)(2,1)S(1)} collective-permute-done((bf16[32,4224]{1,0:T(8,128)(2,1)S(1)}, bf16[32,4224]{1,0:T(8,128)(2,1)S(1)}, u32[]{:S(2)}, u32[]{:S(2)}) %collective-permute-start.22) | collective-permute-done | bytes 270368 | tf_op jit(solution)/shard_map/ppermute | solution.py:239
  59.0 1.8 %collective-permute-start.27 = (bf16[32,4096]{1,0:T(8,128)(2,1)S(1)}, bf16[32,4096]{1,0:T(8,128)(2,1)S(1)}, u32[]{:S(2)}, u32[]{:S(2)}) collective-permute-start(bf16[32,4096]{1,0:T(8,128)(2,1)S(1)} %add_convert_fusion.13), channel_id=1, source_target_pairs={{0,4},{1,5},{4,8},{5,9},{8,12},{9,13},{12,14},{13,15},{14,10},{15,... | collective-permute-start | bytes 786440 | tf_op jit(solution)/shard_map/ppermute | solution.py:239
  60.9 2.7 %expert.13 = (bf16[64,4096]{1,0:T(8,128)(2,1)S(1)}, bf16[64,4096]{1,0:T(8,128)(2,1)S(1)}) custom-call(bf16[64,4224]{1,0:T(8,128)(2,1)S(1)} %constant_dynamic-update-slice_fusion.10.own_ref, bf16[64,4224]{1,0:T(8,128)(2,1)S(1)} %collective-permute-done.23.sib_ref, bf16[1,4096,1536]{2,1,0:T(8,128)(2,1)S(1)} %load.1.in_ref, ...), custom_call_target="tpu_custom_call" | custom-call | flops 2415919104 | bytes 2097152 | tf_op jit(solution)/shard_map/expert/pallas_call | solution.py:140
  70.4 2.7 %expert.14 = (bf16[64,4096]{1,0:T(8,128)(2,1)S(1)}, bf16[64,4096]{1,0:T(8,128)(2,1)S(1)}) custom-call(bf16[64,4224]{1,0:T(8,128)(2,1)S(1)} %constant_dynamic-update-slice_fusion.12.own_ref, bf16[64,4224]{1,0:T(8,128)(2,1)S(1)} %collective-permute-done.24.sib_ref, bf16[1,4096,1536]{2,1,0:T(8,128)(2,1)S(1)} %load.1.in_ref, ...), custom_call_target="tpu_custom_call" | custom-call | flops 2415919104 | bytes 2097152 | tf_op jit(solution)/shard_map/expert/pallas_call | solution.py:140
  73.1 1.8 %collective-permute-done.31 = bf16[32,4096]{1,0:T(8,128)(2,1)S(1)} collective-permute-done((bf16[32,4096]{1,0:T(8,128)(2,1)S(1)}, bf16[32,4096]{1,0:T(8,128)(2,1)S(1)}, u32[]{:S(2)}, u32[]{:S(2)}) %collective-permute-start.31) | collective-permute-done | bytes 262176 | tf_op jit(solution)/shard_map/ppermute | solution.py:239
  75.8 1.9 %collective-permute-start.36 = (bf16[32,4096]{1,0:T(8,128)(2,1)S(1)}, bf16[32,4096]{1,0:T(8,128)(2,1)S(1)}, u32[]{:S(2)}, u32[]{:S(2)}) collective-permute-start(bf16[32,4096]{1,0:T(8,128)(2,1)S(1)} %add_convert_fusion.9), channel_id=1, source_target_pairs={{0,2},{1,3},{4,0},{5,1},{8,4},{9,5},{12,8},{13,9},{14,12},{15,13},... | collective-permute-start | bytes 786440 | tf_op jit(solution)/shard_map/ppermute | solution.py:239
  78.1 3.3 %collective-permute-done.33 = bf16[32,4096]{1,0:T(8,128)(2,1)S(1)} collective-permute-done((bf16[32,4096]{1,0:T(8,128)(2,1)S(1)}, bf16[32,4096]{1,0:T(8,128)(2,1)S(1)}, u32[]{:S(2)}, u32[]{:S(2)}) %collective-permute-start.33) | collective-permute-done | bytes 262176 | tf_op jit(solution)/shard_map/ppermute | solution.py:239
  81.6 3.9 %collective-permute-done.36 = bf16[32,4096]{1,0:T(8,128)(2,1)S(1)} collective-permute-done((bf16[32,4096]{1,0:T(8,128)(2,1)S(1)}, bf16[32,4096]{1,0:T(8,128)(2,1)S(1)}, u32[]{:S(2)}, u32[]{:S(2)}) %collective-permute-start.36) | collective-permute-done | bytes 262176 | tf_op jit(solution)/shard_map/ppermute | solution.py:239
  86.1 1.8 %collective-permute-start.38 = (bf16[32,4096]{1,0:T(8,128)(2,1)S(1)}, bf16[32,4096]{1,0:T(8,128)(2,1)S(1)}, u32[]{:S(2)}, u32[]{:S(2)}) collective-permute-start(bf16[32,4096]{1,0:T(8,128)(2,1)S(1)} %add_convert_fusion.5), channel_id=1, source_target_pairs={{0,2},{1,3},{4,0},{5,1},{8,4},{9,5},{12,8},{13,9},{14,12},{15,13},... | collective-permute-start | bytes 786440 | tf_op jit(solution)/shard_map/ppermute | solution.py:239
  90.3 3.8 %attend.3 = bf16[1,64,128]{2,1,0:T(8,128)(2,1)S(1)} custom-call(s32[2]{0:T(128)S(1)} %copy-done, bf16[2,64,128]{2,1,0:T(8,128)(2,1)S(1)} %bitcast.12, bf16[2,2,1024,512]{3,2,1,0:T(8,128)(2,1)} %kv_hbm.3), custom_call_target="tpu_custom_call" | custom-call | flops 33554432 | bytes 2097152 | tf_op jit(solution)/shard_map/attend/pallas_call | solution.py:87
  97.3 1.8 %collective-permute-start.40 = (bf16[32,4096]{1,0:T(8,128)(2,1)S(1)}, bf16[32,4096]{1,0:T(8,128)(2,1)S(1)}, u32[]{:S(2)}, u32[]{:S(2)}) collective-permute-start(bf16[32,4096]{1,0:T(8,128)(2,1)S(1)} %add_convert_fusion.3), channel_id=1, source_target_pairs={{0,2},{1,3},{4,0},{5,1},{8,4},{9,5},{12,8},{13,9},{14,12},{15,13},... | collective-permute-start | bytes 786440 | tf_op jit(solution)/shard_map/ppermute | solution.py:239
  100.2 2.6 %collective-permute-done.41 = bf16[32,4096]{1,0:T(8,128)(2,1)S(1)} collective-permute-done((bf16[32,4096]{1,0:T(8,128)(2,1)S(1)}, bf16[32,4096]{1,0:T(8,128)(2,1)S(1)}, u32[]{:S(2)}, u32[]{:S(2)}) %collective-permute-start.41) | collective-permute-done | bytes 262176 | tf_op jit(solution)/shard_map/ppermute | solution.py:239
  (112 shorter events, 39.0 us)
Async XLA Ops:
  1.9 14.5 %collective-permute-start = (bf16[32,4224]{1,0:T(8,128)(2,1)S(1)}, bf16[32,4224]{1,0:T(8,128)(2,1)S(1)}, u32[]{:S(2)}, u32[]{:S(2)}) collective-permute-start(bf16[32,4224]{1,0:T(8,128)(2,1)S(1)} %get-tuple-element.129), channel_id=1, source_target_pairs={{0,4},{1,5},{4,8},{5,9},{8,12},{9,13},{12,14},{13,15},{14,10},{15,... | collective-permute-start | bytes 811016 | tf_op jit(solution)/shard_map/ppermute | solution.py:239
  5.0 11.4 %collective-permute-start.1 = (bf16[32,4224]{1,0:T(8,128)(2,1)S(1)}, bf16[32,4224]{1,0:T(8,128)(2,1)S(1)}, u32[]{:S(2)}, u32[]{:S(2)}) collective-permute-start(bf16[32,4224]{1,0:T(8,128)(2,1)S(1)} %get-tuple-element.129), channel_id=1, source_target_pairs={{0,2},{1,3},{4,0},{5,1},{8,4},{9,5},{12,8},{13,9},{14,12},{15,13},... | collective-permute-start | bytes 811016 | tf_op jit(solution)/shard_map/ppermute | solution.py:239
  5.0 13.5 %collective-permute-start.2 = (bf16[32,4224]{1,0:T(8,128)(2,1)S(1)}, bf16[32,4224]{1,0:T(8,128)(2,1)S(1)}, u32[]{:S(2)}, u32[]{:S(2)}) collective-permute-start(bf16[32,4224]{1,0:T(8,128)(2,1)S(1)} %get-tuple-element.128), channel_id=1, source_target_pairs={{0,4},{1,5},{4,8},{5,9},{8,12},{9,13},{12,14},{13,15},{14,10},{15,... | collective-permute-start | bytes 811016 | tf_op jit(solution)/shard_map/ppermute | solution.py:239
  7.0 11.7 %collective-permute-start.3 = (bf16[32,4224]{1,0:T(8,128)(2,1)S(1)}, bf16[32,4224]{1,0:T(8,128)(2,1)S(1)}, u32[]{:S(2)}, u32[]{:S(2)}) collective-permute-start(bf16[32,4224]{1,0:T(8,128)(2,1)S(1)} %get-tuple-element.128), channel_id=1, source_target_pairs={{0,2},{1,3},{4,0},{5,1},{8,4},{9,5},{12,8},{13,9},{14,12},{15,13},... | collective-permute-start | bytes 811016 | tf_op jit(solution)/shard_map/ppermute | solution.py:239
  16.5 9.5 %collective-permute-start.5 = (bf16[32,4224]{1,0:T(8,128)(2,1)S(1)}, bf16[32,4224]{1,0:T(8,128)(2,1)S(1)}, u32[]{:S(2)}, u32[]{:S(2)}) collective-permute-start(bf16[32,4224]{1,0:T(8,128)(2,1)S(1)} %collective-permute-done), channel_id=1, source_target_pairs={{0,4},{1,5},{4,8},{5,9},{8,12},{9,13},{12,14},{13,15},{14,10},{15,... | collective-permute-start | bytes 811016 | tf_op jit(solution)/shard_map/ppermute | solution.py:239
  18.8 16.0 %collective-permute-start.11 = (bf16[32,4224]{1,0:T(8,128)(2,1)S(1)}, bf16[32,4224]{1,0:T(8,128)(2,1)S(1)}, u32[]{:S(2)}, u32[]{:S(2)}) collective-permute-start(bf16[32,4224]{1,0:T(8,128)(2,1)S(1)} %collective-permute-done.2), channel_id=1, source_target_pairs={{0,4},{1,5},{4,8},{5,9},{8,12},{9,13},{12,14},{13,15},{14,10},{15,... | collective-permute-start | bytes 811016 | tf_op jit(solution)/shard_map/ppermute | solution.py:239
  20.4 9.4 %collective-permute-start.6 = (bf16[32,4224]{1,0:T(8,128)(2,1)S(1)}, bf16[32,4224]{1,0:T(8,128)(2,1)S(1)}, u32[]{:S(2)}, u32[]{:S(2)}) collective-permute-start(bf16[32,4224]{1,0:T(8,128)(2,1)S(1)} %collective-permute-done.1), channel_id=1, source_target_pairs={{0,2},{1,3},{4,0},{5,1},{8,4},{9,5},{12,8},{13,9},{14,12},{15,13},... | collective-permute-start | bytes 811016 | tf_op jit(solution)/shard_map/ppermute | solution.py:239
  20.9 14.1 %collective-permute-start.12 = (bf16[32,4224]{1,0:T(8,128)(2,1)S(1)}, bf16[32,4224]{1,0:T(8,128)(2,1)S(1)}, u32[]{:S(2)}, u32[]{:S(2)}) collective-permute-start(bf16[32,4224]{1,0:T(8,128)(2,1)S(1)} %collective-permute-done.3), channel_id=1, source_target_pairs={{0,2},{1,3},{4,0},{5,1},{8,4},{9,5},{12,8},{13,9},{14,12},{15,13},... | collective-permute-start | bytes 811016 | tf_op jit(solution)/shard_map/ppermute | solution.py:239
  29.8 10.6 %collective-permute-start.20 = (bf16[32,4224]{1,0:T(8,128)(2,1)S(1)}, bf16[32,4224]{1,0:T(8,128)(2,1)S(1)}, u32[]{:S(2)}, u32[]{:S(2)}) collective-permute-start(bf16[32,4224]{1,0:T(8,128)(2,1)S(1)} %collective-permute-done.5), channel_id=1, source_target_pairs={{0,4},{1,5},{4,8},{5,9},{8,12},{9,13},{12,14},{13,15},{14,10},{15,... | collective-permute-start | bytes 811016 | tf_op jit(solution)/shard_map/ppermute | solution.py:239
  31.5 9.3 %collective-permute-start.21 = (bf16[32,4224]{1,0:T(8,128)(2,1)S(1)}, bf16[32,4224]{1,0:T(8,128)(2,1)S(1)}, u32[]{:S(2)}, u32[]{:S(2)}) collective-permute-start(bf16[32,4224]{1,0:T(8,128)(2,1)S(1)} %collective-permute-done.6), channel_id=1, source_target_pairs={{0,2},{1,3},{4,0},{5,1},{8,4},{9,5},{12,8},{13,9},{14,12},{15,13},... | collective-permute-start | bytes 811016 | tf_op jit(solution)/shard_map/ppermute | solution.py:239
  35.3 9.8 %collective-permute-start.14 = (bf16[32,4224]{1,0:T(8,128)(2,1)S(1)}, bf16[32,4224]{1,0:T(8,128)(2,1)S(1)}, u32[]{:S(2)}, u32[]{:S(2)}) collective-permute-start(bf16[32,4224]{1,0:T(8,128)(2,1)S(1)} %collective-permute-done.11), channel_id=1, source_target_pairs={{0,4},{1,5},{4,8},{5,9},{8,12},{9,13},{12,14},{13,15},{14,10},{15,... | collective-permute-start | bytes 811016 | tf_op jit(solution)/shard_map/ppermute | solution.py:239
  37.0 9.2 %collective-permute-start.15 = (bf16[32,4224]{1,0:T(8,128)(2,1)S(1)}, bf16[32,4224]{1,0:T(8,128)(2,1)S(1)}, u32[]{:S(2)}, u32[]{:S(2)}) collective-permute-start(bf16[32,4224]{1,0:T(8,128)(2,1)S(1)} %collective-permute-done.12), channel_id=1, source_target_pairs={{0,2},{1,3},{4,0},{5,1},{8,4},{9,5},{12,8},{13,9},{14,12},{15,13},... | collective-permute-start | bytes 811016 | tf_op jit(solution)/shard_map/ppermute | solution.py:239
  49.1 9.2 %collective-permute-start.29 = (bf16[64,4096]{1,0:T(8,128)(2,1)S(1)}, bf16[64,4096]{1,0:T(8,128)(2,1)S(1)}, u32[]{:S(2)}, u32[]{:S(2)}) collective-permute-start(bf16[64,4096]{1,0:T(8,128)(2,1)S(1)} %get-tuple-element.139), channel_id=1, source_target_pairs={{0,1},{1,0},{2,3},{3,2},{4,5},{5,4},{6,7},{7,6},{8,9},{9,8},{10,11... | collective-permute-start | bytes 1572872 | tf_op jit(solution)/shard_map/ppermute | solution.py:239
  51.7 16.4 %collective-permute-start.25 = (bf16[64,4096]{1,0:T(8,128)(2,1)S(1)}, bf16[64,4096]{1,0:T(8,128)(2,1)S(1)}, u32[]{:S(2)}, u32[]{:S(2)}) collective-permute-start(bf16[64,4096]{1,0:T(8,128)(2,1)S(1)} %get-tuple-element.134), channel_id=1, source_target_pairs={{0,1},{1,0},{2,3},{3,2},{4,5},{5,4},{6,7},{7,6},{8,9},{9,8},{10,11... | collective-permute-start | bytes 1572872 | tf_op jit(solution)/shard_map/ppermute | solution.py:239
  65.8 9.2 %collective-permute-start.31 = (bf16[32,4096]{1,0:T(8,128)(2,1)S(1)}, bf16[32,4096]{1,0:T(8,128)(2,1)S(1)}, u32[]{:S(2)}, u32[]{:S(2)}) collective-permute-start(bf16[32,4096]{1,0:T(8,128)(2,1)S(1)} %get-tuple-element.171), channel_id=1, source_target_pairs={{0,2},{1,3},{4,0},{5,1},{8,4},{9,5},{12,8},{13,9},{14,12},{15,13},... | collective-permute-start | bytes 786440 | tf_op jit(solution)/shard_map/ppermute | solution.py:239
  66.5 9.2 %collective-permute-start.32 = (bf16[32,4096]{1,0:T(8,128)(2,1)S(1)}, bf16[32,4096]{1,0:T(8,128)(2,1)S(1)}, u32[]{:S(2)}, u32[]{:S(2)}) collective-permute-start(bf16[32,4096]{1,0:T(8,128)(2,1)S(1)} %get-tuple-element.170), channel_id=1, source_target_pairs={{0,4},{1,5},{4,8},{5,9},{8,12},{9,13},{12,14},{13,15},{14,10},{15,... | collective-permute-start | bytes 786440 | tf_op jit(solution)/shard_map/ppermute | solution.py:239
  68.1 13.2 %collective-permute-start.33 = (bf16[32,4096]{1,0:T(8,128)(2,1)S(1)}, bf16[32,4096]{1,0:T(8,128)(2,1)S(1)}, u32[]{:S(2)}, u32[]{:S(2)}) collective-permute-start(bf16[32,4096]{1,0:T(8,128)(2,1)S(1)} %add_convert_fusion.11), channel_id=1, source_target_pairs={{0,4},{1,5},{4,8},{5,9},{8,12},{9,13},{12,14},{13,15},{14,10},{15,... | collective-permute-start | bytes 786440 | tf_op jit(solution)/shard_map/ppermute | solution.py:239
  69.9 11.5 %collective-permute-start.34 = (bf16[32,4096]{1,0:T(8,128)(2,1)S(1)}, bf16[32,4096]{1,0:T(8,128)(2,1)S(1)}, u32[]{:S(2)}, u32[]{:S(2)}) collective-permute-start(bf16[32,4096]{1,0:T(8,128)(2,1)S(1)} %add_convert_fusion.10), channel_id=1, source_target_pairs={{0,2},{1,3},{4,0},{5,1},{8,4},{9,5},{12,8},{13,9},{14,12},{15,13},... | collective-permute-start | bytes 786440 | tf_op jit(solution)/shard_map/ppermute | solution.py:239
  73.1 12.9 %collective-permute-start.35 = (bf16[64,4096]{1,0:T(8,128)(2,1)S(1)}, bf16[64,4096]{1,0:T(8,128)(2,1)S(1)}, u32[]{:S(2)}, u32[]{:S(2)}) collective-permute-start(bf16[64,4096]{1,0:T(8,128)(2,1)S(1)} %get-tuple-element.150), channel_id=1, source_target_pairs={{0,1},{1,0},{2,3},{3,2},{4,5},{5,4},{6,7},{7,6},{8,9},{9,8},{10,11... | collective-permute-start | bytes 1572872 | tf_op jit(solution)/shard_map/ppermute | solution.py:239
  75.8 9.7 %collective-permute-start.36 = (bf16[32,4096]{1,0:T(8,128)(2,1)S(1)}, bf16[32,4096]{1,0:T(8,128)(2,1)S(1)}, u32[]{:S(2)}, u32[]{:S(2)}) collective-permute-start(bf16[32,4096]{1,0:T(8,128)(2,1)S(1)} %add_convert_fusion.9), channel_id=1, source_target_pairs={{0,2},{1,3},{4,0},{5,1},{8,4},{9,5},{12,8},{13,9},{14,12},{15,13},... | collective-permute-start | bytes 786440 | tf_op jit(solution)/shard_map/ppermute | solution.py:239
  86.1 9.3 %collective-permute-start.38 = (bf16[32,4096]{1,0:T(8,128)(2,1)S(1)}, bf16[32,4096]{1,0:T(8,128)(2,1)S(1)}, u32[]{:S(2)}, u32[]{:S(2)}) collective-permute-start(bf16[32,4096]{1,0:T(8,128)(2,1)S(1)} %add_convert_fusion.5), channel_id=1, source_target_pairs={{0,2},{1,3},{4,0},{5,1},{8,4},{9,5},{12,8},{13,9},{14,12},{15,13},... | collective-permute-start | bytes 786440 | tf_op jit(solution)/shard_map/ppermute | solution.py:239
  87.9 9.2 %collective-permute-start.39 = (bf16[32,4096]{1,0:T(8,128)(2,1)S(1)}, bf16[32,4096]{1,0:T(8,128)(2,1)S(1)}, u32[]{:S(2)}, u32[]{:S(2)}) collective-permute-start(bf16[32,4096]{1,0:T(8,128)(2,1)S(1)} %add_convert_fusion.4), channel_id=1, source_target_pairs={{0,4},{1,5},{4,8},{5,9},{8,12},{9,13},{12,14},{13,15},{14,10},{15,... | collective-permute-start | bytes 786440 | tf_op jit(solution)/shard_map/ppermute | solution.py:239
  88.2 14.6 %collective-permute-start.41 = (bf16[32,4096]{1,0:T(8,128)(2,1)S(1)}, bf16[32,4096]{1,0:T(8,128)(2,1)S(1)}, u32[]{:S(2)}, u32[]{:S(2)}) collective-permute-start(bf16[32,4096]{1,0:T(8,128)(2,1)S(1)} %add_convert_fusion.7), channel_id=1, source_target_pairs={{0,4},{1,5},{4,8},{5,9},{8,12},{9,13},{12,14},{13,15},{14,10},{15,... | collective-permute-start | bytes 786440 | tf_op jit(solution)/shard_map/ppermute | solution.py:239
  89.5 13.3 %collective-permute-start.42 = (bf16[32,4096]{1,0:T(8,128)(2,1)S(1)}, bf16[32,4096]{1,0:T(8,128)(2,1)S(1)}, u32[]{:S(2)}, u32[]{:S(2)}) collective-permute-start(bf16[32,4096]{1,0:T(8,128)(2,1)S(1)} %add_convert_fusion.6), channel_id=1, source_target_pairs={{0,2},{1,3},{4,0},{5,1},{8,4},{9,5},{12,8},{13,9},{14,12},{15,13},... | collective-permute-start | bytes 786440 | tf_op jit(solution)/shard_map/ppermute | solution.py:239
  (21 other events, 116.4 us)

commit v4 on v3

--- a/solution.py
+++ b/solution.py
@@ -13,7 +13,7 @@
 CTX = 1024
 LANES = 128
 CHUNKS = 2
-OPT = {'pair': 'ch', 'swap': 1, 'load_at': (0, 1), 'att_at': (0, 1), 'mine': 2, 'theirs': 3, 'end_mine': 1, 'end_theirs': 1, 'rs': 'B', 'last': 1, 'own_turn': 4, 'att_turn': 6}
+OPT = {'pair': 'ch', 'swap': 0, 'load_at': [0], 'att_at': [0, 1], 'ties': [[0, 3, 0], [0, 3, 0], [2, 3, 0], [2, 3, 0], [2, 3, 0], [2, 3, 0]], 'end_mine': 1, 'end_theirs': 0, 'rs': 'SLSLLSL', 'last': [1, 1, 1, 1, 1, 1, 1, 1], 'own_turn': 3, 'att_turn': [6], 'chain': [0, 2, 0, 0, 0, 1, 0, 0], 'early': 'down', 'own_ag': 9, 'att_ag': [], 'kv': 'msa', 'merge': 0}
 
 
 def attend_body(request, lengths_ref, q_ref, kv, o_ref):
@@ -34,29 +34,19 @@
         o_ref[0, g * group_size : (g + 1) * group_size, :] = mixed.astype(jnp.bfloat16)
 
 
-def attend_kernel(request, lengths_ref, q_ref, kv_hbm, o_ref, kv, sem):
-    copy = pltpu.make_async_copy(kv_hbm.at[request], kv, sem)
-    copy.start()
-    copy.wait()
-    attend_body(request, lengths_ref, q_ref, kv, o_ref)
-
-
-def attend_load_kernel(
-    request, lengths_ref, q_ref, kv_hbm, weight_hbm, o_ref, weight_ref, kv, sem, weight_sem
-):
-    copy = pltpu.make_async_copy(kv_hbm.at[request], kv, sem)
-    copy.start()
-    load = pltpu.make_async_copy(weight_hbm, weight_ref, weight_sem)
-    load.start()
-    copy.wait()
-    attend_body(request, lengths_ref, q_ref, kv, o_ref)
-    load.wait()
-
-
-def load_kernel(weight_hbm, weight_ref, sem):
-    load = pltpu.make_async_copy(weight_hbm, weight_ref, sem)
-    load.start()
-    load.wait()
+def attend_kernel(request, lengths_ref, q_ref, kv_ref, o_ref):
+    attend_body(request, lengths_ref, q_ref, kv_ref.at[request], o_ref)
+
+
+def load_kernel(count, *refs):
+    sems = refs[-1]
+    copies = [
+        pltpu.make_async_copy(refs[i], refs[count + i], sems.at[i]) for i in range(count)
+    ]
+    for copy in copies:
+        copy.start()
+    for copy in copies:
+        copy.wait()
 
 
 VMEM_WHOLE = pl.BlockSpec(memory_space=pltpu.VMEM)
@@ -67,40 +57,35 @@
     return pltpu.with_memory_space_constraint(x, pltpu.HBM)
 
 
-def load(weight):
+def load(*arrays):
     return pl.pallas_call(
-        load_kernel,
-        in_specs=[ANYWHERE],
-        out_specs=VMEM_WHOLE,
-        out_shape=pltpu.VMEM(weight.shape, weight.dtype),
-        scratch_shapes=[pltpu.SemaphoreType.DMA],
+        functools.partial(load_kernel, len(arrays)),
+        in_specs=[ANYWHERE] * len(arrays),
+        out_specs=[VMEM_WHOLE] * len(arrays),
+        out_shape=[pltpu.VMEM(x.shape, x.dtype) for x in arrays],
+        scratch_shapes=[pltpu.SemaphoreType.DMA((len(arrays),))],
         compiler_params=pltpu.CompilerParams(vmem_limit_bytes=1 << 20),
         cost_estimate=pl.CostEstimate(
-            flops=0, bytes_accessed=2 * weight.size, transcendentals=0
+            flops=0, bytes_accessed=2 * sum(x.size for x in arrays), transcendentals=0
         ),
         name="load",
-    )(in_hbm(weight))
-
-
-def attend(request, queries, kv_cache, lengths, *weight):
-    kernel = attend_load_kernel if weight else attend_kernel
+    )(*(in_hbm(x) for x in arrays))
+
+
+def attend(request, queries, kv_cache, lengths):
     return pl.pallas_call(
-        functools.partial(kernel, request),
-        in_specs=[pl.BlockSpec(memory_space=pltpu.SMEM), VMEM_WHOLE, ANYWHERE]
-        + [ANYWHERE] * len(weight),
-        out_specs=[VMEM_WHOLE] * (1 + len(weight)),
-        out_shape=[jax.ShapeDtypeStruct((1, HEADS, HD), jnp.bfloat16)]
-        + [pltpu.VMEM(w.shape, w.dtype) for w in weight],
-        scratch_shapes=[pltpu.VMEM(kv_cache.shape[1:], kv_cache.dtype)]
-        + [pltpu.SemaphoreType.DMA] * (1 + len(weight)),
-        compiler_params=pltpu.CompilerParams(vmem_limit_bytes=6 << 20),
+        functools.partial(attend_kernel, request),
+        in_specs=[pl.BlockSpec(memory_space=pltpu.SMEM), VMEM_WHOLE, VMEM_WHOLE],
+        out_specs=VMEM_WHOLE,
+        out_shape=jax.ShapeDtypeStruct((1, HEADS, HD), jnp.bfloat16),
+        compiler_params=pltpu.CompilerParams(vmem_limit_bytes=2 << 20),
         cost_estimate=pl.CostEstimate(
             flops=4 * HEADS * CTX * HD,
-            bytes_accessed=4 * CTX * KVH * HD + 2 * sum(w.size for w in weight),
+            bytes_accessed=4 * CTX * KVH * HD,
             transcendentals=HEADS * CTX,
         ),
         name="attend",
-    )(lengths, queries, in_hbm(kv_cache), *(in_hbm(w) for w in weight))
+    )(lengths, queries, kv_cache)
 
 
 def expert_kernel(experts, own_ref, sib_ref, in_ref, down_ref, out_own, out_sib, x, hidden):
@@ -241,8 +226,13 @@
     first = prologue(moe_input, route_ids, route_weights, experts)
     requests = queries.shape[0]
     heads = queries.reshape(requests, HEADS, HD)
-    gate_up = load(w_gate_up)
-    begun, down = attend(0, heads, kv_cache, lengths, w_down)
+    rest = list(range(requests))
+    attended = []
+    down = w_down
+    if OPT["kv"] == "load":
+        gate_up, kv_cache = load(w_gate_up, kv_cache)
+    else:
+        (gate_up,) = load(w_gate_up)
 
     long_pair = (("f", 0), ("b", 1))
     short_pair = (("b", 0), ("f", 1))
@@ -257,7 +247,12 @@
     def compute(keys, own):
         slots = {key: i * rows for i, key in enumerate(keys)}
         own = jnp.concatenate(own, axis=0)
-        mine, theirs = expert_apply(experts, own, send(own, swap), gate_up, down)
+        sib = send(own, swap)
+        link = OPT["chain"][min(len(done), 7)]
+        if 0 < link <= len(done):
+            last = done[-link]
+            last[1], sib = lax.optimization_barrier((last[1], sib))
+        mine, theirs = expert_apply(experts, own, sib, gate_up, down)
         return [slots, mine, send(theirs, swap)]
 
     def tie_partial(block, index, group, values):
@@ -272,22 +267,44 @@
     if OPT["swap"]:
         groups = groups[::-1]
     moving = {key: first[key[1]] for key in long_pair + short_pair}
+    def tie_heads(heads, done):
+        if done:
+            done[-1][1], heads = lax.optimization_barrier((done[-1][1], heads))
+        return heads
+
     partial = {}
     done = []
+    own_rows = None
+    waiting = {}
     for s in range(1, half + 1):
         for turn, group in enumerate(groups):
             if s == 2 and turn in OPT["load_at"]:
                 gate_up = tie(gate_up, group, moving)
-            if s == 2 and turn in OPT["att_at"]:
-                begun = tie(begun, group, moving)
-            if s > 2 and OPT["mine"] and len(done) >= OPT["mine"]:
-                tie_partial(done[-OPT["mine"]], 1, group, moving)
-            if OPT["theirs"] and len(done) >= OPT["theirs"]:
-                tie_partial(done[-OPT["theirs"]], 2, group, moving)
-            own = {key: moving[key] for key in group}
+            before = dict(moving)
+            if s > 1:
+                mine, theirs, late = OPT["ties"][min(2 * (s - 2) + turn, 5)]
+                if 0 < mine <= len(done):
+                    tie_partial(done[-mine], 1, group, moving)
+                if 0 < theirs <= len(done):
+                    tie_partial(done[-theirs], 2, group, moving)
+                if not late:
+                    before = dict(moving)
+            if s == 2 and turn == OPT["own_ag"]:
+                own_rows = compute(list(range(CHUNKS)), first)
+                done.append(own_rows)
+            if s > 1 and 2 * (s - 2) + turn in OPT["att_ag"] and rest:
+                heads = tie_heads(heads, done)
+                attended.append(attend(rest.pop(0), heads, kv_cache, lengths))
+                attended[-1] = tie(attended[-1], group, moving)
+            own = {key: before[key] for key in group}
             for key in group:
                 if s < half or key in longs:
                     moving[key] = send(moving[key], outward[key[0]])
+            if s == half and OPT["merge"]:
+                waiting.update(own)
+                if turn == 0:
+                    continue
+                own = waiting
             if s > 1:
                 done.append(compute(list(own), list(own.values())))
                 for key in own:
@@ -300,35 +317,35 @@
     done.append(compute(list(own), list(own.values())))
     for key in own:
         partial[half, key] = done[-1]
-    done[-1][1], first = lax.optimization_barrier((done[-1][1], first))
-    own_rows = compute(list(range(CHUNKS)), first)
+    if own_rows is None:
+        done[-1][1], first = lax.optimization_barrier((done[-1][1], first))
+        own_rows = compute(list(range(CHUNKS)), first)
 
     def local(block, key):
         slots, mine, theirs = block
         span = slice(slots[key], slots[key] + rows)
         return mine[span].astype(jnp.float32) + theirs[span].astype(jnp.float32)
 
-    if OPT["rs"] == "A":
-        order = [(half, long_pair)]
-        for s in range(half - 1, 0, -1):
-            order += [(s, short_pair), (s, long_pair)]
-    else:
-        order = [(half - 1, short_pair), (half, long_pair)]
-        for s in range(half - 2, 0, -1):
-            order += [(s, short_pair), (s + 1, long_pair)]
-        order.append((1, long_pair))
-    rest = list(range(1, requests))
-    attended = [begun]
+    left = {"S": half - 1, "L": half}
+    order = []
+    for letter in OPT["rs"]:
+        order.append((left[letter], short_pair if letter == "S" else long_pair))
+        left[letter] -= 1
+    for s in range(left["S"], 0, -1):
+        order += [(s, short_pair), (left["L"], long_pair)]
+        left["L"] -= 1
+    for s in range(left["L"], 0, -1):
+        order.append((s, long_pair))
     moving = {}
     last = None
     for turn, (s, group) in enumerate(order):
-        if OPT["last"] and last is not None and group[0] in moving:
+        if OPT["last"][min(turn, 7)] and last is not None and group[0] in moving:
             last = tie(last, group, moving)
         if turn == OPT["own_turn"]:
             tie_partial(own_rows, 1, group, moving)
             own_rows[1], heads = lax.optimization_barrier((own_rows[1], heads))
-        if turn >= OPT["att_turn"] and rest:
-            attended += attend(rest.pop(0), heads, kv_cache, lengths)
+        if turn in OPT["att_turn"] and rest:
+            attended.append(attend(rest.pop(0), heads, kv_cache, lengths))
             attended[-1] = tie(attended[-1], group, moving)
         if turn == len(order) - 2:
             tie_partial(own_rows, 2, group, moving)
@@ -341,7 +358,7 @@
         last = totals
         for key, total in zip(group, last):
             moving[key] = send(total, homeward[key[0]])
-    attended += [attend(r, heads, kv_cache, lengths)[0] for r in rest]
+    attended += [attend(r, heads, kv_cache, lengths) for r in rest]
     attended = jnp.concatenate(attended, axis=0).reshape(requests, HEADS * HD)
     out = []
     for k in range(CHUNKS):

time: 107 us -> 102 us (0.953)
  Pallas kernels: 35.3 us -> 31.9 us
    pallas_call x3, Pallas kernels: 12.4 us -> 8.92 us  [the longest x1 4.58 us: load(): pl.pallas_call(functools.partial(load_kernel, len(arrays)), in_specs=[ANY...]
  transfers between devices with their start and end apart: 44 -> 44, of which waited for: 21 -> 23; matrix products, arithmetic and copies ran while one was open for 3% -> 2% of each run, Pallas kernels for 32% -> 30%
where the time goes in v4:
time: 102 us; the launch traced here: 101 us
  starting transfers between devices  33.7 us (33%)
  Pallas kernels  31.9 us (31%)
  waiting for transfers between devices  31.5 us (31%)
  other arithmetic  2.35 us (2%)
  local copies, waits for them, and re-layouts  1.05 us (1%)
  between operations  1.02 us (1%)
    ppermute x44, starting transfers between devices, send(): return lax.ppermute(x, 'expert', pairs)  33.7 us
    ppermute x44, waiting for transfers between devices, send(): return lax.ppermute(x, 'expert', pairs)  31.5 us
    pallas_call x8, Pallas kernels, expert_apply(): pl.pallas_call(functools.partial(expert_kernel, experts), in_specs=[whole...  21.7 us
    pallas_call x1, Pallas kernels, load(): pl.pallas_call(functools.partial(load_kernel, len(arrays)), in_specs=[ANY...  4.58 us
    pallas_call x2, Pallas kernels, attend(): pl.pallas_call(functools.partial(attend_kernel, request), in_specs=[pl.Bl...  4.34 us
  transfers between devices with their start and end apart: 44, of which 23 were waited for; matrix products, arithmetic and copies ran while one was open for 2% of the time, Pallas kernels for 30%

profile of v4, /device:TPU:0, one launch (start us, length us, event | category | flops | bytes accessed | tf_op | source)
XLA Modules:
  0.0 101.5 jit_solution(2355371890959339352)
XLA Ops:
  1.9 3.1 %collective-permute-start = (bf16[32,4224]{1,0:T(8,128)(2,1)S(1)}, bf16[32,4224]{1,0:T(8,128)(2,1)S(1)}, u32[]{:S(2)}, u32[]{:S(2)}) collective-permute-start(bf16[32,4224]{1,0:T(8,128)(2,1)S(1)} %get-tuple-element.105), channel_id=1, source_target_pairs={{0,4},{1,5},{4,8},{5,9},{8,12},{9,13},{12,14},{13,15},{14,10},{15,... | collective-permute-start | bytes 811016 | tf_op jit(solution)/shard_map/ppermute | solution.py:224
  5.0 2.0 %collective-permute-start.8 = (bf16[32,4224]{1,0:T(8,128)(2,1)S(1)}, bf16[32,4224]{1,0:T(8,128)(2,1)S(1)}, u32[]{:S(2)}, u32[]{:S(2)}) collective-permute-start(bf16[32,4224]{1,0:T(8,128)(2,1)S(1)} %get-tuple-element.106), channel_id=1, source_target_pairs={{0,4},{1,5},{4,8},{5,9},{8,12},{9,13},{12,14},{13,15},{14,10},{15,... | collective-permute-start | bytes 811016 | tf_op jit(solution)/shard_map/ppermute | solution.py:224
  7.0 4.6 %load.1.in_ref = bf16[1,4096,1536]{2,1,0:T(8,128)(2,1)S(1)} custom-call(bf16[1,4096,1536]{2,1,0:T(8,128)(2,1)} %refs_0_.1), custom_call_target="tpu_custom_call" | custom-call | bytes 12582912 | tf_op jit(solution)/shard_map/load/pallas_call | solution.py:61
  12.2 2.2 %collective-permute-done.1 = bf16[32,4224]{1,0:T(8,128)(2,1)S(1)} collective-permute-done((bf16[32,4224]{1,0:T(8,128)(2,1)S(1)}, bf16[32,4224]{1,0:T(8,128)(2,1)S(1)}, u32[]{:S(2)}, u32[]{:S(2)}) %collective-permute-start.1) | collective-permute-done | bytes 270368 | tf_op jit(solution)/shard_map/ppermute | solution.py:224
  14.4 1.6 %collective-permute-start.3 = (bf16[32,4224]{1,0:T(8,128)(2,1)S(1)}, bf16[32,4224]{1,0:T(8,128)(2,1)S(1)}, u32[]{:S(2)}, u32[]{:S(2)}) collective-permute-start(bf16[32,4224]{1,0:T(8,128)(2,1)S(1)} %collective-permute-done), channel_id=1, source_target_pairs={{0,4},{1,5},{4,8},{5,9},{8,12},{9,13},{12,14},{13,15},{14,10},{15,... | collective-permute-start | bytes 811016 | tf_op jit(solution)/shard_map/ppermute | solution.py:224
  18.1 2.1 %collective-permute-done.9 = bf16[32,4224]{1,0:T(8,128)(2,1)S(1)} collective-permute-done((bf16[32,4224]{1,0:T(8,128)(2,1)S(1)}, bf16[32,4224]{1,0:T(8,128)(2,1)S(1)}, u32[]{:S(2)}, u32[]{:S(2)}) %collective-permute-start.9) | collective-permute-done | bytes 270368 | tf_op jit(solution)/shard_map/ppermute | solution.py:224
  20.3 1.6 %collective-permute-start.11 = (bf16[32,4224]{1,0:T(8,128)(2,1)S(1)}, bf16[32,4224]{1,0:T(8,128)(2,1)S(1)}, u32[]{:S(2)}, u32[]{:S(2)}) collective-permute-start(bf16[32,4224]{1,0:T(8,128)(2,1)S(1)} %collective-permute-done.8), channel_id=1, source_target_pairs={{0,4},{1,5},{4,8},{5,9},{8,12},{9,13},{12,14},{13,15},{14,10},{15,... | collective-permute-start | bytes 811016 | tf_op jit(solution)/shard_map/ppermute | solution.py:224
  22.4 2.7 %expert.8 = (bf16[64,4096]{1,0:T(8,128)(2,1)S(1)}, bf16[64,4096]{1,0:T(8,128)(2,1)S(1)}) custom-call(bf16[64,4224]{1,0:T(8,128)(2,1)S(1)} %constant_dynamic-update-slice_fusion.own_ref, bf16[64,4224]{1,0:T(8,128)(2,1)S(1)} %collective-permute-done.2.sib_ref, bf16[1,4096,1536]{2,1,0:T(8,128)(2,1)S(1)} %load.1.in_ref, bf16[1,768,4096]{2,1,0:T(8,128)(2,1)S(1)} %bitcast.12), custom_call_target="tpu_custom_call" | custom-call | flops 2415919104 | bytes 2097152 | tf_op jit(solution)/shard_map/expert/pallas_call | solution.py:125
  27.3 2.7 %expert.10 = (bf16[64,4096]{1,0:T(8,128)(2,1)S(1)}, bf16[64,4096]{1,0:T(8,128)(2,1)S(1)}) custom-call(bf16[64,4224]{1,0:T(8,128)(2,1)S(1)} %constant_dynamic-update-slice_fusion.4.own_ref, bf16[64,4224]{1,0:T(8,128)(2,1)S(1)} %collective-permute-done.10.sib_ref, bf16[1,4096,1536]{2,1,0:T(8,128)(2,1)S(1)} %load.1.in_ref, bf16[1,768,4096]{2,1,0:T(8,128)(2,1)S(1)} %bitcast.12), custom_call_target="tpu_custom_call" | custom-call | flops 2415919104 | bytes 2097152 | tf_op jit(solution)/shard_map/expert/pallas_call | solution.py:125
  33.5 2.7 %expert.9 = (bf16[64,4096]{1,0:T(8,128)(2,1)S(1)}, bf16[64,4096]{1,0:T(8,128)(2,1)S(1)}) custom-call(bf16[64,4224]{1,0:T(8,128)(2,1)S(1)} %constant_dynamic-update-slice_fusion.2.own_ref, bf16[64,4224]{1,0:T(8,128)(2,1)S(1)} %collective-permute-done.5.sib_ref, bf16[1,4096,1536]{2,1,0:T(8,128)(2,1)S(1)} %load.1.in_ref, bf16[1,768,4096]{2,1,0:T(8,128)(2,1)S(1)} %bitcast.12), custom_call_target="tpu_custom_call" | custom-call | flops 2415919104 | bytes 2097152 | tf_op jit(solution)/shard_map/expert/pallas_call | solution.py:125
  38.3 2.7 %expert.11 = (bf16[64,4096]{1,0:T(8,128)(2,1)S(1)}, bf16[64,4096]{1,0:T(8,128)(2,1)S(1)}) custom-call(bf16[64,4224]{1,0:T(8,128)(2,1)S(1)} %constant_dynamic-update-slice_fusion.6.own_ref, bf16[64,4224]{1,0:T(8,128)(2,1)S(1)} %collective-permute-done.13.sib_ref, bf16[1,4096,1536]{2,1,0:T(8,128)(2,1)S(1)} %load.1.in_ref, bf16[1,768,4096]{2,1,0:T(8,128)(2,1)S(1)} %bitcast.12), custom_call_target="tpu_custom_call" | custom-call | flops 2415919104 | bytes 2097152 | tf_op jit(solution)/shard_map/expert/pallas_call | solution.py:125
  44.3 2.7 %expert.12 = (bf16[64,4096]{1,0:T(8,128)(2,1)S(1)}, bf16[64,4096]{1,0:T(8,128)(2,1)S(1)}) custom-call(bf16[64,4224]{1,0:T(8,128)(2,1)S(1)} %constant_dynamic-update-slice_fusion.10.own_ref, bf16[64,4224]{1,0:T(8,128)(2,1)S(1)} %collective-permute-done.19.sib_ref, bf16[1,4096,1536]{2,1,0:T(8,128)(2,1)S(1)} %load.1.in_ref, bf16[1,768,4096]{2,1,0:T(8,128)(2,1)S(1)} %bitcast.12), custom_call_target="tpu_custom_call" | custom-call | flops 2415919104 | bytes 2097152 | tf_op jit(solution)/shard_map/expert/pallas_call | solution.py:125
  47.6 2.7 %expert.13 = (bf16[64,4096]{1,0:T(8,128)(2,1)S(1)}, bf16[64,4096]{1,0:T(8,128)(2,1)S(1)}) custom-call(bf16[64,4224]{1,0:T(8,128)(2,1)S(1)} %constant_dynamic-update-slice_fusion.8.own_ref, bf16[64,4224]{1,0:T(8,128)(2,1)S(1)} %collective-permute-done.20.sib_ref, bf16[1,4096,1536]{2,1,0:T(8,128)(2,1)S(1)} %load.1.in_ref, bf16[1,768,4096]{2,1,0:T(8,128)(2,1)S(1)} %bitcast.12), custom_call_target="tpu_custom_call" | custom-call | flops 2415919104 | bytes 2097152 | tf_op jit(solution)/shard_map/expert/pallas_call | solution.py:125
  55.8 2.7 %expert.14 = (bf16[64,4096]{1,0:T(8,128)(2,1)S(1)}, bf16[64,4096]{1,0:T(8,128)(2,1)S(1)}) custom-call(bf16[64,4224]{1,0:T(8,128)(2,1)S(1)} %constant_dynamic-update-slice_fusion.12.own_ref, bf16[64,4224]{1,0:T(8,128)(2,1)S(1)} %collective-permute-done.23.sib_ref, bf16[1,4096,1536]{2,1,0:T(8,128)(2,1)S(1)} %load.1.in_ref, bf16[1,768,4096]{2,1,0:T(8,128)(2,1)S(1)} %bitcast.12), custom_call_target="tpu_custom_call" | custom-call | flops 2415919104 | bytes 2097152 | tf_op jit(solution)/shard_map/expert/pallas_call | solution.py:125
  64.1 2.7 %expert.15 = (bf16[64,4096]{1,0:T(8,128)(2,1)S(1)}, bf16[64,4096]{1,0:T(8,128)(2,1)S(1)}) custom-call(bf16[64,4224]{1,0:T(8,128)(2,1)S(1)} %constant_dynamic-update-slice_fusion.14.own_ref, bf16[64,4224]{1,0:T(8,128)(2,1)S(1)} %collective-permute-done.24.sib_ref, bf16[1,4096,1536]{2,1,0:T(8,128)(2,1)S(1)} %load.1.in_ref, bf16[1,768,4096]{2,1,0:T(8,128)(2,1)S(1)} %bitcast.12), custom_call_target="tpu_custom_call" | custom-call | flops 2415919104 | bytes 2097152 | tf_op jit(solution)/shard_map/expert/pallas_call | solution.py:125
  66.8 2.5 %collective-permute-done.31 = bf16[32,4096]{1,0:T(8,128)(2,1)S(1)} collective-permute-done((bf16[32,4096]{1,0:T(8,128)(2,1)S(1)}, bf16[32,4096]{1,0:T(8,128)(2,1)S(1)}, u32[]{:S(2)}, u32[]{:S(2)}) %collective-permute-start.31) | collective-permute-done | bytes 262176 | tf_op jit(solution)/shard_map/ppermute | solution.py:224
  73.7 2.2 %attend.2 = bf16[1,64,128]{2,1,0:T(8,128)(2,1)S(1)} custom-call(s32[2]{0:T(128)S(1)} %copy-done.1, bf16[2,64,128]{2,1,0:T(8,128)(2,1)S(1)} %bitcast.13, bf16[2,2,1024,512]{3,2,1,0:T(8,128)(2,1)S(1)} %copy-done), custom_call_target="tpu_custom_call" | custom-call | flops 33554432 | bytes 2097152 | tf_op jit(solution)/shard_map/attend/pallas_call | solution.py:76
  75.9 2.8 %collective-permute-done.34 = bf16[32,4096]{1,0:T(8,128)(2,1)S(1)} collective-permute-done((bf16[32,4096]{1,0:T(8,128)(2,1)S(1)}, bf16[32,4096]{1,0:T(8,128)(2,1)S(1)}, u32[]{:S(2)}, u32[]{:S(2)}) %collective-permute-start.34) | collective-permute-done | bytes 262176 | tf_op jit(solution)/shard_map/ppermute | solution.py:224
  80.4 1.6 %collective-permute-start.38 = (bf16[32,4096]{1,0:T(8,128)(2,1)S(1)}, bf16[32,4096]{1,0:T(8,128)(2,1)S(1)}, u32[]{:S(2)}, u32[]{:S(2)}) collective-permute-start(bf16[32,4096]{1,0:T(8,128)(2,1)S(1)} %add_convert_fusion.7), channel_id=1, source_target_pairs={{0,2},{1,3},{4,0},{5,1},{8,4},{9,5},{12,8},{13,9},{14,12},{15,13},... | collective-permute-start | bytes 786440 | tf_op jit(solution)/shard_map/ppermute | solution.py:224
  82.6 3.3 %collective-permute-done.36 = bf16[32,4096]{1,0:T(8,128)(2,1)S(1)} collective-permute-done((bf16[32,4096]{1,0:T(8,128)(2,1)S(1)}, bf16[32,4096]{1,0:T(8,128)(2,1)S(1)}, u32[]{:S(2)}, u32[]{:S(2)}) %collective-permute-start.36) | collective-permute-done | bytes 262176 | tf_op jit(solution)/shard_map/ppermute | solution.py:224
  88.2 1.7 %collective-permute-done.38 = bf16[32,4096]{1,0:T(8,128)(2,1)S(1)} collective-permute-done((bf16[32,4096]{1,0:T(8,128)(2,1)S(1)}, bf16[32,4096]{1,0:T(8,128)(2,1)S(1)}, u32[]{:S(2)}, u32[]{:S(2)}) %collective-permute-start.38) | collective-permute-done | bytes 262176 | tf_op jit(solution)/shard_map/ppermute | solution.py:224
  91.6 1.6 %collective-permute-start.40 = (bf16[32,4096]{1,0:T(8,128)(2,1)S(1)}, bf16[32,4096]{1,0:T(8,128)(2,1)S(1)}, u32[]{:S(2)}, u32[]{:S(2)}) collective-permute-start(bf16[32,4096]{1,0:T(8,128)(2,1)S(1)} %add_convert_fusion.3), channel_id=1, source_target_pairs={{0,2},{1,3},{4,0},{5,1},{8,4},{9,5},{12,8},{13,9},{14,12},{15,13},... | collective-permute-start | bytes 786440 | tf_op jit(solution)/shard_map/ppermute | solution.py:224
  93.8 2.2 %attend.3 = bf16[1,64,128]{2,1,0:T(8,128)(2,1)S(1)} custom-call(s32[2]{0:T(128)S(1)} %copy-done.1, bf16[2,64,128]{2,1,0:T(8,128)(2,1)S(1)} %bitcast.14, bf16[2,2,1024,512]{3,2,1,0:T(8,128)(2,1)S(1)} %copy-done), custom_call_target="tpu_custom_call" | custom-call | flops 33554432 | bytes 2097152 | tf_op jit(solution)/shard_map/attend/pallas_call | solution.py:76
  97.1 2.6 %collective-permute-done.40 = bf16[32,4096]{1,0:T(8,128)(2,1)S(1)} collective-permute-done((bf16[32,4096]{1,0:T(8,128)(2,1)S(1)}, bf16[32,4096]{1,0:T(8,128)(2,1)S(1)}, u32[]{:S(2)}, u32[]{:S(2)}) %collective-permute-start.40) | collective-permute-done | bytes 262176 | tf_op jit(solution)/shard_map/ppermute | solution.py:224
  (121 shorter events, 41.1 us)
Async XLA Ops:
  1.9 10.3 %collective-permute-start = (bf16[32,4224]{1,0:T(8,128)(2,1)S(1)}, bf16[32,4224]{1,0:T(8,128)(2,1)S(1)}, u32[]{:S(2)}, u32[]{:S(2)}) collective-permute-start(bf16[32,4224]{1,0:T(8,128)(2,1)S(1)} %get-tuple-element.105), channel_id=1, source_target_pairs={{0,4},{1,5},{4,8},{5,9},{8,12},{9,13},{12,14},{13,15},{14,10},{15,... | collective-permute-start | bytes 811016 | tf_op jit(solution)/shard_map/ppermute | solution.py:224
  5.0 9.4 %collective-permute-start.1 = (bf16[32,4224]{1,0:T(8,128)(2,1)S(1)}, bf16[32,4224]{1,0:T(8,128)(2,1)S(1)}, u32[]{:S(2)}, u32[]{:S(2)}) collective-permute-start(bf16[32,4224]{1,0:T(8,128)(2,1)S(1)} %get-tuple-element.105), channel_id=1, source_target_pairs={{0,2},{1,3},{4,0},{5,1},{8,4},{9,5},{12,8},{13,9},{14,12},{15,13},... | collective-permute-start | bytes 811016 | tf_op jit(solution)/shard_map/ppermute | solution.py:224
  5.0 13.0 %collective-permute-start.8 = (bf16[32,4224]{1,0:T(8,128)(2,1)S(1)}, bf16[32,4224]{1,0:T(8,128)(2,1)S(1)}, u32[]{:S(2)}, u32[]{:S(2)}) collective-permute-start(bf16[32,4224]{1,0:T(8,128)(2,1)S(1)} %get-tuple-element.106), channel_id=1, source_target_pairs={{0,4},{1,5},{4,8},{5,9},{8,12},{9,13},{12,14},{13,15},{14,10},{15,... | collective-permute-start | bytes 811016 | tf_op jit(solution)/shard_map/ppermute | solution.py:224
  7.0 13.2 %collective-permute-start.9 = (bf16[32,4224]{1,0:T(8,128)(2,1)S(1)}, bf16[32,4224]{1,0:T(8,128)(2,1)S(1)}, u32[]{:S(2)}, u32[]{:S(2)}) collective-permute-start(bf16[32,4224]{1,0:T(8,128)(2,1)S(1)} %get-tuple-element.106), channel_id=1, source_target_pairs={{0,2},{1,3},{4,0},{5,1},{8,4},{9,5},{12,8},{13,9},{14,12},{15,13},... | collective-permute-start | bytes 811016 | tf_op jit(solution)/shard_map/ppermute | solution.py:224
  14.4 10.7 %collective-permute-start.3 = (bf16[32,4224]{1,0:T(8,128)(2,1)S(1)}, bf16[32,4224]{1,0:T(8,128)(2,1)S(1)}, u32[]{:S(2)}, u32[]{:S(2)}) collective-permute-start(bf16[32,4224]{1,0:T(8,128)(2,1)S(1)} %collective-permute-done), channel_id=1, source_target_pairs={{0,4},{1,5},{4,8},{5,9},{8,12},{9,13},{12,14},{13,15},{14,10},{15,... | collective-permute-start | bytes 811016 | tf_op jit(solution)/shard_map/ppermute | solution.py:224
  16.1 9.1 %collective-permute-start.4 = (bf16[32,4224]{1,0:T(8,128)(2,1)S(1)}, bf16[32,4224]{1,0:T(8,128)(2,1)S(1)}, u32[]{:S(2)}, u32[]{:S(2)}) collective-permute-start(bf16[32,4224]{1,0:T(8,128)(2,1)S(1)} %collective-permute-done.1), channel_id=1, source_target_pairs={{0,2},{1,3},{4,0},{5,1},{8,4},{9,5},{12,8},{13,9},{14,12},{15,13},... | collective-permute-start | bytes 811016 | tf_op jit(solution)/shard_map/ppermute | solution.py:224
  20.3 9.8 %collective-permute-start.11 = (bf16[32,4224]{1,0:T(8,128)(2,1)S(1)}, bf16[32,4224]{1,0:T(8,128)(2,1)S(1)}, u32[]{:S(2)}, u32[]{:S(2)}) collective-permute-start(bf16[32,4224]{1,0:T(8,128)(2,1)S(1)} %collective-permute-done.8), channel_id=1, source_target_pairs={{0,4},{1,5},{4,8},{5,9},{8,12},{9,13},{12,14},{13,15},{14,10},{15,... | collective-permute-start | bytes 811016 | tf_op jit(solution)/shard_map/ppermute | solution.py:224
  21.9 9.0 %collective-permute-start.12 = (bf16[32,4224]{1,0:T(8,128)(2,1)S(1)}, bf16[32,4224]{1,0:T(8,128)(2,1)S(1)}, u32[]{:S(2)}, u32[]{:S(2)}) collective-permute-start(bf16[32,4224]{1,0:T(8,128)(2,1)S(1)} %collective-permute-done.9), channel_id=1, source_target_pairs={{0,2},{1,3},{4,0},{5,1},{8,4},{9,5},{12,8},{13,9},{14,12},{15,13},... | collective-permute-start | bytes 811016 | tf_op jit(solution)/shard_map/ppermute | solution.py:224
  25.2 11.1 %collective-permute-start.17 = (bf16[32,4224]{1,0:T(8,128)(2,1)S(1)}, bf16[32,4224]{1,0:T(8,128)(2,1)S(1)}, u32[]{:S(2)}, u32[]{:S(2)}) collective-permute-start(bf16[32,4224]{1,0:T(8,128)(2,1)S(1)} %collective-permute-done.3), channel_id=1, source_target_pairs={{0,4},{1,5},{4,8},{5,9},{8,12},{9,13},{12,14},{13,15},{14,10},{15,... | collective-permute-start | bytes 811016 | tf_op jit(solution)/shard_map/ppermute | solution.py:224
  26.8 9.9 %collective-permute-start.18 = (bf16[32,4224]{1,0:T(8,128)(2,1)S(1)}, bf16[32,4224]{1,0:T(8,128)(2,1)S(1)}, u32[]{:S(2)}, u32[]{:S(2)}) collective-permute-start(bf16[32,4224]{1,0:T(8,128)(2,1)S(1)} %collective-permute-done.4), channel_id=1, source_target_pairs={{0,2},{1,3},{4,0},{5,1},{8,4},{9,5},{12,8},{13,9},{14,12},{15,13},... | collective-permute-start | bytes 811016 | tf_op jit(solution)/shard_map/ppermute | solution.py:224
  30.9 10.1 %collective-permute-start.14 = (bf16[32,4224]{1,0:T(8,128)(2,1)S(1)}, bf16[32,4224]{1,0:T(8,128)(2,1)S(1)}, u32[]{:S(2)}, u32[]{:S(2)}) collective-permute-start(bf16[32,4224]{1,0:T(8,128)(2,1)S(1)} %collective-permute-done.11), channel_id=1, source_target_pairs={{0,4},{1,5},{4,8},{5,9},{8,12},{9,13},{12,14},{13,15},{14,10},{15,... | collective-permute-start | bytes 811016 | tf_op jit(solution)/shard_map/ppermute | solution.py:224
  32.6 9.5 %collective-permute-start.15 = (bf16[32,4224]{1,0:T(8,128)(2,1)S(1)}, bf16[32,4224]{1,0:T(8,128)(2,1)S(1)}, u32[]{:S(2)}, u32[]{:S(2)}) collective-permute-start(bf16[32,4224]{1,0:T(8,128)(2,1)S(1)} %collective-permute-done.12), channel_id=1, source_target_pairs={{0,2},{1,3},{4,0},{5,1},{8,4},{9,5},{12,8},{13,9},{14,12},{15,13},... | collective-permute-start | bytes 811016 | tf_op jit(solution)/shard_map/ppermute | solution.py:224
  42.2 8.9 %collective-permute-start.21 = (bf16[32,4224]{1,0:T(8,128)(2,1)S(1)}, bf16[32,4224]{1,0:T(8,128)(2,1)S(1)}, u32[]{:S(2)}, u32[]{:S(2)}) collective-permute-start(bf16[32,4224]{1,0:T(8,128)(2,1)S(1)} %collective-permute-done.17), channel_id=1, source_target_pairs={{0,4},{1,5},{4,8},{5,9},{8,12},{9,13},{12,14},{13,15},{14,10},{15,... | collective-permute-start | bytes 811016 | tf_op jit(solution)/shard_map/ppermute | solution.py:224
  44.3 19.7 %collective-permute-start.30 = (bf16[64,4096]{1,0:T(8,128)(2,1)S(1)}, bf16[64,4096]{1,0:T(8,128)(2,1)S(1)}, u32[]{:S(2)}, u32[]{:S(2)}) collective-permute-start(bf16[64,4096]{1,0:T(8,128)(2,1)S(1)} %get-tuple-element.118), channel_id=1, source_target_pairs={{0,1},{1,0},{2,3},{3,2},{4,5},{5,4},{6,7},{7,6},{8,9},{9,8},{10,11... | collective-permute-start | bytes 1572872 | tf_op jit(solution)/shard_map/ppermute | solution.py:224
  60.6 8.6 %collective-permute-start.31 = (bf16[32,4096]{1,0:T(8,128)(2,1)S(1)}, bf16[32,4096]{1,0:T(8,128)(2,1)S(1)}, u32[]{:S(2)}, u32[]{:S(2)}) collective-permute-start(bf16[32,4096]{1,0:T(8,128)(2,1)S(1)} %get-tuple-element.147), channel_id=1, source_target_pairs={{0,2},{1,3},{4,0},{5,1},{8,4},{9,5},{12,8},{13,9},{14,12},{15,13},... | collective-permute-start | bytes 786440 | tf_op jit(solution)/shard_map/ppermute | solution.py:224
  69.4 9.3 %collective-permute-start.34 = (bf16[32,4096]{1,0:T(8,128)(2,1)S(1)}, bf16[32,4096]{1,0:T(8,128)(2,1)S(1)}, u32[]{:S(2)}, u32[]{:S(2)}) collective-permute-start(bf16[32,4096]{1,0:T(8,128)(2,1)S(1)} %add_convert_fusion.9), channel_id=1, source_target_pairs={{0,2},{1,3},{4,0},{5,1},{8,4},{9,5},{12,8},{13,9},{14,12},{15,13},... | collective-permute-start | bytes 786440 | tf_op jit(solution)/shard_map/ppermute | solution.py:224
  71.0 9.3 %collective-permute-start.35 = (bf16[32,4096]{1,0:T(8,128)(2,1)S(1)}, bf16[32,4096]{1,0:T(8,128)(2,1)S(1)}, u32[]{:S(2)}, u32[]{:S(2)}) collective-permute-start(bf16[32,4096]{1,0:T(8,128)(2,1)S(1)} %add_convert_fusion.8), channel_id=1, source_target_pairs={{0,4},{1,5},{4,8},{5,9},{8,12},{9,13},{12,14},{13,15},{14,10},{15,... | collective-permute-start | bytes 786440 | tf_op jit(solution)/shard_map/ppermute | solution.py:224
  71.6 14.2 %collective-permute-start.36 = (bf16[32,4096]{1,0:T(8,128)(2,1)S(1)}, bf16[32,4096]{1,0:T(8,128)(2,1)S(1)}, u32[]{:S(2)}, u32[]{:S(2)}) collective-permute-start(bf16[32,4096]{1,0:T(8,128)(2,1)S(1)} %add_convert_fusion.11), channel_id=1, source_target_pairs={{0,4},{1,5},{4,8},{5,9},{8,12},{9,13},{12,14},{13,15},{14,10},{15,... | collective-permute-start | bytes 786440 | tf_op jit(solution)/shard_map/ppermute | solution.py:224
  73.2 12.7 %collective-permute-start.37 = (bf16[32,4096]{1,0:T(8,128)(2,1)S(1)}, bf16[32,4096]{1,0:T(8,128)(2,1)S(1)}, u32[]{:S(2)}, u32[]{:S(2)}) collective-permute-start(bf16[32,4096]{1,0:T(8,128)(2,1)S(1)} %add_convert_fusion.10), channel_id=1, source_target_pairs={{0,2},{1,3},{4,0},{5,1},{8,4},{9,5},{12,8},{13,9},{14,12},{15,13},... | collective-permute-start | bytes 786440 | tf_op jit(solution)/shard_map/ppermute | solution.py:224
  73.7 12.2 %collective-permute-start.33 = (bf16[64,4096]{1,0:T(8,128)(2,1)S(1)}, bf16[64,4096]{1,0:T(8,128)(2,1)S(1)}, u32[]{:S(2)}, u32[]{:S(2)}) collective-permute-start(bf16[64,4096]{1,0:T(8,128)(2,1)S(1)} %get-tuple-element.126), channel_id=1, source_target_pairs={{0,1},{1,0},{2,3},{3,2},{4,5},{5,4},{6,7},{7,6},{8,9},{9,8},{10,11... | collective-permute-start | bytes 1572872 | tf_op jit(solution)/shard_map/ppermute | solution.py:224
  80.4 9.5 %collective-permute-start.38 = (bf16[32,4096]{1,0:T(8,128)(2,1)S(1)}, bf16[32,4096]{1,0:T(8,128)(2,1)S(1)}, u32[]{:S(2)}, u32[]{:S(2)}) collective-permute-start(bf16[32,4096]{1,0:T(8,128)(2,1)S(1)} %add_convert_fusion.7), channel_id=1, source_target_pairs={{0,2},{1,3},{4,0},{5,1},{8,4},{9,5},{12,8},{13,9},{14,12},{15,13},... | collective-permute-start | bytes 786440 | tf_op jit(solution)/shard_map/ppermute | solution.py:224
  82.1 9.4 %collective-permute-start.39 = (bf16[32,4096]{1,0:T(8,128)(2,1)S(1)}, bf16[32,4096]{1,0:T(8,128)(2,1)S(1)}, u32[]{:S(2)}, u32[]{:S(2)}) collective-permute-start(bf16[32,4096]{1,0:T(8,128)(2,1)S(1)} %add_convert_fusion.6), channel_id=1, source_target_pairs={{0,4},{1,5},{4,8},{5,9},{8,12},{9,13},{12,14},{13,15},{14,10},{15,... | collective-permute-start | bytes 786440 | tf_op jit(solution)/shard_map/ppermute | solution.py:224
  86.0 11.1 %collective-permute-start.41 = (bf16[32,4096]{1,0:T(8,128)(2,1)S(1)}, bf16[32,4096]{1,0:T(8,128)(2,1)S(1)}, u32[]{:S(2)}, u32[]{:S(2)}) collective-permute-start(bf16[32,4096]{1,0:T(8,128)(2,1)S(1)} %add_convert_fusion.5), channel_id=1, source_target_pairs={{0,4},{1,5},{4,8},{5,9},{8,12},{9,13},{12,14},{13,15},{14,10},{15,... | collective-permute-start | bytes 786440 | tf_op jit(solution)/shard_map/ppermute | solution.py:224
  86.7 10.4 %collective-permute-start.42 = (bf16[32,4096]{1,0:T(8,128)(2,1)S(1)}, bf16[32,4096]{1,0:T(8,128)(2,1)S(1)}, u32[]{:S(2)}, u32[]{:S(2)}) collective-permute-start(bf16[32,4096]{1,0:T(8,128)(2,1)S(1)} %add_convert_fusion.4), channel_id=1, source_target_pairs={{0,2},{1,3},{4,0},{5,1},{8,4},{9,5},{12,8},{13,9},{14,12},{15,13},... | collective-permute-start | bytes 786440 | tf_op jit(solution)/shard_map/ppermute | solution.py:224
  (25 other events, 190.4 us)

commit v5 on v4

--- a/solution.py
+++ b/solution.py
@@ -13,7 +13,7 @@
 CTX = 1024
 LANES = 128
 CHUNKS = 2
-OPT = {'pair': 'ch', 'swap': 0, 'load_at': [0], 'att_at': [0, 1], 'ties': [[0, 3, 0], [0, 3, 0], [2, 3, 0], [2, 3, 0], [2, 3, 0], [2, 3, 0]], 'end_mine': 1, 'end_theirs': 0, 'rs': 'SLSLLSL', 'last': [1, 1, 1, 1, 1, 1, 1, 1], 'own_turn': 3, 'att_turn': [6], 'chain': [0, 2, 0, 0, 0, 1, 0, 0], 'early': 'down', 'own_ag': 9, 'att_ag': [], 'kv': 'msa', 'merge': 0}
+OPT = {'pair': 'ls', 'swap': 1, 'load_at': [0], 'att_at': [0, 1], 'ties': [[0, 3, 0], [0, 3, 0], [2, 3, 0], [2, 3, 0], [2, 3, 0], [0, 4, 0]], 'end_mine': 1, 'end_theirs': 2, 'rs': 'SSLLLSL', 'last': [1, 1, 0, 1, 1, 1, 1, 1], 'own_turn': 3, 'att_turn': [6], 'chain': [0, 2, 0, 0, 0, 1, 0, 0], 'early': 'down', 'own_ag': 9, 'att_ag': [], 'kv': 'msa', 'merge': 0}
 
 
 def attend_body(request, lengths_ref, q_ref, kv, o_ref):
@@ -146,8 +146,8 @@
 
 
 def prologue_kernel(experts, x_hbm, ids_hbm, weights_hbm, *refs):
-    chunk_refs = refs[:CHUNKS]
-    ids_ref, weights_ref, sems = refs[CHUNKS:]
+    chunk_refs = refs[: 2 * CHUNKS]
+    ids_ref, weights_ref, sems = refs[2 * CHUNKS :]
     tokens, width = x_hbm.shape
     top = ids_hbm.shape[0]
     rows = tokens // CHUNKS
@@ -157,7 +157,7 @@
     ]
     large = [
         pltpu.make_async_copy(
-            x_hbm.at[pl.ds(k * rows, rows)], ref.at[:, pl.ds(0, width)], sems.at[2 + k]
+            x_hbm.at[pl.ds(k % CHUNKS * rows, rows)], ref.at[:, pl.ds(0, width)], sems.at[2 + k]
         )
         for k, ref in enumerate(chunk_refs)
     ]
@@ -179,7 +179,7 @@
     parts = jnp.where(lane < experts, high, jnp.where(lane < 2 * experts, middle, low))
     parts = jnp.where(lane < 3 * experts, parts, 0.0).astype(jnp.bfloat16)
     for k, ref in enumerate(chunk_refs):
-        ref[:, width:] = parts[k * rows : (k + 1) * rows, :]
+        ref[:, width:] = parts[k % CHUNKS * rows : (k % CHUNKS + 1) * rows, :]
     for copy in large:
         copy.wait()
 
@@ -190,14 +190,14 @@
     return pl.pallas_call(
         functools.partial(prologue_kernel, experts),
         in_specs=[ANYWHERE] * 3,
-        out_specs=[VMEM_WHOLE] * CHUNKS,
+        out_specs=[VMEM_WHOLE] * (2 * CHUNKS),
         out_shape=[
             jax.ShapeDtypeStruct((tokens // CHUNKS, width + LANES), jnp.bfloat16)
-        ] * CHUNKS,
+        ] * (2 * CHUNKS),
         scratch_shapes=[
             pltpu.VMEM((top, tokens), jnp.int32),
             pltpu.VMEM((top, tokens), jnp.float32),
-            pltpu.SemaphoreType.DMA((2 + CHUNKS,)),
+            pltpu.SemaphoreType.DMA((2 + 2 * CHUNKS,)),
         ],
         compiler_params=pltpu.CompilerParams(vmem_limit_bytes=4 << 20),
         name="prologue",
@@ -266,7 +266,8 @@
         groups = ((("f", 0), ("b", 0)), (("f", 1), ("b", 1)))
     if OPT["swap"]:
         groups = groups[::-1]
-    moving = {key: first[key[1]] for key in long_pair + short_pair}
+    moving = {key: first[key[1] if key in groups[0] else CHUNKS + key[1]] for key in long_pair + short_pair}
+    first = first[:CHUNKS]
     def tie_heads(heads, done):
         if done:
             done[-1][1], heads = lax.optimization_barrier((done[-1][1], heads))

time: 102 us -> 101 us (level)
  waiting for transfers between devices: 31.5 us -> 30.1 us
    ppermute x44, waiting for transfers between devices: 31.5 us -> 30.1 us  [send(): return lax.ppermute(x, 'expert', pairs)]
  transfers between devices with their start and end apart: 44 -> 44, of which waited for: 23 -> 18; matrix products, arithmetic and copies ran while one was open for 2% -> 2% of each run, Pallas kernels for 30% -> 31%
where the time goes in v5:
time: 101 us
  starting transfers between devices  34 us (34%)
  Pallas kernels  32.2 us (32%)
  waiting for transfers between devices  30.1 us (30%)
  other arithmetic  2.35 us (2%)
  local copies, waits for them, and re-layouts  1.04 us (1%)
  between operations  1.01 us (1%)
    ppermute x44, starting transfers between devices, send(): return lax.ppermute(x, 'expert', pairs)  34 us
    ppermute x44, waiting for transfers between devices, send(): return lax.ppermute(x, 'expert', pairs)  30.1 us
    pallas_call x8, Pallas kernels, expert_apply(): pl.pallas_call(functools.partial(expert_kernel, experts), in_specs=[whole...  21.6 us
    pallas_call x1, Pallas kernels, load(): pl.pallas_call(functools.partial(load_kernel, len(arrays)), in_specs=[ANY...  4.73 us
    pallas_call x2, Pallas kernels, attend(): pl.pallas_call(functools.partial(attend_kernel, request), in_specs=[pl.Bl...  4.34 us
  transfers between devices with their start and end apart: 44, of which 18 were waited for; matrix products, arithmetic and copies ran while one was open for 2% of the time, Pallas kernels for 31%

profile of v5, /device:TPU:0, one launch (start us, length us, event | category | flops | bytes accessed | tf_op | source)
XLA Modules:
  0.0 100.6 jit_solution(6215986443606717851)
XLA Ops:
  2.1 3.0 %collective-permute-start.3 = (bf16[32,4224]{1,0:T(8,128)(2,1)S(1)}, bf16[32,4224]{1,0:T(8,128)(2,1)S(1)}, u32[]{:S(2)}, u32[]{:S(2)}) collective-permute-start(bf16[32,4224]{1,0:T(8,128)(2,1)S(1)} %get-tuple-element.109), channel_id=1, source_target_pairs={{0,2},{1,3},{4,0},{5,1},{8,4},{9,5},{12,8},{13,9},{14,12},{15,13},... | collective-permute-start | bytes 811016 | tf_op jit(solution)/shard_map/ppermute | solution.py:224
  5.2 2.0 %collective-permute-start = (bf16[32,4224]{1,0:T(8,128)(2,1)S(1)}, bf16[32,4224]{1,0:T(8,128)(2,1)S(1)}, u32[]{:S(2)}, u32[]{:S(2)}) collective-permute-start(bf16[32,4224]{1,0:T(8,128)(2,1)S(1)} %get-tuple-element.75), channel_id=1, source_target_pairs={{0,4},{1,5},{4,8},{5,9},{8,12},{9,13},{12,14},{13,15},{14,10},{15,... | collective-permute-start | bytes 811016 | tf_op jit(solution)/shard_map/ppermute | solution.py:224
  7.3 4.7 %load.1.in_ref = bf16[1,4096,1536]{2,1,0:T(8,128)(2,1)S(1)} custom-call(bf16[1,4096,1536]{2,1,0:T(8,128)(2,1)} %refs_0_.1), custom_call_target="tpu_custom_call" | custom-call | bytes 12582912 | tf_op jit(solution)/shard_map/load/pallas_call | solution.py:61
  12.5 2.0 %collective-permute-done.4 = bf16[32,4224]{1,0:T(8,128)(2,1)S(1)} collective-permute-done((bf16[32,4224]{1,0:T(8,128)(2,1)S(1)}, bf16[32,4224]{1,0:T(8,128)(2,1)S(1)}, u32[]{:S(2)}, u32[]{:S(2)}) %collective-permute-start.4) | collective-permute-done | bytes 270368 | tf_op jit(solution)/shard_map/ppermute | solution.py:224
  14.5 1.6 %collective-permute-start.7 = (bf16[32,4224]{1,0:T(8,128)(2,1)S(1)}, bf16[32,4224]{1,0:T(8,128)(2,1)S(1)}, u32[]{:S(2)}, u32[]{:S(2)}) collective-permute-start(bf16[32,4224]{1,0:T(8,128)(2,1)S(1)} %collective-permute-done.3), channel_id=1, source_target_pairs={{0,2},{1,3},{4,0},{5,1},{8,4},{9,5},{12,8},{13,9},{14,12},{15,13},... | collective-permute-start | bytes 811016 | tf_op jit(solution)/shard_map/ppermute | solution.py:224
  16.7 3.6 %collective-permute-done = bf16[32,4224]{1,0:T(8,128)(2,1)S(1)} collective-permute-done((bf16[32,4224]{1,0:T(8,128)(2,1)S(1)}, bf16[32,4224]{1,0:T(8,128)(2,1)S(1)}, u32[]{:S(2)}, u32[]{:S(2)}) %collective-permute-start) | collective-permute-done | bytes 270368 | tf_op jit(solution)/shard_map/ppermute | solution.py:224
  20.6 1.9 %collective-permute-start.16 = (bf16[32,4224]{1,0:T(8,128)(2,1)S(1)}, bf16[32,4224]{1,0:T(8,128)(2,1)S(1)}, u32[]{:S(2)}, u32[]{:S(2)}) collective-permute-start(bf16[32,4224]{1,0:T(8,128)(2,1)S(1)} %collective-permute-done.1), channel_id=1, source_target_pairs={{0,2},{1,3},{4,0},{5,1},{8,4},{9,5},{12,8},{13,9},{14,12},{15,13},... | collective-permute-start | bytes 811016 | tf_op jit(solution)/shard_map/ppermute | solution.py:224
  22.5 2.7 %expert.9 = (bf16[64,4096]{1,0:T(8,128)(2,1)S(1)}, bf16[64,4096]{1,0:T(8,128)(2,1)S(1)}) custom-call(bf16[64,4224]{1,0:T(8,128)(2,1)S(1)} %constant_dynamic-update-slice_fusion.2.own_ref, bf16[64,4224]{1,0:T(8,128)(2,1)S(1)} %collective-permute-done.6.sib_ref, bf16[1,4096,1536]{2,1,0:T(8,128)(2,1)S(1)} %load.1.in_ref, bf16[1,768,4096]{2,1,0:T(8,128)(2,1)S(1)} %bitcast.12), custom_call_target="tpu_custom_call" | custom-call | flops 2415919104 | bytes 2097152 | tf_op jit(solution)/shard_map/expert/pallas_call | solution.py:125
  25.7 1.6 %collective-permute-start.10 = (bf16[32,4224]{1,0:T(8,128)(2,1)S(1)}, bf16[32,4224]{1,0:T(8,128)(2,1)S(1)}, u32[]{:S(2)}, u32[]{:S(2)}) collective-permute-start(bf16[32,4224]{1,0:T(8,128)(2,1)S(1)} %collective-permute-done.7), channel_id=1, source_target_pairs={{0,2},{1,3},{4,0},{5,1},{8,4},{9,5},{12,8},{13,9},{14,12},{15,13},... | collective-permute-start | bytes 811016 | tf_op jit(solution)/shard_map/ppermute | solution.py:224
  27.8 2.7 %expert.8 = (bf16[64,4096]{1,0:T(8,128)(2,1)S(1)}, bf16[64,4096]{1,0:T(8,128)(2,1)S(1)}) custom-call(bf16[64,4224]{1,0:T(8,128)(2,1)S(1)} %constant_dynamic-update-slice_fusion.own_ref, bf16[64,4224]{1,0:T(8,128)(2,1)S(1)} %collective-permute-done.2.sib_ref, bf16[1,4096,1536]{2,1,0:T(8,128)(2,1)S(1)} %load.1.in_ref, bf16[1,768,4096]{2,1,0:T(8,128)(2,1)S(1)} %bitcast.12), custom_call_target="tpu_custom_call" | custom-call | flops 2415919104 | bytes 2097152 | tf_op jit(solution)/shard_map/expert/pallas_call | solution.py:125
  34.2 2.7 %expert.10 = (bf16[64,4096]{1,0:T(8,128)(2,1)S(1)}, bf16[64,4096]{1,0:T(8,128)(2,1)S(1)}) custom-call(bf16[64,4224]{1,0:T(8,128)(2,1)S(1)} %constant_dynamic-update-slice_fusion.4.own_ref, bf16[64,4224]{1,0:T(8,128)(2,1)S(1)} %collective-permute-done.9.sib_ref, bf16[1,4096,1536]{2,1,0:T(8,128)(2,1)S(1)} %load.1.in_ref, bf16[1,768,4096]{2,1,0:T(8,128)(2,1)S(1)} %bitcast.12), custom_call_target="tpu_custom_call" | custom-call | flops 2415919104 | bytes 2097152 | tf_op jit(solution)/shard_map/expert/pallas_call | solution.py:125
  37.1 5.0 %collective-permute-done.17 = bf16[32,4224]{1,0:T(8,128)(2,1)S(1)} collective-permute-done((bf16[32,4224]{1,0:T(8,128)(2,1)S(1)}, bf16[32,4224]{1,0:T(8,128)(2,1)S(1)}, u32[]{:S(2)}, u32[]{:S(2)}) %collective-permute-start.17) | collective-permute-done | bytes 270368 | tf_op jit(solution)/shard_map/ppermute | solution.py:224
  44.3 2.7 %expert.11 = (bf16[64,4096]{1,0:T(8,128)(2,1)S(1)}, bf16[64,4096]{1,0:T(8,128)(2,1)S(1)}) custom-call(bf16[64,4224]{1,0:T(8,128)(2,1)S(1)} %constant_dynamic-update-slice_fusion.6.own_ref, bf16[64,4224]{1,0:T(8,128)(2,1)S(1)} %collective-permute-done.12.sib_ref, bf16[1,4096,1536]{2,1,0:T(8,128)(2,1)S(1)} %load.1.in_ref, bf16[1,768,4096]{2,1,0:T(8,128)(2,1)S(1)} %bitcast.12), custom_call_target="tpu_custom_call" | custom-call | flops 2415919104 | bytes 2097152 | tf_op jit(solution)/shard_map/expert/pallas_call | solution.py:125
  47.7 2.7 %expert.12 = (bf16[64,4096]{1,0:T(8,128)(2,1)S(1)}, bf16[64,4096]{1,0:T(8,128)(2,1)S(1)}) custom-call(bf16[64,4224]{1,0:T(8,128)(2,1)S(1)} %constant_dynamic-update-slice_fusion.8.own_ref, bf16[64,4224]{1,0:T(8,128)(2,1)S(1)} %collective-permute-done.19.sib_ref, bf16[1,4096,1536]{2,1,0:T(8,128)(2,1)S(1)} %load.1.in_ref, bf16[1,768,4096]{2,1,0:T(8,128)(2,1)S(1)} %bitcast.12), custom_call_target="tpu_custom_call" | custom-call | flops 2415919104 | bytes 2097152 | tf_op jit(solution)/shard_map/expert/pallas_call | solution.py:125
  53.4 2.7 %expert.13 = (bf16[64,4096]{1,0:T(8,128)(2,1)S(1)}, bf16[64,4096]{1,0:T(8,128)(2,1)S(1)}) custom-call(bf16[64,4224]{1,0:T(8,128)(2,1)S(1)} %constant_dynamic-update-slice_fusion.10.own_ref, bf16[64,4224]{1,0:T(8,128)(2,1)S(1)} %collective-permute-done.22.sib_ref, bf16[1,4096,1536]{2,1,0:T(8,128)(2,1)S(1)} %load.1.in_ref, bf16[1,768,4096]{2,1,0:T(8,128)(2,1)S(1)} %bitcast.12), custom_call_target="tpu_custom_call" | custom-call | flops 2415919104 | bytes 2097152 | tf_op jit(solution)/shard_map/expert/pallas_call | solution.py:125
  58.5 1.6 %collective-permute-start.25 = (bf16[32,4096]{1,0:T(8,128)(2,1)S(1)}, bf16[32,4096]{1,0:T(8,128)(2,1)S(1)}, u32[]{:S(2)}, u32[]{:S(2)}) collective-permute-start(bf16[32,4096]{1,0:T(8,128)(2,1)S(1)} %get-tuple-element.163), channel_id=1, source_target_pairs={{0,2},{1,3},{4,0},{5,1},{8,4},{9,5},{12,8},{13,9},{14,12},{15,13},... | collective-permute-start | bytes 786440 | tf_op jit(solution)/shard_map/ppermute | solution.py:224
  60.9 2.7 %expert.15 = (bf16[64,4096]{1,0:T(8,128)(2,1)S(1)}, bf16[64,4096]{1,0:T(8,128)(2,1)S(1)}) custom-call(bf16[64,4224]{1,0:T(8,128)(2,1)S(1)} %constant_dynamic-update-slice_fusion.14.own_ref, bf16[64,4224]{1,0:T(8,128)(2,1)S(1)} %collective-permute-done.28.sib_ref, bf16[1,4096,1536]{2,1,0:T(8,128)(2,1)S(1)} %load.1.in_ref, bf16[1,768,4096]{2,1,0:T(8,128)(2,1)S(1)} %bitcast.12), custom_call_target="tpu_custom_call" | custom-call | flops 2415919104 | bytes 2097152 | tf_op jit(solution)/shard_map/expert/pallas_call | solution.py:125
  64.2 2.7 %expert.14 = (bf16[64,4096]{1,0:T(8,128)(2,1)S(1)}, bf16[64,4096]{1,0:T(8,128)(2,1)S(1)}) custom-call(bf16[64,4224]{1,0:T(8,128)(2,1)S(1)} %constant_dynamic-update-slice_fusion.12.own_ref, bf16[64,4224]{1,0:T(8,128)(2,1)S(1)} %collective-permute-done.23.sib_ref, bf16[1,4096,1536]{2,1,0:T(8,128)(2,1)S(1)} %load.1.in_ref, bf16[1,768,4096]{2,1,0:T(8,128)(2,1)S(1)} %bitcast.12), custom_call_target="tpu_custom_call" | custom-call | flops 2415919104 | bytes 2097152 | tf_op jit(solution)/shard_map/expert/pallas_call | solution.py:125
  68.4 1.6 %collective-permute-start.31 = (bf16[32,4096]{1,0:T(8,128)(2,1)S(1)}, bf16[32,4096]{1,0:T(8,128)(2,1)S(1)}, u32[]{:S(2)}, u32[]{:S(2)}) collective-permute-start(bf16[32,4096]{1,0:T(8,128)(2,1)S(1)} %get-tuple-element.161), channel_id=1, source_target_pairs={{0,2},{1,3},{4,0},{5,1},{8,4},{9,5},{12,8},{13,9},{14,12},{15,13},... | collective-permute-start | bytes 786440 | tf_op jit(solution)/shard_map/ppermute | solution.py:224
  72.8 2.2 %attend.2 = bf16[1,64,128]{2,1,0:T(8,128)(2,1)S(1)} custom-call(s32[2]{0:T(128)S(1)} %copy-done.1, bf16[2,64,128]{2,1,0:T(8,128)(2,1)S(1)} %bitcast.13, bf16[2,2,1024,512]{3,2,1,0:T(8,128)(2,1)S(1)} %copy-done), custom_call_target="tpu_custom_call" | custom-call | flops 33554432 | bytes 2097152 | tf_op jit(solution)/shard_map/attend/pallas_call | solution.py:76
  75.0 2.8 %collective-permute-done.31 = bf16[32,4096]{1,0:T(8,128)(2,1)S(1)} collective-permute-done((bf16[32,4096]{1,0:T(8,128)(2,1)S(1)}, bf16[32,4096]{1,0:T(8,128)(2,1)S(1)}, u32[]{:S(2)}, u32[]{:S(2)}) %collective-permute-start.31) | collective-permute-done | bytes 262176 | tf_op jit(solution)/shard_map/ppermute | solution.py:224
  85.2 3.6 %collective-permute-done.38 = bf16[32,4096]{1,0:T(8,128)(2,1)S(1)} collective-permute-done((bf16[32,4096]{1,0:T(8,128)(2,1)S(1)}, bf16[32,4096]{1,0:T(8,128)(2,1)S(1)}, u32[]{:S(2)}, u32[]{:S(2)}) %collective-permute-start.38) | collective-permute-done | bytes 262176 | tf_op jit(solution)/shard_map/ppermute | solution.py:224
  92.6 2.2 %attend.3 = bf16[1,64,128]{2,1,0:T(8,128)(2,1)S(1)} custom-call(s32[2]{0:T(128)S(1)} %copy-done.1, bf16[2,64,128]{2,1,0:T(8,128)(2,1)S(1)} %bitcast.14, bf16[2,2,1024,512]{3,2,1,0:T(8,128)(2,1)S(1)} %copy-done), custom_call_target="tpu_custom_call" | custom-call | flops 33554432 | bytes 2097152 | tf_op jit(solution)/shard_map/attend/pallas_call | solution.py:76
  95.9 2.3 %collective-permute-done.40 = bf16[32,4096]{1,0:T(8,128)(2,1)S(1)} collective-permute-done((bf16[32,4096]{1,0:T(8,128)(2,1)S(1)}, bf16[32,4096]{1,0:T(8,128)(2,1)S(1)}, u32[]{:S(2)}, u32[]{:S(2)}) %collective-permute-start.40) | collective-permute-done | bytes 262176 | tf_op jit(solution)/shard_map/ppermute | solution.py:224
  (115 shorter events, 36.2 us)
Async XLA Ops:
  2.1 10.4 %collective-permute-start.3 = (bf16[32,4224]{1,0:T(8,128)(2,1)S(1)}, bf16[32,4224]{1,0:T(8,128)(2,1)S(1)}, u32[]{:S(2)}, u32[]{:S(2)}) collective-permute-start(bf16[32,4224]{1,0:T(8,128)(2,1)S(1)} %get-tuple-element.109), channel_id=1, source_target_pairs={{0,2},{1,3},{4,0},{5,1},{8,4},{9,5},{12,8},{13,9},{14,12},{15,13},... | collective-permute-start | bytes 811016 | tf_op jit(solution)/shard_map/ppermute | solution.py:224
  5.1 9.4 %collective-permute-start.4 = (bf16[32,4224]{1,0:T(8,128)(2,1)S(1)}, bf16[32,4224]{1,0:T(8,128)(2,1)S(1)}, u32[]{:S(2)}, u32[]{:S(2)}) collective-permute-start(bf16[32,4224]{1,0:T(8,128)(2,1)S(1)} %get-tuple-element.110), channel_id=1, source_target_pairs={{0,4},{1,5},{4,8},{5,9},{8,12},{9,13},{12,14},{13,15},{14,10},{15,... | collective-permute-start | bytes 811016 | tf_op jit(solution)/shard_map/ppermute | solution.py:224
  5.2 15.1 %collective-permute-start = (bf16[32,4224]{1,0:T(8,128)(2,1)S(1)}, bf16[32,4224]{1,0:T(8,128)(2,1)S(1)}, u32[]{:S(2)}, u32[]{:S(2)}) collective-permute-start(bf16[32,4224]{1,0:T(8,128)(2,1)S(1)} %get-tuple-element.75), channel_id=1, source_target_pairs={{0,4},{1,5},{4,8},{5,9},{8,12},{9,13},{12,14},{13,15},{14,10},{15,... | collective-permute-start | bytes 811016 | tf_op jit(solution)/shard_map/ppermute | solution.py:224
  7.2 13.1 %collective-permute-start.1 = (bf16[32,4224]{1,0:T(8,128)(2,1)S(1)}, bf16[32,4224]{1,0:T(8,128)(2,1)S(1)}, u32[]{:S(2)}, u32[]{:S(2)}) collective-permute-start(bf16[32,4224]{1,0:T(8,128)(2,1)S(1)} %get-tuple-element.76), channel_id=1, source_target_pairs={{0,2},{1,3},{4,0},{5,1},{8,4},{9,5},{12,8},{13,9},{14,12},{15,13},... | collective-permute-start | bytes 811016 | tf_op jit(solution)/shard_map/ppermute | solution.py:224
  14.5 10.7 %collective-permute-start.7 = (bf16[32,4224]{1,0:T(8,128)(2,1)S(1)}, bf16[32,4224]{1,0:T(8,128)(2,1)S(1)}, u32[]{:S(2)}, u32[]{:S(2)}) collective-permute-start(bf16[32,4224]{1,0:T(8,128)(2,1)S(1)} %collective-permute-done.3), channel_id=1, source_target_pairs={{0,2},{1,3},{4,0},{5,1},{8,4},{9,5},{12,8},{13,9},{14,12},{15,13},... | collective-permute-start | bytes 811016 | tf_op jit(solution)/shard_map/ppermute | solution.py:224
  16.2 9.5 %collective-permute-start.8 = (bf16[32,4224]{1,0:T(8,128)(2,1)S(1)}, bf16[32,4224]{1,0:T(8,128)(2,1)S(1)}, u32[]{:S(2)}, u32[]{:S(2)}) collective-permute-start(bf16[32,4224]{1,0:T(8,128)(2,1)S(1)} %collective-permute-done.4), channel_id=1, source_target_pairs={{0,4},{1,5},{4,8},{5,9},{8,12},{9,13},{12,14},{13,15},{14,10},{15,... | collective-permute-start | bytes 811016 | tf_op jit(solution)/shard_map/ppermute | solution.py:224
  20.4 10.1 %collective-permute-start.15 = (bf16[32,4224]{1,0:T(8,128)(2,1)S(1)}, bf16[32,4224]{1,0:T(8,128)(2,1)S(1)}, u32[]{:S(2)}, u32[]{:S(2)}) collective-permute-start(bf16[32,4224]{1,0:T(8,128)(2,1)S(1)} %collective-permute-done), channel_id=1, source_target_pairs={{0,4},{1,5},{4,8},{5,9},{8,12},{9,13},{12,14},{13,15},{14,10},{15,... | collective-permute-start | bytes 811016 | tf_op jit(solution)/shard_map/ppermute | solution.py:224
  20.6 10.3 %collective-permute-start.16 = (bf16[32,4224]{1,0:T(8,128)(2,1)S(1)}, bf16[32,4224]{1,0:T(8,128)(2,1)S(1)}, u32[]{:S(2)}, u32[]{:S(2)}) collective-permute-start(bf16[32,4224]{1,0:T(8,128)(2,1)S(1)} %collective-permute-done.1), channel_id=1, source_target_pairs={{0,2},{1,3},{4,0},{5,1},{8,4},{9,5},{12,8},{13,9},{14,12},{15,13},... | collective-permute-start | bytes 811016 | tf_op jit(solution)/shard_map/ppermute | solution.py:224
  25.7 11.2 %collective-permute-start.10 = (bf16[32,4224]{1,0:T(8,128)(2,1)S(1)}, bf16[32,4224]{1,0:T(8,128)(2,1)S(1)}, u32[]{:S(2)}, u32[]{:S(2)}) collective-permute-start(bf16[32,4224]{1,0:T(8,128)(2,1)S(1)} %collective-permute-done.7), channel_id=1, source_target_pairs={{0,2},{1,3},{4,0},{5,1},{8,4},{9,5},{12,8},{13,9},{14,12},{15,13},... | collective-permute-start | bytes 811016 | tf_op jit(solution)/shard_map/ppermute | solution.py:224
  27.3 9.6 %collective-permute-start.11 = (bf16[32,4224]{1,0:T(8,128)(2,1)S(1)}, bf16[32,4224]{1,0:T(8,128)(2,1)S(1)}, u32[]{:S(2)}, u32[]{:S(2)}) collective-permute-start(bf16[32,4224]{1,0:T(8,128)(2,1)S(1)} %collective-permute-done.8), channel_id=1, source_target_pairs={{0,4},{1,5},{4,8},{5,9},{8,12},{9,13},{12,14},{13,15},{14,10},{15,... | collective-permute-start | bytes 811016 | tf_op jit(solution)/shard_map/ppermute | solution.py:224
  31.2 10.9 %collective-permute-start.17 = (bf16[32,4224]{1,0:T(8,128)(2,1)S(1)}, bf16[32,4224]{1,0:T(8,128)(2,1)S(1)}, u32[]{:S(2)}, u32[]{:S(2)}) collective-permute-start(bf16[32,4224]{1,0:T(8,128)(2,1)S(1)} %collective-permute-done.15), channel_id=1, source_target_pairs={{0,4},{1,5},{4,8},{5,9},{8,12},{9,13},{12,14},{13,15},{14,10},{15,... | collective-permute-start | bytes 811016 | tf_op jit(solution)/shard_map/ppermute | solution.py:224
  32.6 9.5 %collective-permute-start.18 = (bf16[32,4224]{1,0:T(8,128)(2,1)S(1)}, bf16[32,4224]{1,0:T(8,128)(2,1)S(1)}, u32[]{:S(2)}, u32[]{:S(2)}) collective-permute-start(bf16[32,4224]{1,0:T(8,128)(2,1)S(1)} %collective-permute-done.16), channel_id=1, source_target_pairs={{0,2},{1,3},{4,0},{5,1},{8,4},{9,5},{12,8},{13,9},{14,12},{15,13},... | collective-permute-start | bytes 811016 | tf_op jit(solution)/shard_map/ppermute | solution.py:224
  47.6 10.9 %collective-permute-start.28 = (bf16[64,4224]{1,0:T(8,128)(2,1)S(1)}, bf16[64,4224]{1,0:T(8,128)(2,1)S(1)}, u32[]{:S(2)}, u32[]{:S(2)}) collective-permute-start(bf16[64,4224]{1,0:T(8,128)(2,1)S(1)} %constant_dynamic-update-slice_fusion.14.own_ref), channel_id=1, source_target_pairs={{0,1},{1,0},{2,3},{3,2},{4,5},{5,4},{6,7},{7,6},{8,9},{9,8},{10,11... | collective-permute-start | bytes 1622024 | tf_op jit(solution)/shard_map/ppermute | solution.py:224
  50.5 17.7 %collective-permute-start.30 = (bf16[64,4096]{1,0:T(8,128)(2,1)S(1)}, bf16[64,4096]{1,0:T(8,128)(2,1)S(1)}, u32[]{:S(2)}, u32[]{:S(2)}) collective-permute-start(bf16[64,4096]{1,0:T(8,128)(2,1)S(1)} %get-tuple-element.124), channel_id=1, source_target_pairs={{0,1},{1,0},{2,3},{3,2},{4,5},{5,4},{6,7},{7,6},{8,9},{9,8},{10,11... | collective-permute-start | bytes 1572872 | tf_op jit(solution)/shard_map/ppermute | solution.py:224
  52.6 10.9 %collective-permute-start.35 = (bf16[32,4096]{1,0:T(8,128)(2,1)S(1)}, bf16[32,4096]{1,0:T(8,128)(2,1)S(1)}, u32[]{:S(2)}, u32[]{:S(2)}) collective-permute-start(bf16[32,4096]{1,0:T(8,128)(2,1)S(1)} %get-tuple-element.156), channel_id=1, source_target_pairs={{0,2},{1,3},{4,0},{5,1},{8,4},{9,5},{12,8},{13,9},{14,12},{15,13},... | collective-permute-start | bytes 786440 | tf_op jit(solution)/shard_map/ppermute | solution.py:224
  63.7 15.7 %collective-permute-start.29 = (bf16[64,4096]{1,0:T(8,128)(2,1)S(1)}, bf16[64,4096]{1,0:T(8,128)(2,1)S(1)}, u32[]{:S(2)}, u32[]{:S(2)}) collective-permute-start(bf16[64,4096]{1,0:T(8,128)(2,1)S(1)} %get-tuple-element.122), channel_id=1, source_target_pairs={{0,1},{1,0},{2,3},{3,2},{4,5},{5,4},{6,7},{7,6},{8,9},{9,8},{10,11... | collective-permute-start | bytes 1572872 | tf_op jit(solution)/shard_map/ppermute | solution.py:224
  68.4 9.3 %collective-permute-start.31 = (bf16[32,4096]{1,0:T(8,128)(2,1)S(1)}, bf16[32,4096]{1,0:T(8,128)(2,1)S(1)}, u32[]{:S(2)}, u32[]{:S(2)}) collective-permute-start(bf16[32,4096]{1,0:T(8,128)(2,1)S(1)} %get-tuple-element.161), channel_id=1, source_target_pairs={{0,2},{1,3},{4,0},{5,1},{8,4},{9,5},{12,8},{13,9},{14,12},{15,13},... | collective-permute-start | bytes 786440 | tf_op jit(solution)/shard_map/ppermute | solution.py:224
  70.1 9.2 %collective-permute-start.32 = (bf16[32,4096]{1,0:T(8,128)(2,1)S(1)}, bf16[32,4096]{1,0:T(8,128)(2,1)S(1)}, u32[]{:S(2)}, u32[]{:S(2)}) collective-permute-start(bf16[32,4096]{1,0:T(8,128)(2,1)S(1)} %get-tuple-element.160), channel_id=1, source_target_pairs={{0,4},{1,5},{4,8},{5,9},{8,12},{9,13},{12,14},{13,15},{14,10},{15,... | collective-permute-start | bytes 786440 | tf_op jit(solution)/shard_map/ppermute | solution.py:224
  70.7 12.2 %collective-permute-start.36 = (bf16[32,4096]{1,0:T(8,128)(2,1)S(1)}, bf16[32,4096]{1,0:T(8,128)(2,1)S(1)}, u32[]{:S(2)}, u32[]{:S(2)}) collective-permute-start(bf16[32,4096]{1,0:T(8,128)(2,1)S(1)} %get-tuple-element.155), channel_id=1, source_target_pairs={{0,4},{1,5},{4,8},{5,9},{8,12},{9,13},{12,14},{13,15},{14,10},{15,... | collective-permute-start | bytes 786440 | tf_op jit(solution)/shard_map/ppermute | solution.py:224
  71.2 11.7 %collective-permute-start.37 = (bf16[32,4096]{1,0:T(8,128)(2,1)S(1)}, bf16[32,4096]{1,0:T(8,128)(2,1)S(1)}, u32[]{:S(2)}, u32[]{:S(2)}) collective-permute-start(bf16[32,4096]{1,0:T(8,128)(2,1)S(1)} %get-tuple-element.154), channel_id=1, source_target_pairs={{0,2},{1,3},{4,0},{5,1},{8,4},{9,5},{12,8},{13,9},{14,12},{15,13},... | collective-permute-start | bytes 786440 | tf_op jit(solution)/shard_map/ppermute | solution.py:224
  79.5 9.3 %collective-permute-start.38 = (bf16[32,4096]{1,0:T(8,128)(2,1)S(1)}, bf16[32,4096]{1,0:T(8,128)(2,1)S(1)}, u32[]{:S(2)}, u32[]{:S(2)}) collective-permute-start(bf16[32,4096]{1,0:T(8,128)(2,1)S(1)} %get-tuple-element.159), channel_id=1, source_target_pairs={{0,2},{1,3},{4,0},{5,1},{8,4},{9,5},{12,8},{13,9},{14,12},{15,13},... | collective-permute-start | bytes 786440 | tf_op jit(solution)/shard_map/ppermute | solution.py:224
  81.1 9.2 %collective-permute-start.39 = (bf16[32,4096]{1,0:T(8,128)(2,1)S(1)}, bf16[32,4096]{1,0:T(8,128)(2,1)S(1)}, u32[]{:S(2)}, u32[]{:S(2)}) collective-permute-start(bf16[32,4096]{1,0:T(8,128)(2,1)S(1)} %get-tuple-element.158), channel_id=1, source_target_pairs={{0,4},{1,5},{4,8},{5,9},{8,12},{9,13},{12,14},{13,15},{14,10},{15,... | collective-permute-start | bytes 786440 | tf_op jit(solution)/shard_map/ppermute | solution.py:224
  83.1 12.8 %collective-permute-start.41 = (bf16[32,4096]{1,0:T(8,128)(2,1)S(1)}, bf16[32,4096]{1,0:T(8,128)(2,1)S(1)}, u32[]{:S(2)}, u32[]{:S(2)}) collective-permute-start(bf16[32,4096]{1,0:T(8,128)(2,1)S(1)} %get-tuple-element.153), channel_id=1, source_target_pairs={{0,4},{1,5},{4,8},{5,9},{8,12},{9,13},{12,14},{13,15},{14,10},{15,... | collective-permute-start | bytes 786440 | tf_op jit(solution)/shard_map/ppermute | solution.py:224
  83.9 12.0 %collective-permute-start.42 = (bf16[32,4096]{1,0:T(8,128)(2,1)S(1)}, bf16[32,4096]{1,0:T(8,128)(2,1)S(1)}, u32[]{:S(2)}, u32[]{:S(2)}) collective-permute-start(bf16[32,4096]{1,0:T(8,128)(2,1)S(1)} %get-tuple-element.152), channel_id=1, source_target_pairs={{0,2},{1,3},{4,0},{5,1},{8,4},{9,5},{12,8},{13,9},{14,12},{15,13},... | collective-permute-start | bytes 786440 | tf_op jit(solution)/shard_map/ppermute | solution.py:224
  (25 other events, 170.5 us)
